TPU v7x, 256 devices: a whole 4x4x8 slice. The times are simulated.
256 devices in a mesh: row: 32 (over y_hi, z, core), col: 8 (over x, y_lo).
Axes of the slice: x: 4, y: 4 (y_hi: 2, y_lo: 2; y = y_hi * 2 + y_lo), z: 8, core: 2. Of those that a mesh axis runs over, the one named last changes fastest.
Arguments:
- tokens: bfloat16 [256, 128, 384], P('row', 'col'), may hold values from -6 to 6
- timestep: int32 [1], replicated, may hold values from 0 to 999
- time_weight: float32 [256, 384], replicated, may hold values from -0.375 to 0.375
- query0: bfloat16 [384, 384], replicated, may hold values from -0.3125 to 0.3125
- key0: bfloat16 [384, 384], replicated, may hold values from -0.3125 to 0.3125
- value0: bfloat16 [384, 384], replicated, may hold values from -0.3125 to 0.3125
- out0: bfloat16 [384, 384], replicated, may hold values from -0.3125 to 0.3125
- merge_one: bfloat16 [1536, 768], replicated, may hold values from -0.15625 to 0.15625
- merge_two: bfloat16 [3072, 1536], P('row', 'col'), may hold values from -0.109375 to 0.109375
- gain_two: float32 [1536], replicated, may hold values from 0.25 to 1.75
- query2: bfloat16 [1536, 1536], P(None, 'col'), may hold values from -0.3125 to 0.3125
- key2: bfloat16 [1536, 1536], P(None, 'col'), may hold values from -0.3125 to 0.3125
- value2: bfloat16 [1536, 1536], P(None, 'col'), may hold values from -0.15625 to 0.15625
- out2: bfloat16 [1536, 1536], P('col'), may hold values from -0.15625 to 0.15625
- split_two: bfloat16 [1536, 3072], P('row', 'col'), may hold values from -0.15625 to 0.15625
- split_one: bfloat16 [768, 1536], replicated, may hold values from -0.21875 to 0.21875
Outputs:
- out_tokens: bfloat16 [256, 128, 384], P('row', 'col')
All inputs are finite; a program needn't handle non-finite values.
Results may differ from a plain program's by a relative error of at most 0.035.
Values may be sent and summed in bfloat16 or wider, within the bound.
No kernel may reach another device: no remote copies, remote signals or barrier semaphores. Data moves between devices by JAX's collectives and lax.ppermute only.
A program may use at most 64 MiB of HBM per device.

v0:
```python
import math

import jax
import jax.numpy as jnp
from jax import lax
from jax.sharding import PartitionSpec as P

HEAD = 64
RADIUS = 3
FREQ = 256


epsilon = 1e-06


def padded_2(block, sides, width):
    for axis, dim in sides:
        count = lax.axis_size(axis)
        forward = [(i, i + 1) for i in range(count - 1)]
        backward = [(target, source) for source, target in forward]
        low = lax.ppermute(
            lax.slice_in_dim(block, block.shape[dim] - width, None, axis=dim), axis, forward
        )
        high = lax.ppermute(lax.slice_in_dim(block, 0, width, axis=dim), axis, backward)
        block = jnp.concatenate([low, block, high], axis=dim)
    return block


def time_features(timestep, count):
    half_count = count // 2
    ladder = jnp.arange(half_count, dtype=jnp.float32)
    freqs = jnp.exp(-math.log(10000.0) * ladder / half_count)
    angles = timestep.astype(jnp.float32)[0] * freqs
    return jnp.concatenate([jnp.cos(angles), jnp.sin(angles)])


def rms_norm(values):
    floats = values.astype(jnp.float32)
    return floats * lax.rsqrt(jnp.mean(floats * floats, axis=-1, keepdims=True) + epsilon)


def group_quads(values):
    height, breadth, feature = values.shape
    return (
        values.reshape(height // 2, 2, breadth // 2, 2, feature)
        .transpose(0, 2, 1, 3, 4)
        .reshape(height // 2, breadth // 2, 4 * feature)
    )


def ungroup(values):
    height, breadth, feature = values.shape
    inner = feature // 4
    return (
        values.reshape(height, breadth, 2, 2, inner)
        .transpose(0, 2, 1, 3, 4)
        .reshape(2 * height, 2 * breadth, inner)
    )


def project(values, weight):
    return jnp.dot(values, weight, preferred_element_type=jnp.float32)


def neighbour_attention(queries, keys_ext, values_ext, valid_rows, valid_cols):
    height, breadth, feature = queries.shape
    factor = 1.0 / math.sqrt(HEAD)
    window = 2 * RADIUS + 1
    head_of = jnp.arange(feature) // HEAD
    head_sum = (head_of[:, None] == head_of[None, :]).astype(jnp.float32)
    query_floats = queries.astype(jnp.float32)
    score_list = []
    for offset_row in range(window):
        for offset_col in range(window):
            key_block = keys_ext[
                offset_row : offset_row + height, offset_col : offset_col + breadth
            ].astype(jnp.float32)
            products = (query_floats * key_block).reshape(height * breadth, feature)
            scores = (
                jnp.dot(products, head_sum, precision=lax.Precision.HIGHEST).reshape(
                    height, breadth, feature
                )
                * factor
            )
            inside = (
                valid_rows[offset_row : offset_row + height][:, None]
                & valid_cols[offset_col : offset_col + breadth][None, :]
            )
            score_list.append(jnp.where(inside[:, :, None], scores, -1e30))
    weights = jax.nn.softmax(jnp.stack(score_list), axis=0).astype(jnp.bfloat16)
    summed = jnp.zeros((height, breadth, feature), jnp.float32)
    position = 0
    for offset_row in range(window):
        for offset_col in range(window):
            value_block = values_ext[
                offset_row : offset_row + height, offset_col : offset_col + breadth
            ].astype(jnp.float32)
            summed = summed + weights[position].astype(jnp.float32) * value_block
            position += 1
    return summed.astype(jnp.bfloat16)


def on_device(
    tokens,
    timestep,
    time_weight,
    query0,
    key0,
    value0,
    out0,
    merge_one,
    merge_two,
    gain_two,
    query2,
    key2,
    value2,
    out2,
    split_two,
    split_one,
):
    height, breadth, feature = tokens.shape
    condition = jnp.dot(
        time_features(timestep, FREQ)[None, :], time_weight, precision=lax.Precision.HIGHEST
    )[0]
    normed = (rms_norm(tokens) * (1.0 + condition)).astype(jnp.bfloat16)
    flat_in = normed.reshape(-1, feature)
    queries = project(flat_in, query0).astype(jnp.bfloat16).reshape(height, breadth, feature)
    keys = project(flat_in, key0).astype(jnp.bfloat16)
    values = project(flat_in, value0).astype(jnp.bfloat16)
    key_value = jnp.concatenate([keys, values], axis=1).reshape(height, breadth, 2 * feature)
    padded = padded_2(key_value, (("row", 0), ("col", 1)), RADIUS)
    keys_ext = padded[:, :, :feature]
    values_ext = padded[:, :, feature:]
    row_first = lax.axis_index("row") * height - RADIUS
    col_first = lax.axis_index("col") * breadth - RADIUS
    row_global = row_first + jnp.arange(height + 2 * RADIUS)
    col_global = col_first + jnp.arange(breadth + 2 * RADIUS)
    valid_rows = (row_global >= 0) & (row_global < height * lax.axis_size("row"))
    valid_cols = (col_global >= 0) & (col_global < breadth * lax.axis_size("col"))
    attended = neighbour_attention(queries, keys_ext, values_ext, valid_rows, valid_cols)
    resid0 = (
        tokens.astype(jnp.float32)
        + project(attended.reshape(-1, feature), out0).reshape(height, breadth, feature)
    ).astype(jnp.bfloat16)
    level1 = project(group_quads(resid0).reshape(-1, 4 * feature), merge_one).astype(jnp.bfloat16)
    level1 = level1.reshape(height // 2, breadth // 2, -1)
    grouped = group_quads(level1)
    band_tokens = lax.all_gather(grouped, "col", axis=1, tiled=True)
    band_rows, band_cols, merged_width = band_tokens.shape
    band_flat = band_tokens.reshape(band_rows * band_cols, merged_width)
    band_count = band_rows * band_cols
    columns = band_flat
    middle_slice = jnp.dot(
        columns,
        lax.all_gather(merge_two, "row", axis=0, tiled=True),
        preferred_element_type=jnp.float32,
    ).astype(jnp.bfloat16)
    middle = lax.all_gather(middle_slice, "col", axis=1, tiled=True)
    normed2 = (rms_norm(middle) * gain_two).astype(jnp.bfloat16)
    heads_here = query2.shape[1] // HEAD
    queries2 = project(normed2, query2).astype(jnp.bfloat16)
    keys2 = project(normed2, key2).astype(jnp.bfloat16)
    values2 = project(normed2, value2).astype(jnp.bfloat16)
    factor = 1.0 / math.sqrt(HEAD)
    contract_last = (((1,), (1,)), ((), ()))
    running_max = jnp.full((heads_here, band_count), -1e30, jnp.float32)
    running_sum = jnp.zeros((heads_here, band_count), jnp.float32)
    weighted = jnp.zeros((heads_here, band_count, HEAD), jnp.float32)
    key_block = lax.all_gather(keys2, "row", axis=0, tiled=True)
    value_block = lax.all_gather(values2, "row", axis=0, tiled=True)
    max_list = []
    sum_list = []
    weighted_list = []
    for attend_head in range(heads_here):
        lower = attend_head * HEAD
        query_head = queries2[:, lower : lower + HEAD]
        key_head = key_block[:, lower : lower + HEAD]
        value_head = value_block[:, lower : lower + HEAD]
        scores = (
            lax.dot_general(query_head, key_head, contract_last, preferred_element_type=jnp.float32)
            * factor
        )
        new_max = jnp.maximum(running_max[attend_head], jnp.max(scores, axis=-1))
        faded = jnp.exp(running_max[attend_head] - new_max)
        exps = jnp.exp(scores - new_max[:, None])
        max_list.append(new_max)
        sum_list.append(running_sum[attend_head] * faded + jnp.sum(exps, axis=-1))
        weighted_list.append(
            weighted[attend_head] * faded[:, None]
            + jnp.dot(exps.astype(jnp.bfloat16), value_head, preferred_element_type=jnp.float32)
        )
    running_sum = jnp.stack(sum_list)
    weighted = jnp.stack(weighted_list)
    attended2 = jnp.concatenate(
        [
            (weighted[head] / running_sum[head][:, None]).astype(jnp.bfloat16)
            for head in range(heads_here)
        ],
        axis=1,
    )
    partial_value = project(attended2, out2)
    lifted_mid = (
        middle.astype(jnp.float32)
        + lax.psum(partial_value.astype(jnp.bfloat16), "col").astype(jnp.float32)
    ).astype(jnp.bfloat16)
    columns = lifted_mid
    up_band = jnp.dot(
        columns,
        lax.all_gather(split_two, "row", axis=0, tiled=True),
        preferred_element_type=jnp.float32,
    )
    up_band = up_band.reshape(band_rows, band_cols, split_two.shape[1])
    up_local = lax.all_to_all(
        up_band.astype(jnp.bfloat16), "col", split_axis=1, concat_axis=2, tiled=True
    ).astype(up_band.dtype)
    lifted1 = (level1.astype(jnp.float32) + ungroup(up_local)).astype(jnp.bfloat16)
    up_zero = project(lifted1.reshape(-1, lifted1.shape[-1]), split_one).reshape(
        height // 2, breadth // 2, -1
    )
    return (resid0.astype(jnp.float32) + ungroup(up_zero)).astype(jnp.bfloat16)


def solution(mesh):
    in_specs = (
        P("row", "col", None),
        P(),
        P(),
        P(),
        P(),
        P(),
        P(),
        P(),
        P("row", "col"),
        P(),
        P(None, "col"),
        P(None, "col"),
        P(None, "col"),
        P("col", None),
        P("row", "col"),
        P(),
    )
    out_specs = P("row", "col", None)
    return jax.shard_map(
        on_device, mesh=mesh, in_specs=in_specs, out_specs=out_specs, check_vma=False
    )
```

profile of v0, /device:TPU:8, one launch (start us, length us, event | category | flops | bytes accessed | tf_op | source)
XLA Modules:
  0.0 317.3 jit_solution(8231169646779152519)
XLA Ops:
  9.0 1.3 convolution_reduce_fusion
  12.5 1.2 convolution_convert_fusion.2
  13.7 1.7 collective-permute-start
  15.5 1.3 collective-permute-start.1
  18.4 1.9 collective-permute-done.1
  20.4 3.3 %collective-permute-start.2 = (bf16[14,3,768]{2,1,0:T(4,128)(2,1)S(1)}, bf16[14,3,768]{2,1,0:T(4,128)(2,1)S(1)}, u32[]{:S(2)}, u32[]{:S(2)}) collective-permute-start(bf16[14,3,768]{2,1,0:T(4,128)(2,1)S(1)} %get-tuple-element.7), channel_id=1, source_target_pairs={{0,1},{1,2},{2,3},{3,4},{4,5},{5,6},{6,7},{8,9},{9,10},{10,11},{11... | collective-permute-start | bytes 193544 | tf_op jit(solution)/shard_map/ppermute | solution.py:21
  23.7 2.6 collective-permute-start.3
  26.8 4.2 %collective-permute-done.3 = bf16[14,3,768]{2,1,0:T(4,128)(2,1)S(1)} collective-permute-done((bf16[14,3,768]{2,1,0:T(4,128)(2,1)S(1)}, bf16[14,3,768]{2,1,0:T(4,128)(2,1)S(1)}, u32[]{:S(2)}, u32[]{:S(2)}) %collective-permute-start.3) | collective-permute-done | bytes 64544 | tf_op jit(solution)/shard_map/ppermute | solution.py:24
  56.8 1.3 fusion
  58.2 4.1 %divide_convert_fusion = bf16[49,8,16,384]{3,2,1,0:T(8,128)(2,1)} fusion(f32[49,8,16,384]{3,2,1,0:T(8,128)S(1)} %get-tuple-element.176, f32[8,16,384]{2,1,0:T(8,128)S(1)} %fusion, f32[8,16,384]{2,1,0:T(8,128)S(1)} %maximum_maximum_fusion.1), kind=kLoop, calls=%fused_computation | loop fusion | flops 7225344 | bytes 14843904 | tf_op jit(solution)/shard_map/convert_element_type | solution.py:90
  62.3 4.3 %fusion.50 = bf16[8,16,384]{2,1,0:T(8,128)(2,1)S(1)} fusion(bf16[8,16,384]{2,1,0:T(8,128)(2,1)S(1)} %copy-done.2, bf16[384,384]{1,0:T(8,128)(2,1)S(1)} %copy-done.4, bf16[8,16,768]{2,1,0:T(8,128)(2,1)S(1)} %bitcast.679, bf16[3,16,768]{2,1,0:T(8,128)(2,1)S(1)} %collective-permute-done.1, bf16[3,16,768]{2,1,0:T(8,128)(2,1)S(1)} %collective-permute-done, ...), kind=kOutput, calls=%fused_computation.156 | convolution fusion | flops 48414720 | bytes 9879552 | tf_op jit(solution)/shard_map/dot_general | solution.py:62
  67.5 27.0 %all_gather.18 = bf16[2,32,3072]{2,0,1:T(2,128)(2,1)S(1)} all-gather(bf16[2,4,3072]{2,0,1:T(2,128)(2,1)S(1)} %copy.44), channel_id=1, replica_groups=mesh['row'=32,'col'=8] {'col'}, dimensions={1}, use_global_device_ids=true | all-gather | bytes 442368 | tf_op jit(solution)/shard_map/all_gather | solution.py:148
  94.6 1.8 fusion.51
  96.4 28.4 %all-gather = bf16[8,192,64]{1,2,0:T(8,128)(2,1)S(1)} all-gather(bf16[1,192,64]{1,2,0:T(8,128)(2,1)S(1)} %fusion.51), channel_id=1, replica_groups=mesh['row'=32,'col'=8] {'col'}, dimensions={0}, use_global_device_ids=true | all-gather | bytes 221184 | tf_op jit(solution)/shard_map/all_gather | solution.py:158
  125.5 1.4 convolution_convert_fusion.7
  126.8 48.1 %all_gather.21 = bf16[2048,192]{1,0:T(8,128)(2,1)S(1)} all-gather(bf16[64,192]{1,0:T(8,128)(2,1)S(1)} %convolution_convert_fusion.7), channel_id=1, replica_groups=mesh['row'=32,'col'=8] {'row'}, dimensions={0}, use_global_device_ids=true | all-gather | bytes 811008 | tf_op jit(solution)/shard_map/all_gather | solution.py:169
  174.9 1.4 convolution_convert_fusion.8
  178.4 1.4 convolution_convert_fusion.6
  179.8 39.6 %all_gather.22 = bf16[2048,192]{1,0:T(8,128)(2,1)S(1)} all-gather(bf16[64,192]{1,0:T(8,128)(2,1)S(1)} %convolution_convert_fusion.6), channel_id=1, replica_groups=mesh['row'=32,'col'=8] {'row'}, dimensions={0}, use_global_device_ids=true | all-gather | bytes 811008 | tf_op jit(solution)/shard_map/all_gather | solution.py:170
  221.3 72.3 %all-reduce.2.cloned.1.call-done = bf16[64,1536]{1,0:T(8,128)(2,1)} async-done(((bf16[64,1536]{1,0:T(8,128)(2,1)}), bf16[64,1536]{1,0:T(8,128)(2,1)}) %all-reduce.2.cloned.1.call-update) | async-done | bytes 196624 | tf_op jit(solution)/shard_map/psum | solution.py:204
  293.6 1.7 convolution_convert_fusion.4
  296.0 6.1 %all-to-all-start = ((bf16[2,32,384]{2,0,1:T(2,128)(2,1)}), bf16[2,32,384]{2,0,1:T(2,128)(2,1)S(1)}, u32[]{:S(2)}, u32[]{:S(2)}) async-start(bf16[2,32,384]{2,0,1:T(2,128)(2,1)} %copy.47), calls=%async_computation | async-start | bytes 98304 | tf_op jit(solution)/shard_map/all_to_all | solution.py:213
  302.1 4.3 %copy.53 = bf16[1536,768]{1,0:T(8,128)(2,1)} copy(bf16[1536,768]{0,1:T(8,128)(2,1)} %bitcast.668) | data formatting | bytes 4718592 | tf_op jit(solution)/shard_map/dot_general | solution.py:62
  307.4 2.4 convolution_bitcast_fusion
  (128 shorter events, 39.6 us)
Async XLA Ops:
  6.5 60.3 %copy-start = (bf16[1536,768]{1,0:T(8,128)(2,1)S(1)}, bf16[1536,768]{1,0:T(8,128)(2,1)}, u32[]{:S(2)}) copy-start(bf16[1536,768]{1,0:T(8,128)(2,1)} %param.23) | copy-start | bytes 7077892
  6.5 88.1 %all-gather.4.cloned.1.call-start = ((), (), s32[]{:S(2)}) async-start(), calls=%async_computation.1 | async-start | bytes 1622016 | tf_op jit(solution)/shard_map/all_gather | solution.py:155
  7.3 214.1 %all-gather.6.cloned.1.call-start = ((), (), s32[]{:S(2)}) async-start(), calls=%async_computation.3 | async-start | bytes 1216512 | tf_op jit(solution)/shard_map/all_gather | solution.py:209
  13.7 4.7 %collective-permute-start = (bf16[3,16,768]{2,1,0:T(8,128)(2,1)S(1)}, bf16[3,16,768]{2,1,0:T(8,128)(2,1)S(1)}, u32[]{:S(2)}, u32[]{:S(2)}) collective-permute-start(bf16[3,16,768]{2,1,0:T(8,128)(2,1)S(1)} %bitcast.739), channel_id=1, source_target_pairs={{0,8},{8,16},{16,24},{24,32},{32,40},{40,48},{48,56},{56,64},{64,7... | collective-permute-start | bytes 221192 | tf_op jit(solution)/shard_map/ppermute | solution.py:21
  15.5 4.9 %collective-permute-start.1 = (bf16[3,16,768]{2,1,0:T(8,128)(2,1)S(1)}, bf16[3,16,768]{2,1,0:T(8,128)(2,1)S(1)}, u32[]{:S(2)}, u32[]{:S(2)}) collective-permute-start(bf16[3,16,768]{2,1,0:T(8,128)(2,1)S(1)} %bitcast.738), channel_id=1, source_target_pairs={{8,0},{16,8},{24,16},{32,24},{40,32},{48,40},{56,48},{64,56},{72,6... | collective-permute-start | bytes 221192 | tf_op jit(solution)/shard_map/ppermute | solution.py:24
  16.8 276.8 %all-reduce.2.cloned.1.call-start = ((), (), s32[]{:S(2)}) async-start(), calls=%async_computation.2 | async-start | bytes 393216 | tf_op jit(solution)/shard_map/psum | solution.py:204
  20.4 6.4 %collective-permute-start.2 = (bf16[14,3,768]{2,1,0:T(4,128)(2,1)S(1)}, bf16[14,3,768]{2,1,0:T(4,128)(2,1)S(1)}, u32[]{:S(2)}, u32[]{:S(2)}) collective-permute-start(bf16[14,3,768]{2,1,0:T(4,128)(2,1)S(1)} %get-tuple-element.7), channel_id=1, source_target_pairs={{0,1},{1,2},{2,3},{3,4},{4,5},{5,6},{6,7},{8,9},{9,10},{10,11},{11... | collective-permute-start | bytes 193544 | tf_op jit(solution)/shard_map/ppermute | solution.py:21
  23.7 7.3 %collective-permute-start.3 = (bf16[14,3,768]{2,1,0:T(4,128)(2,1)S(1)}, bf16[14,3,768]{2,1,0:T(4,128)(2,1)S(1)}, u32[]{:S(2)}, u32[]{:S(2)}) collective-permute-start(bf16[14,3,768]{2,1,0:T(4,128)(2,1)S(1)} %get-tuple-element.8), channel_id=1, source_target_pairs={{1,0},{2,1},{3,2},{4,3},{5,4},{6,5},{7,6},{9,8},{10,9},{11,10},{12... | collective-permute-start | bytes 193544 | tf_op jit(solution)/shard_map/ppermute | solution.py:24
  58.2 4.2 %copy-start.2 = (bf16[8,16,384]{2,1,0:T(8,128)(2,1)S(1)}, bf16[8,16,384]{2,1,0:T(8,128)(2,1)}, u32[]{:S(2)}) copy-start(bf16[8,16,384]{2,1,0:T(8,128)(2,1)} %param.16) | copy-start | bytes 294916
  58.2 4.2 %copy-start.4 = (bf16[384,384]{1,0:T(8,128)(2,1)S(1)}, bf16[384,384]{1,0:T(8,128)(2,1)}, u32[]{:S(2)}) copy-start(bf16[384,384]{1,0:T(8,128)(2,1)} %param.22) | copy-start | bytes 884740
  62.3 63.0 %copy-start.3 = (f32[1536]{0:T(1024)S(1)}, f32[1536]{0:T(1024)}, u32[]{:S(2)}) copy-start(f32[1536]{0:T(1024)} %param.25) | copy-start | bytes 18436
  125.2 95.1 %copy-start.1 = (bf16[192,1536]{1,0:T(8,128)(2,1)S(1)}, bf16[192,1536]{1,0:T(8,128)(2,1)}, u32[]{:S(2)}) copy-start(bf16[192,1536]{1,0:T(8,128)(2,1)} %param.29) | copy-start | bytes 1769476
  296.0 11.1 %all-to-all-start = ((bf16[2,32,384]{2,0,1:T(2,128)(2,1)}), bf16[2,32,384]{2,0,1:T(2,128)(2,1)S(1)}, u32[]{:S(2)}, u32[]{:S(2)}) async-start(bf16[2,32,384]{2,0,1:T(2,128)(2,1)} %copy.47), calls=%async_computation | async-start | bytes 98304 | tf_op jit(solution)/shard_map/all_to_all | solution.py:213
Sparse Core Ops, SparseCore 0:
  10.1 80.7 all-gather.3
  93.6 74.2 all-gather.5
  221.4 72.1 all-reduce.1
where the time goes:
time: 319 us; the launch traced here: 317 us
  blocking collectives  143 us (45%)
  waiting for transfers between devices  80.5 us (25%)
  matrix products  47.4 us (15%)
  starting transfers between devices  15.1 us (5%)
  between operations  14.5 us (5%)
  other arithmetic  10.5 us (3%)
  local copies, waits for them, and re-layouts  6.26 us (2%)
    psum x1, waiting for transfers between devices, on_device(): lax.psum(partial_value.astype(jnp.bfloat16), 'col').astype(jnp.float32)  72.3 us
    all_gather x1, blocking collectives, on_device(): key_block = lax.all_gather(keys2, 'row', axis=0, tiled=True)  48.1 us
    all_gather x1, blocking collectives, on_device(): value_block = lax.all_gather(values2, 'row', axis=0, tiled=True)  39.6 us
    all_gather x1, blocking collectives, on_device(): middle = lax.all_gather(middle_slice, 'col', axis=1, tiled=True)  28.4 us
    all_gather x1, blocking collectives, on_device(): band_tokens = lax.all_gather(grouped, 'col', axis=1, tiled=True)  27 us
    dot_general x49, matrix products, neighbour_attention(): jnp.dot(products, head_sum, precision=lax.Precision.HIGHEST)  24.5 us
    dot_general x10, matrix products, project(): return jnp.dot(values, weight, preferred_element_type=jnp.float32)  15.8 us
  transfers between devices with their start and end apart: 8, of which 5 were waited for; matrix products, arithmetic and copies ran while one was open for 18% of the time, Pallas kernels for 0%

commit v1 on v0

v1 whole, which is shorter than its diff:
```python
import functools
import math

import jax
import jax.numpy as jnp
from jax import lax
from jax.experimental import pallas as pl
from jax.experimental.pallas import tpu as pltpu
from jax.sharding import Mesh, PartitionSpec as P

HEAD = 64
RADIUS = 3
FREQ = 256
EPSILON = 1e-06
LOWEST = -1e30

ROW = ("yh", "z", "k")
COL = ("x", "yl")
BF = jnp.bfloat16
F32 = jnp.float32
MIB = 1 << 20


def shift(axis, step):
    count = lax.axis_size(axis)
    pairs = [(i, i + 1) for i in range(count - 1)]
    return pairs if step > 0 else [(b, a) for a, b in pairs]


def swap(axis):
    return [(0, 1), (1, 0)]


def exchange(block, axis):
    return lax.all_to_all(block, axis, split_axis=0, concat_axis=0, tiled=True)


def in_order(block, axis):
    other = lax.ppermute(block, axis, swap(axis))
    first = lax.axis_index(axis) == 0
    low = jnp.where(first, block, other)
    high = jnp.where(first, other, block)
    return jnp.concatenate([low, high], axis=0)


def copies(block, count):
    return jnp.broadcast_to(block[None], (count,) + block.shape).reshape(
        (count * block.shape[0],) + block.shape[1:]
    )


def dot(a, b):
    return jnp.dot(a, b, preferred_element_type=F32)


def dot_nt(a, b):
    return lax.dot_general(a, b, (((1,), (1,)), ((), ())), preferred_element_type=F32)


def call(body, out_shape, args, us, smem=(), name=None):
    specs = [
        pl.BlockSpec(memory_space=pltpu.SMEM if i in smem else pltpu.VMEM)
        for i in range(len(args))
    ]
    many = isinstance(out_shape, (tuple, list))
    out_specs = (
        tuple(pl.BlockSpec(memory_space=pltpu.VMEM) for _ in out_shape)
        if many
        else pl.BlockSpec(memory_space=pltpu.VMEM)
    )
    return pl.pallas_call(
        body,
        out_shape=out_shape,
        in_specs=specs,
        out_specs=out_specs,
        compiler_params=pltpu.CompilerParams(vmem_limit_bytes=24 * MIB),
        cost_estimate=pl.CostEstimate(
            flops=int(us * 1e9), bytes_accessed=int(us * 3e6), transcendentals=0
        ),
        name=name,
    )(*args)


def place_of(order):
    pos1, pos2, mid = order // 32, (order // 8) % 4, order % 8
    row = (mid // 4) * 4 + (pos2 // 2) * 2 + pos1 // 2
    col = (mid % 4) * 4 + (pos2 % 2) * 2 + pos1 % 2
    return row, col


def finest_kernel(
    where, ext, top, bottom, scale, wq, wk, wv, wo, merge, resid_out, level1_out, band_out
):
    tokens = jnp.concatenate([top[...], ext[...], bottom[...]], axis=0)
    floats = tokens.astype(F32).reshape(448, 384)
    mean = jnp.mean(floats * floats, axis=1, keepdims=True)
    normed = (floats * lax.rsqrt(mean + EPSILON) * scale[...]).astype(BF)
    keys = dot(normed, wk[...]).astype(BF)
    values = dot(normed, wv[...]).astype(BF)

    row, col = place_of(lax.broadcasted_iota(jnp.int32, (128, 448), 0))
    place = lax.broadcasted_iota(jnp.int32, (128, 448), 1)
    key_row, slot = place // 32 - RADIUS, place % 32
    key_col = jnp.where(slot < 16, slot, jnp.where(slot < 24, slot - 24, slot - 8))
    pick = ((key_row == row) & (slot == col)).astype(F32).astype(BF)
    mine = dot(pick, floats.astype(BF))
    queries = dot(dot(pick, normed).astype(BF), wq[...]).astype(BF)

    global_row, global_col = key_row + where[0], key_col + where[1]
    inside = (jnp.abs(key_row - row) <= RADIUS) & (jnp.abs(key_col - col) <= RADIUS)
    inside &= (global_row >= 0) & (global_row < where[2])
    inside &= (global_col >= 0) & (global_col < where[3])
    bias = jnp.where(inside, 0.0, LOWEST)

    lane = lax.broadcasted_iota(jnp.int32, (1, 128), 1)
    low = (lane < HEAD).astype(F32).astype(BF)
    high = (lane >= HEAD).astype(F32).astype(BF)
    blocks = []
    for pair in range(3):
        cut = slice(128 * pair, 128 * pair + 128)
        outs = []
        for half in (low, high):
            scores = dot_nt(queries[:, cut] * half, keys[:, cut]) * (1.0 / math.sqrt(HEAD)) + bias
            exps = jnp.exp(scores - jnp.max(scores, axis=1, keepdims=True))
            weights = (exps / jnp.sum(exps, axis=1, keepdims=True)).astype(BF)
            outs.append(dot(weights, values[:, cut]))
        blocks.append(jnp.where(lane < HEAD, outs[0], outs[1]))
    attended = jnp.concatenate(blocks, axis=1).astype(BF)
    resid = (mine + dot(attended, wo[...])).astype(BF)
    resid_out[...] = resid
    level1 = jnp.zeros((32, 768), F32)
    for pos in range(4):
        level1 += dot(resid[32 * pos : 32 * pos + 32], merge[384 * pos : 384 * pos + 384, :])
    level1_out[...] = level1.astype(BF)
    grouped = jnp.concatenate([level1[8 * pos : 8 * pos + 8] for pos in range(4)], axis=1)
    band_out[...] = jnp.concatenate([grouped] * 8, axis=0).astype(BF)


def middle_kernel(band, weight, mid_out, copies_out):
    blocks = [
        weight[((k * 8 + z) * 2 + yh) * 96 : ((k * 8 + z) * 2 + yh) * 96 + 96, :]
        for yh in range(2)
        for z in range(8)
        for k in range(2)
    ]
    mid = dot(band[...], jnp.concatenate(blocks, axis=0)).astype(BF)
    mid_out[...] = mid
    copies_out[...] = jnp.concatenate([mid] * 8, axis=0)


def project_kernel(mids, gain, wq, wk, wv, q_out, kv_out):
    parts = [mids[64 * i : 64 * i + 64, :].astype(F32) for i in range(8)]
    total = jnp.zeros((64, 1), F32)
    for part in parts:
        total += jnp.sum(part * part, axis=1, keepdims=True)
    inverse = lax.rsqrt(total * (1.0 / 1536.0) + EPSILON)
    sums = [jnp.zeros((64, 192), F32) for _ in range(3)]
    for i, part in enumerate(parts):
        normed = (part * inverse * gain[i : i + 1, :]).astype(BF)
        for j, weight in enumerate((wq, wk, wv)):
            sums[j] += dot(normed, weight[192 * i : 192 * i + 192, :])
    queries, keys, values = sums
    q_out[...] = queries.astype(BF)
    both = jnp.concatenate([keys, values[:, 128:192], values[:, 0:128]], axis=1).astype(BF)
    kv_out[...] = jnp.concatenate([both] * 8, axis=0)


def attend_kernel(q_own, q_other, kv, own_out, other_out):
    queries = jnp.concatenate([q_own[...], q_other[...]], axis=0)
    lane = lax.broadcasted_iota(jnp.int32, (1, 128), 1)
    low = (lane < HEAD).astype(F32).astype(BF)
    high = (lane >= HEAD).astype(F32).astype(BF)
    first = queries[:, 0:128]
    third = jnp.concatenate([queries[:, 128:192], jnp.zeros((128, HEAD), BF)], axis=1)
    stats = jnp.zeros((128, 128), F32)
    nums = []
    for head in range(3):
        query = (first * low, first * high, third)[head]
        keys = kv[:, 128:256] if head == 2 else kv[:, 0:128]
        values = kv[:, 128:256] if head == 2 else kv[:, 256:384]
        scores = dot_nt(query, keys) * (1.0 / math.sqrt(HEAD))
        top = jnp.max(scores, axis=1, keepdims=True)
        exps = jnp.exp(scores - top)
        total = jnp.sum(exps, axis=1, keepdims=True)
        nums.append(dot(exps.astype(BF), values))
        stats = jnp.where(lane == head, top, stats)
        stats = jnp.where(lane == 8 + head, total, stats)
    result = jnp.concatenate(
        [jnp.where(lane < HEAD, nums[0], nums[1]), jnp.where(lane < HEAD, stats, nums[2])], axis=1
    )
    own_out[...] = result[0:64]
    other_out[...] = result[64:128]


def combine_kernel(mine, theirs, out2, parts_out):
    a, b = mine[...], theirs[...]
    factors = []
    for head in range(3):
        top_a, top_b = a[:, 128 + head : 129 + head], b[:, 128 + head : 129 + head]
        sum_a, sum_b = a[:, 136 + head : 137 + head], b[:, 136 + head : 137 + head]
        top = jnp.maximum(top_a, top_b)
        fade_a, fade_b = jnp.exp(top_a - top), jnp.exp(top_b - top)
        whole = 1.0 / (sum_a * fade_a + sum_b * fade_b)
        factors.append((fade_a * whole, fade_b * whole))
    lane = lax.broadcasted_iota(jnp.int32, (1, 128), 1)
    first_a = jnp.where(lane < HEAD, factors[0][0], factors[1][0])
    first_b = jnp.where(lane < HEAD, factors[0][1], factors[1][1])
    pair = (a[:, 0:128] * first_a + b[:, 0:128] * first_b).astype(BF)
    last = (a[:, 192:256] * factors[2][0] + b[:, 192:256] * factors[2][1]).astype(BF)
    result = dot(pair, out2[0:128, :]) + dot(last, out2[128:192, :])
    parts_out[...] = jnp.concatenate(
        [result[:, 192 * i : 192 * i + 192] for i in range(8)], axis=0
    ).astype(BF)


def lift_kernel(parts, mid, weight, up_out):
    total = mid[...].astype(F32)
    sums = jnp.zeros((64, 192), F32)
    for i in range(8):
        sums += parts[64 * i : 64 * i + 64, :].astype(F32)
    lifted = (total + sums).astype(BF)
    for i in range(8):
        up_out[:, 384 * i : 384 * i + 384] = dot(
            lifted, weight[192 * i : 192 * i + 192, :]
        ).astype(BF)


def last_kernel(parts, level1, resid, split, out):
    up = jnp.sum(parts[...].astype(F32).reshape(8, 8, 3072), axis=0)
    spread = jnp.concatenate([up[:, 768 * pos : 768 * pos + 768] for pos in range(4)], axis=0)
    lifted = (level1[...].astype(F32) + spread).astype(BF)
    zero = dot(lifted, split[...])
    rise = jnp.concatenate([zero[:, 384 * pos : 384 * pos + 384] for pos in range(4)], axis=0)
    result = (resid[...].astype(F32) + rise).astype(BF)
    place = lax.broadcasted_iota(jnp.int32, (128, 128), 0)
    row, col = place_of(lax.broadcasted_iota(jnp.int32, (128, 128), 1))
    back = ((place // 16 == row) & (place % 16 == col)).astype(F32).astype(BF)
    out[...] = dot(back, result).reshape(8, 16, 384).astype(BF)


def time_features(timestep, count):
    half_count = count // 2
    ladder = jnp.arange(half_count, dtype=F32)
    freqs = jnp.exp(-math.log(10000.0) * ladder / half_count)
    angles = timestep.astype(F32)[0] * freqs
    return jnp.concatenate([jnp.cos(angles), jnp.sin(angles)])


def on_device(
    tokens,
    timestep,
    time_weight,
    query0,
    key0,
    value0,
    out0,
    merge_one,
    merge_two,
    gain_two,
    query2,
    key2,
    value2,
    out2,
    split_two,
    split_one,
):
    shaped = jax.ShapeDtypeStruct
    left = lax.ppermute(tokens[:, 8:16], COL, shift(COL, 1))
    right = lax.ppermute(tokens[:, 0:8], COL, shift(COL, -1))
    ext = jnp.concatenate([tokens, left, right], axis=1)
    top = lax.ppermute(ext[8 - RADIUS : 8], ROW, shift(ROW, 1))
    bottom = lax.ppermute(ext[0:RADIUS], ROW, shift(ROW, -1))

    merge_block = exchange(copies(in_order(merge_two, "yh"), 8), "z")
    merge_block = lax.all_gather(merge_block, "k", axis=0, tiled=True)

    perm = []
    for row in range(32):
        for col in range(8):
            yh, k = (row % 4) // 2, row % 2
            perm.append((row * 8 + col, ((yh * 8 + col) * 2 + k) * 8 + row // 4))
    split_block = lax.ppermute(split_two, ROW + COL, perm)
    split_block = lax.all_gather(split_block, "k", axis=0, tiled=True)
    split_block = in_order(split_block, "yh")
    split_block = lax.all_gather(split_block, "z", axis=0, tiled=True)

    condition = jnp.dot(
        time_features(timestep, FREQ)[None, :], time_weight, precision=lax.Precision.HIGHEST
    )
    where = jnp.stack(
        [
            lax.axis_index(ROW) * 8,
            lax.axis_index(COL) * 16,
            jnp.int32(8 * lax.axis_size(ROW)),
            jnp.int32(16 * lax.axis_size(COL)),
        ]
    ).astype(jnp.int32)
    resid, level1, band = call(
        finest_kernel,
        (shaped((128, 384), BF), shaped((32, 768), BF), shaped((64, 3072), BF)),
        (where, ext, top, bottom, 1.0 + condition, query0, key0, value0, out0, merge_one),
        6,
        smem=(0,),
        name="finest",
    )
    band = exchange(band, COL)
    mid, mids = call(
        middle_kernel,
        (shaped((64, 192), BF), shaped((512, 192), BF)),
        (band, merge_block),
        2,
        name="middle",
    )
    mids = exchange(mids, COL)
    q, kv = call(
        project_kernel,
        (shaped((64, 192), BF), shaped((512, 384), BF)),
        (mids, gain_two.reshape(8, 192), query2, key2, value2),
        2,
        name="project",
    )
    q_other = lax.ppermute(q, "yh", swap("yh"))
    kv = exchange(kv, "z")
    kv = lax.all_gather(kv, "k", axis=0, tiled=True)
    own, other = call(
        attend_kernel,
        (shaped((64, 256), F32), shaped((64, 256), F32)),
        (q, q_other, kv),
        3,
        name="attend",
    )
    theirs = lax.ppermute(other, "yh", swap("yh"))
    parts = call(combine_kernel, shaped((512, 192), BF), (own, theirs, out2), 1, name="combine")
    parts = exchange(parts, COL)
    up = call(lift_kernel, shaped((64, 3072), BF), (parts, mid, split_block), 1, name="lift")
    up = exchange(up, COL)
    return call(
        last_kernel, shaped((8, 16, 384), BF), (up, level1, resid, split_one), 2, name="last"
    )


def solution(mesh):
    fine = Mesh(mesh.devices.reshape(2, 8, 2, 4, 2), ROW + COL)
    in_specs = (
        P(ROW, COL, None),
        P(),
        P(),
        P(),
        P(),
        P(),
        P(),
        P(),
        P(ROW, COL),
        P(),
        P(None, COL),
        P(None, COL),
        P(None, COL),
        P(COL, None),
        P(ROW, COL),
        P(),
    )
    return jax.shard_map(
        on_device, mesh=fine, in_specs=in_specs, out_specs=P(ROW, COL, None), check_vma=False
    )
```

time: 319 us -> 160 us (0.50)
  blocking collectives: 143 us -> 19.1 us
  matrix products: 47.4 us -> 0.32 us
  starting transfers between devices: 15.1 us -> 50 us
  waiting for transfers between devices: 80.5 us -> 48.4 us
  Pallas kernels: 0 us -> 12.2 us
  other arithmetic: 10.5 us -> 2.59 us
  local copies, waits for them, and re-layouts: 6.26 us -> 12 us
    all_gather x4 -> x2, blocking collectives: 143 us -> 8.54 us  [the longest x1 6.18 us: on_device(): split_block = lax.all_gather(split_block, 'k', axis=0, tiled=True)]
    psum x1 -> x0, waiting for transfers between devices: 72.3 us -> none  [on_device(): lax.psum(partial_value.astype(jnp.bfloat16), 'col').astype(jnp.float32)]
    dot_general x67 -> x0, matrix products: 46.1 us -> none  [the longest x49 24.5 us: neighbour_attention(): jnp.dot(products, head_sum, precision=lax.Precision.HIGHEST)]
    all_to_all x1 -> x5, waiting for transfers between devices: 0.73 us -> 40.1 us  [exchange(): return lax.all_to_all(block, axis, split_axis=0, concat_axis=0, tiled=True)]
    all_to_all x1 -> x5, starting transfers between devices: 6.13 us -> 28.5 us  [exchange(): return lax.all_to_all(block, axis, split_axis=0, concat_axis=0, tiled=True)]
    ppermute x4 -> x9, starting transfers between devices: 8.88 us -> 21.5 us  [the longest x2 8.26 us: in_order(): other = lax.ppermute(block, axis, swap(axis))]
    pallas_call x0 -> x7, Pallas kernels: none -> 12.2 us  [call(): pl.pallas_call(body, out_shape=out_shape, in_specs=specs, out_specs=out_s...]
    all_to_all x0 -> x1, blocking collectives: none -> 10.5 us  [exchange(): return lax.all_to_all(block, axis, split_axis=0, concat_axis=0, tiled=True)]
  transfers between devices with their start and end apart: 8 -> 16, of which waited for: 5 -> 7; matrix products, arithmetic and copies ran while one was open for 18% -> 5% of each run, Pallas kernels for 0% -> 7%
where the time goes in v1:
time: 160 us; the launch traced here: 159 us
  starting transfers between devices  50 us (31%)
  waiting for transfers between devices  48.4 us (30%)
  blocking collectives  19.1 us (12%)
  between operations  14.3 us (9%)
  Pallas kernels  12.2 us (8%)
  local copies, waits for them, and re-layouts  12 us (8%)
  other arithmetic  2.59 us (2%)
    all_to_all x5, waiting for transfers between devices, exchange(): return lax.all_to_all(block, axis, split_axis=0, concat_axis=0, tiled=True)  40.1 us
    all_to_all x5, starting transfers between devices, exchange(): return lax.all_to_all(block, axis, split_axis=0, concat_axis=0, tiled=True)  28.5 us
    pallas_call x7, Pallas kernels, call(): pl.pallas_call(body, out_shape=out_shape, in_specs=specs, out_specs=out_s...  12.2 us
    all_to_all x1, blocking collectives, exchange(): return lax.all_to_all(block, axis, split_axis=0, concat_axis=0, tiled=True)  10.5 us
    unnamed x41, local copies, waits for them, and re-layouts  9.55 us
    ppermute x2, starting transfers between devices, in_order(): other = lax.ppermute(block, axis, swap(axis))  8.26 us
    all_gather x1, blocking collectives, on_device(): split_block = lax.all_gather(split_block, 'k', axis=0, tiled=True)  6.18 us
    ppermute x1, waiting for transfers between devices, on_device(): theirs = lax.ppermute(other, 'yh', swap('yh'))  4.65 us
  transfers between devices with their start and end apart: 16, of which 7 were waited for; matrix products, arithmetic and copies ran while one was open for 5% of the time, Pallas kernels for 7%

profile of v1, /device:TPU:8, one launch (start us, length us, event | category | flops | bytes accessed | tf_op | source)
XLA Modules:
  0.0 158.8 jit_solution(7760507081777126336)
XLA Ops:
  6.5 2.3 %collective-permute-start.4 = (bf16[96,192]{1,0:T(8,128)(2,1)}, bf16[96,192]{1,0:T(8,128)(2,1)S(1)}, u32[]{:S(2)}, u32[]{:S(2)}) collective-permute-start(bf16[96,192]{1,0:T(8,128)(2,1)} %param.24), channel_id=1, source_target_pairs={{0,128},{128,0},{1,129},{129,1},{2,130},{130,2},{3,131},{131,3},{4... | collective-permute-start | bytes 110600 | tf_op jit(solution)/shard_map/ppermute | solution.py:39
  8.8 3.5 %collective-permute-done.4 = bf16[96,192]{1,0:T(8,128)(2,1)S(1)} collective-permute-done((bf16[96,192]{1,0:T(8,128)(2,1)}, bf16[96,192]{1,0:T(8,128)(2,1)S(1)}, u32[]{:S(2)}, u32[]{:S(2)}) %collective-permute-start.4) | collective-permute-done | bytes 36896 | tf_op jit(solution)/shard_map/ppermute | solution.py:39
  14.2 8.6 %all-to-all-start.1 = ((bf16[8,192,192]{2,1,0:T(8,128)(2,1)}), bf16[8,192,192]{2,1,0:T(8,128)(2,1)}, u32[]{:S(2)}, u32[]{:S(2)}) async-start(bf16[8,192,192]{2,1,0:T(8,128)(2,1)} %broadcast_in_dim.2), calls=%async_computation.1 | async-start | bytes 1572864 | tf_op jit(solution)/shard_map/all_to_all | solution.py:35
  23.5 3.3 %collective-permute-start = (bf16[8,8,384]{2,1,0:T(8,128)(2,1)}, bf16[8,8,384]{2,1,0:T(8,128)(2,1)}, u32[]{:S(2)}, u32[]{:S(2)}) collective-permute-start(bf16[8,8,384]{2,1,0:T(8,128)(2,1)} %get-tuple-element.30), channel_id=1, source_target_pairs={{0,1},{1,2},{2,3},{3,4},{4,5},{5,6},{6,7},{8,9},{9,10},{10,11},{11... | collective-permute-start | bytes 147464 | tf_op jit(solution)/shard_map/ppermute | solution.py:268
  26.7 3.2 %collective-permute-start.1 = (bf16[8,8,384]{2,1,0:T(8,128)(2,1)}, bf16[8,8,384]{2,1,0:T(8,128)(2,1)}, u32[]{:S(2)}, u32[]{:S(2)}) collective-permute-start(bf16[8,8,384]{2,1,0:T(8,128)(2,1)} %get-tuple-element.29), channel_id=1, source_target_pairs={{1,0},{2,1},{3,2},{4,3},{5,4},{6,5},{7,6},{9,8},{10,9},{11,10},{12... | collective-permute-start | bytes 147464 | tf_op jit(solution)/shard_map/ppermute | solution.py:269
  29.9 2.7 %collective-permute-start.7 = (bf16[48,384]{1,0:T(8,128)(2,1)}, bf16[48,384]{1,0:T(8,128)(2,1)}, u32[]{:S(2)}, u32[]{:S(2)}) collective-permute-start(bf16[48,384]{1,0:T(8,128)(2,1)} %param.30), channel_id=1, source_target_pairs={{0,0},{1,16},{2,32},{3,48},{4,64},{5,80},{6,96},{7,112},{8,8},{9,2... | collective-permute-start | bytes 110600 | tf_op jit(solution)/shard_map/ppermute | solution.py:282
  36.2 8.6 %all-to-all-done.1 = bf16[8,192,192]{2,1,0:T(8,128)(2,1)} async-done(((bf16[8,192,192]{2,1,0:T(8,128)(2,1)}), bf16[8,192,192]{2,1,0:T(8,128)(2,1)}, u32[]{:S(2)}, u32[]{:S(2)}) %all-to-all-start.1) | async-done | bytes 589856 | tf_op jit(solution)/shard_map/all_to_all | solution.py:35
  47.6 6.2 %all_gather.14 = bf16[96,384]{1,0:T(8,128)(2,1)} all-gather(bf16[48,384]{1,0:T(8,128)(2,1)} %collective-permute-done.7), channel_id=1, replica_groups=mesh['yh'=2,'z'=8,'k'=2,'x'=4,'yl'=2] {'k'}, dimensions={0}, use_global_device_ids=true | all-gather | bytes 110592 | tf_op jit(solution)/shard_map/all_gather | solution.py:283
  53.8 6.0 %collective-permute-start.8 = (bf16[96,384]{1,0:T(8,128)(2,1)}, bf16[96,384]{1,0:T(8,128)(2,1)}, u32[]{:S(2)}, u32[]{:S(2)}) collective-permute-start(bf16[96,384]{1,0:T(8,128)(2,1)} %all_gather.14), channel_id=1, source_target_pairs={{0,128},{128,0},{1,129},{129,1},{2,130},{130,2},{3,131},{131,3},{4... | collective-permute-start | bytes 221192 | tf_op jit(solution)/shard_map/ppermute | solution.py:39
  61.7 5.4 %finest.1 = (bf16[128,384]{1,0:T(8,128)(2,1)S(1)}, bf16[32,768]{1,0:T(8,128)(2,1)S(1)}, bf16[64,3072]{1,0:T(8,128)(2,1)}) custom-call(s32[4]{0:T(128)S(1)} %pad_add_fusion.where, bf16[8,32,384]{2,1,0:T(8,128)(2,1)S(1)} %constant_dynamic-update-slice_fusion.ext, bf16[3,32,384]{2,1,0:T(8,128)(2,1)S(1)} %collective-permute-done.2.top, ...), custom_call_target="tpu_custom_call" | custom-call | flops 6000000000 | bytes 18000000 | tf_op jit(solution)/shard_map/finest/pallas_call | solution.py:71
  68.3 7.7 %all-to-all-start = ((bf16[8,8,3072]{2,1,0:T(8,128)(2,1)}), bf16[8,8,3072]{2,1,0:T(8,128)(2,1)S(1)}, u32[]{:S(2)}, u32[]{:S(2)}) async-start(bf16[8,8,3072]{2,1,0:T(8,128)(2,1)} %bitcast.4), calls=%async_computation | async-start | bytes 786432 | tf_op jit(solution)/shard_map/all_to_all | solution.py:35
  77.7 6.1 %all-to-all-done = bf16[8,8,3072]{2,1,0:T(8,128)(2,1)S(1)} async-done(((bf16[8,8,3072]{2,1,0:T(8,128)(2,1)}), bf16[8,8,3072]{2,1,0:T(8,128)(2,1)S(1)}, u32[]{:S(2)}, u32[]{:S(2)}) %all-to-all-start) | async-done | bytes 393248 | tf_op jit(solution)/shard_map/all_to_all | solution.py:35
  83.8 1.5 copy-done.3
  86.4 4.1 %all-to-all-start.2 = ((bf16[8,64,192]{2,1,0:T(8,128)(2,1)}), bf16[8,64,192]{2,1,0:T(8,128)(2,1)S(1)}, u32[]{:S(2)}, u32[]{:S(2)}) async-start(bf16[8,64,192]{2,1,0:T(8,128)(2,1)} %bitcast.7), calls=%async_computation.2 | async-start | bytes 524288 | tf_op jit(solution)/shard_map/all_to_all | solution.py:35
  91.0 1.3 copy.19.wv
  92.5 4.2 %all-to-all-done.2 = bf16[8,64,192]{2,1,0:T(8,128)(2,1)S(1)} async-done(((bf16[8,64,192]{2,1,0:T(8,128)(2,1)}), bf16[8,64,192]{2,1,0:T(8,128)(2,1)S(1)}, u32[]{:S(2)}, u32[]{:S(2)}) %all-to-all-start.2) | async-done | bytes 196640 | tf_op jit(solution)/shard_map/all_to_all | solution.py:35
  96.6 1.5 project.1
  98.1 3.5 %all-to-all-start.3 = ((bf16[8,64,384]{2,1,0:T(8,128)(2,1)}), bf16[8,64,384]{2,1,0:T(8,128)(2,1)S(1)}, u32[]{:S(2)}, u32[]{:S(2)}) async-start(bf16[8,64,384]{2,1,0:T(8,128)(2,1)} %bitcast.9), calls=%async_computation.3 | async-start | bytes 786432 | tf_op jit(solution)/shard_map/all_to_all | solution.py:35
  101.9 15.2 %all-to-all-done.3 = bf16[8,64,384]{2,1,0:T(8,128)(2,1)S(1)} async-done(((bf16[8,64,384]{2,1,0:T(8,128)(2,1)}), bf16[8,64,384]{2,1,0:T(8,128)(2,1)S(1)}, u32[]{:S(2)}, u32[]{:S(2)}) %all-to-all-start.3) | async-done | bytes 393248 | tf_op jit(solution)/shard_map/all_to_all | solution.py:35
  117.0 2.4 %all_gather.13.kv = bf16[1024,384]{1,0:T(8,128)(2,1)S(1)} all-gather(bf16[512,384]{1,0:T(8,128)(2,1)S(1)} %bitcast.22), channel_id=1, replica_groups=mesh['yh'=2,'z'=8,'k'=2,'x'=4,'yl'=2] {'k'}, dimensions={0}, use_global_device_ids=true | all-gather | bytes 1179648 | tf_op jit(solution)/shard_map/all_gather | solution.py:324
  121.8 4.7 %collective-permute-done.6.theirs = f32[64,256]{1,0:T(8,128)S(1)} collective-permute-done((f32[64,256]{1,0:T(8,128)S(1)}, f32[64,256]{1,0:T(8,128)S(1)}, u32[]{:S(2)}, u32[]{:S(2)}) %collective-permute-start.6) | collective-permute-done | bytes 65568 | tf_op jit(solution)/shard_map/ppermute | solution.py:332
  127.8 4.6 %all-to-all-start.4 = ((bf16[8,64,192]{2,1,0:T(8,128)(2,1)}), bf16[8,64,192]{2,1,0:T(8,128)(2,1)S(1)}, u32[]{:S(2)}, u32[]{:S(2)}) async-start(bf16[8,64,192]{2,1,0:T(8,128)(2,1)} %bitcast.11), calls=%async_computation.4 | async-start | bytes 524288 | tf_op jit(solution)/shard_map/all_to_all | solution.py:35
  132.4 6.1 %all-to-all-done.4 = bf16[8,64,192]{2,1,0:T(8,128)(2,1)S(1)} async-done(((bf16[8,64,192]{2,1,0:T(8,128)(2,1)}), bf16[8,64,192]{2,1,0:T(8,128)(2,1)S(1)}, u32[]{:S(2)}, u32[]{:S(2)}) %all-to-all-start.4) | async-done | bytes 196640 | tf_op jit(solution)/shard_map/all_to_all | solution.py:35
  140.2 10.5 %all_to_all.65 = bf16[8,8,3072]{2,1,0:T(8,128)(2,1)S(1)} all-to-all(bf16[8,8,3072]{2,1,0:T(8,128)(2,1)S(1)} %bitcast.19), channel_id=1, replica_groups=mesh['yh'=2,'z'=8,'k'=2,'x'=4,'yl'=2] {'x','yl'}, dimensions={0} | all-to-all | bytes 786432 | tf_op jit(solution)/shard_map/all_to_all | solution.py:35
  (76 shorter events, 21.7 us)
Async XLA Ops:
  6.5 26.8 %copy-start = (f32[256,384]{1,0:T(8,128)S(1)}, f32[256,384]{1,0:T(8,128)}, u32[]{:S(2)}) copy-start(f32[256,384]{1,0:T(8,128)} %param.18) | copy-start | bytes 1179652
  6.5 16.3 %copy-start.16 = (bf16[8,16,384]{2,1,0:T(8,128)(2,1)S(1)}, bf16[8,16,384]{2,1,0:T(8,128)(2,1)}, u32[]{:S(2)}) copy-start(bf16[8,16,384]{2,1,0:T(8,128)(2,1)} %param.16) | copy-start | bytes 294916
  6.5 5.8 %collective-permute-start.4 = (bf16[96,192]{1,0:T(8,128)(2,1)}, bf16[96,192]{1,0:T(8,128)(2,1)S(1)}, u32[]{:S(2)}, u32[]{:S(2)}) collective-permute-start(bf16[96,192]{1,0:T(8,128)(2,1)} %param.24), channel_id=1, source_target_pairs={{0,128},{128,0},{1,129},{129,1},{2,130},{130,2},{3,131},{131,3},{4... | collective-permute-start | bytes 110600 | tf_op jit(solution)/shard_map/ppermute | solution.py:39
  13.2 46.5 %copy-start.1 = (bf16[1536,768]{1,0:T(8,128)(2,1)S(1)}, bf16[1536,768]{1,0:T(8,128)(2,1)}, u32[]{:S(2)}) copy-start(bf16[1536,768]{1,0:T(8,128)(2,1)} %merge.1) | copy-start | bytes 7077892
  13.2 46.5 %copy-start.6 = (bf16[384,384]{1,0:T(8,128)(2,1)S(1)}, bf16[384,384]{1,0:T(8,128)(2,1)}, u32[]{:S(2)}) copy-start(bf16[384,384]{1,0:T(8,128)(2,1)} %wq.2) | copy-start | bytes 884740
  13.2 46.5 %copy-start.7 = (bf16[384,384]{1,0:T(8,128)(2,1)S(1)}, bf16[384,384]{1,0:T(8,128)(2,1)}, u32[]{:S(2)}) copy-start(bf16[384,384]{1,0:T(8,128)(2,1)} %wk.2) | copy-start | bytes 884740
  14.2 30.7 %all-to-all-start.1 = ((bf16[8,192,192]{2,1,0:T(8,128)(2,1)}), bf16[8,192,192]{2,1,0:T(8,128)(2,1)}, u32[]{:S(2)}, u32[]{:S(2)}) async-start(bf16[8,192,192]{2,1,0:T(8,128)(2,1)} %broadcast_in_dim.2), calls=%async_computation.1 | async-start | bytes 1572864 | tf_op jit(solution)/shard_map/all_to_all | solution.py:35
  22.8 61.0 %all-gather.3.cloned.1.call-start = ((), (), s32[]{:S(2)}) async-start(), calls=%async_computation.6 | async-start | bytes 2359296 | tf_op jit(solution)/shard_map/all_gather | solution.py:275
  23.5 11.1 %collective-permute-start = (bf16[8,8,384]{2,1,0:T(8,128)(2,1)}, bf16[8,8,384]{2,1,0:T(8,128)(2,1)}, u32[]{:S(2)}, u32[]{:S(2)}) collective-permute-start(bf16[8,8,384]{2,1,0:T(8,128)(2,1)} %get-tuple-element.30), channel_id=1, source_target_pairs={{0,1},{1,2},{2,3},{3,4},{4,5},{5,6},{6,7},{8,9},{9,10},{10,11},{11... | collective-permute-start | bytes 147464 | tf_op jit(solution)/shard_map/ppermute | solution.py:268
  26.7 8.7 %collective-permute-start.1 = (bf16[8,8,384]{2,1,0:T(8,128)(2,1)}, bf16[8,8,384]{2,1,0:T(8,128)(2,1)}, u32[]{:S(2)}, u32[]{:S(2)}) collective-permute-start(bf16[8,8,384]{2,1,0:T(8,128)(2,1)} %get-tuple-element.29), channel_id=1, source_target_pairs={{1,0},{2,1},{3,2},{4,3},{5,4},{6,5},{7,6},{9,8},{10,9},{11,10},{12... | collective-permute-start | bytes 147464 | tf_op jit(solution)/shard_map/ppermute | solution.py:269
  29.9 17.7 %collective-permute-start.7 = (bf16[48,384]{1,0:T(8,128)(2,1)}, bf16[48,384]{1,0:T(8,128)(2,1)}, u32[]{:S(2)}, u32[]{:S(2)}) collective-permute-start(bf16[48,384]{1,0:T(8,128)(2,1)} %param.30), channel_id=1, source_target_pairs={{0,0},{1,16},{2,32},{3,48},{4,64},{5,80},{6,96},{7,112},{8,8},{9,2... | collective-permute-start | bytes 110600 | tf_op jit(solution)/shard_map/ppermute | solution.py:282
  44.9 14.8 %collective-permute-start.2 = (bf16[3,32,384]{2,1,0:T(8,128)(2,1)S(1)}, bf16[3,32,384]{2,1,0:T(8,128)(2,1)S(1)}, u32[]{:S(2)}, u32[]{:S(2)}) collective-permute-start(bf16[3,32,384]{2,1,0:T(8,128)(2,1)S(1)} %get-tuple-element.24), channel_id=1, source_target_pairs={{0,8},{8,16},{16,24},{24,32},{32,40},{40,48},{48,56},{56,64},{64,7... | collective-permute-start | bytes 221192 | tf_op jit(solution)/shard_map/ppermute | solution.py:271
  46.2 13.5 %collective-permute-start.3 = (bf16[3,32,384]{2,1,0:T(8,128)(2,1)S(1)}, bf16[3,32,384]{2,1,0:T(8,128)(2,1)S(1)}, u32[]{:S(2)}, u32[]{:S(2)}) collective-permute-start(bf16[3,32,384]{2,1,0:T(8,128)(2,1)S(1)} %get-tuple-element.23), channel_id=1, source_target_pairs={{8,0},{16,8},{24,16},{32,24},{40,32},{48,40},{56,48},{64,56},{72,6... | collective-permute-start | bytes 221192 | tf_op jit(solution)/shard_map/ppermute | solution.py:272
  53.8 22.3 %collective-permute-start.8 = (bf16[96,384]{1,0:T(8,128)(2,1)}, bf16[96,384]{1,0:T(8,128)(2,1)}, u32[]{:S(2)}, u32[]{:S(2)}) collective-permute-start(bf16[96,384]{1,0:T(8,128)(2,1)} %all_gather.14), channel_id=1, source_target_pairs={{0,128},{128,0},{1,129},{129,1},{2,130},{130,2},{3,131},{131,3},{4... | collective-permute-start | bytes 221192 | tf_op jit(solution)/shard_map/ppermute | solution.py:39
  68.3 15.5 %all-to-all-start = ((bf16[8,8,3072]{2,1,0:T(8,128)(2,1)}), bf16[8,8,3072]{2,1,0:T(8,128)(2,1)S(1)}, u32[]{:S(2)}, u32[]{:S(2)}) async-start(bf16[8,8,3072]{2,1,0:T(8,128)(2,1)} %bitcast.4), calls=%async_computation | async-start | bytes 786432 | tf_op jit(solution)/shard_map/all_to_all | solution.py:35
  76.0 56.3 %all-gather.5.cloned.1.call-start = ((), (), s32[]{:S(2)}) async-start(), calls=%async_computation.7 | async-start | bytes 1327104 | tf_op jit(solution)/shard_map/all_gather | solution.py:285
  86.4 10.2 %all-to-all-start.2 = ((bf16[8,64,192]{2,1,0:T(8,128)(2,1)}), bf16[8,64,192]{2,1,0:T(8,128)(2,1)S(1)}, u32[]{:S(2)}, u32[]{:S(2)}) async-start(bf16[8,64,192]{2,1,0:T(8,128)(2,1)} %bitcast.7), calls=%async_computation.2 | async-start | bytes 524288 | tf_op jit(solution)/shard_map/all_to_all | solution.py:35
  98.1 19.0 %all-to-all-start.3 = ((bf16[8,64,384]{2,1,0:T(8,128)(2,1)}), bf16[8,64,384]{2,1,0:T(8,128)(2,1)S(1)}, u32[]{:S(2)}, u32[]{:S(2)}) async-start(bf16[8,64,384]{2,1,0:T(8,128)(2,1)} %bitcast.9), calls=%async_computation.3 | async-start | bytes 786432 | tf_op jit(solution)/shard_map/all_to_all | solution.py:35
  101.5 17.9 %collective-permute-start.5 = (bf16[64,192]{1,0:T(8,128)(2,1)S(1)}, bf16[64,192]{1,0:T(8,128)(2,1)S(1)}, u32[]{:S(2)}, u32[]{:S(2)}) collective-permute-start(bf16[64,192]{1,0:T(8,128)(2,1)S(1)} %get-tuple-element.16.q_own), channel_id=1, source_target_pairs={{0,128},{128,0},{1,129},{129,1},{2,130},{130,2},{3,131},{131,3},{4... | collective-permute-start | bytes 73736 | tf_op jit(solution)/shard_map/ppermute | solution.py:322
  120.6 5.9 %collective-permute-start.6 = (f32[64,256]{1,0:T(8,128)S(1)}, f32[64,256]{1,0:T(8,128)S(1)}, u32[]{:S(2)}, u32[]{:S(2)}) collective-permute-start(f32[64,256]{1,0:T(8,128)S(1)} %get-tuple-element.19), channel_id=1, source_target_pairs={{0,128},{128,0},{1,129},{129,1},{2,130},{130,2},{3,131},{131,3},{4... | collective-permute-start | bytes 196616 | tf_op jit(solution)/shard_map/ppermute | solution.py:332
  127.8 22.9 %copy-start.11 = (bf16[128,384]{1,0:T(8,128)(2,1)S(1)}, bf16[128,384]{1,0:T(8,128)(2,1)}, u32[]{:S(2)}) copy-start(bf16[128,384]{1,0:T(8,128)(2,1)} %copy-done.10) | copy-start | bytes 294916
  127.8 22.9 %copy-start.13 = (bf16[32,768]{1,0:T(8,128)(2,1)S(1)}, bf16[32,768]{1,0:T(8,128)(2,1)}, u32[]{:S(2)}) copy-start(bf16[32,768]{1,0:T(8,128)(2,1)} %copy-done.12) | copy-start | bytes 147460
  127.8 10.7 %all-to-all-start.4 = ((bf16[8,64,192]{2,1,0:T(8,128)(2,1)}), bf16[8,64,192]{2,1,0:T(8,128)(2,1)S(1)}, u32[]{:S(2)}, u32[]{:S(2)}) async-start(bf16[8,64,192]{2,1,0:T(8,128)(2,1)} %bitcast.11), calls=%async_computation.4 | async-start | bytes 524288 | tf_op jit(solution)/shard_map/all_to_all | solution.py:35
  132.4 18.3 %copy-start.2 = (bf16[768,1536]{1,0:T(8,128)(2,1)S(1)}, bf16[768,1536]{1,0:T(8,128)(2,1)}, u32[]{:S(2)}) copy-start(bf16[768,1536]{1,0:T(8,128)(2,1)} %split.1) | copy-start | bytes 7077892
  (10 other events, 29.7 us)
Sparse Core Ops, SparseCore 0:
  45.0 14.1 all-gather.2
  78.7 35.6 all-gather.4

commit v2 on v1

--- a/solution.py
+++ b/solution.py
@@ -57,28 +57,44 @@
     return lax.dot_general(a, b, (((1,), (1,)), ((), ())), preferred_element_type=F32)
 
 
-def call(body, out_shape, args, us, smem=(), name=None):
+def call(body, out_shape, args, us, smem=(), far=(), through=(), scratch=(), name=None, vmem=16, out_far=()):
+    ins, outs = len(args), len(out_shape)
     specs = [
-        pl.BlockSpec(memory_space=pltpu.SMEM if i in smem else pltpu.VMEM)
-        for i in range(len(args))
-    ]
-    many = isinstance(out_shape, (tuple, list))
-    out_specs = (
-        tuple(pl.BlockSpec(memory_space=pltpu.VMEM) for _ in out_shape)
-        if many
-        else pl.BlockSpec(memory_space=pltpu.VMEM)
-    )
-    return pl.pallas_call(
-        body,
+        pl.BlockSpec(
+            memory_space=pltpu.SMEM if i in smem else pltpu.HBM if i in far else pltpu.VMEM
+        )
+        for i in range(ins)
+    ] + [pl.BlockSpec(memory_space=pl.ANY) for _ in through]
+    out_specs = tuple(
+        pl.BlockSpec(memory_space=pltpu.HBM if i in out_far else pltpu.VMEM) for i in range(outs)
+    ) + tuple(
+        pl.BlockSpec(memory_space=pl.ANY) for _ in through
+    )
+    out_shape = tuple(
+        pltpu.HBM(a.shape, a.dtype) if i in out_far else a for i, a in enumerate(out_shape)
+    ) + tuple(
+        jax.ShapeDtypeStruct(a.shape, a.dtype) for a in through
+    )
+    args = tuple(args) + tuple(through)
+    count = len(through)
+
+    def kernel(*refs):
+        body(*refs[:ins], *refs[ins + count : ins + count + outs], *refs[ins + 2 * count + outs :])
+
+    result = pl.pallas_call(
+        kernel,
         out_shape=out_shape,
         in_specs=specs,
         out_specs=out_specs,
-        compiler_params=pltpu.CompilerParams(vmem_limit_bytes=24 * MIB),
+        scratch_shapes=tuple(scratch),
+        input_output_aliases={ins + i: outs + i for i in range(count)},
+        compiler_params=pltpu.CompilerParams(vmem_limit_bytes=vmem * MIB),
         cost_estimate=pl.CostEstimate(
             flops=int(us * 1e9), bytes_accessed=int(us * 3e6), transcendentals=0
         ),
         name=name,
     )(*args)
+    return result if len(result) > 1 else result[0]
 
 
 def place_of(order):
@@ -88,11 +104,61 @@
     return row, col
 
 
+def widen(*blocks):
+    return jnp.concatenate([block.astype(F32) for block in blocks], axis=1)
+
+
+def rows_kernel(tokens, left, right, first_out, last_out):
+    wide = widen(tokens[...], left[...], right[...])
+    first_out[...] = wide[0:RADIUS].astype(BF)
+    last_out[...] = wide[8 - RADIUS : 8].astype(BF)
+
+
+def ordered(where, own, over_k, over_yh, over_both):
+    blocks = [block[...] for block in (own, over_k, over_yh, over_both)]
+    here = where[5] * 2 + where[4]
+    result = []
+    for i in range(4):
+        row = blocks[3]
+        for j in range(3):
+            row = jnp.where(here == (i ^ j), blocks[j], row)
+        result.append(row)
+    return result
+
+
+def join_kernel(where, own, over_k, over_yh, over_both, out):
+    blocks = [block.astype(F32) for block in ordered(where, own, over_k, over_yh, over_both)]
+    for k in range(2):
+        out[k] = jnp.concatenate([blocks[k], blocks[2 + k]], axis=1).astype(BF)
+
+
 def finest_kernel(
-    where, ext, top, bottom, scale, wq, wk, wv, wo, merge, resid_out, level1_out, band_out
+    where,
+    tokens,
+    left,
+    right,
+    top,
+    bottom,
+    scale,
+    wk,
+    wv,
+    wq,
+    wo,
+    merge,
+    split,
+    resid_out,
+    level1_out,
+    band_out,
+    split_out,
+    resid_near,
+    level1_near,
+    sent,
 ):
-    tokens = jnp.concatenate([top[...], ext[...], bottom[...]], axis=0)
-    floats = tokens.astype(F32).reshape(448, 384)
+    split_out[...] = split[...]
+    wide = widen(tokens[...], left[...], right[...])
+    floats = jnp.concatenate(
+        [top[...].astype(F32), wide, bottom[...].astype(F32)], axis=0
+    ).reshape(448, 384)
     mean = jnp.mean(floats * floats, axis=1, keepdims=True)
     normed = (floats * lax.rsqrt(mean + EPSILON) * scale[...]).astype(BF)
     keys = dot(normed, wk[...]).astype(BF)
@@ -127,28 +193,33 @@
         blocks.append(jnp.where(lane < HEAD, outs[0], outs[1]))
     attended = jnp.concatenate(blocks, axis=1).astype(BF)
     resid = (mine + dot(attended, wo[...])).astype(BF)
-    resid_out[...] = resid
+    resid_near[...] = resid
+    send_resid = pltpu.make_async_copy(resid_near, resid_out, sent.at[0])
+    send_resid.start()
     level1 = jnp.zeros((32, 768), F32)
     for pos in range(4):
         level1 += dot(resid[32 * pos : 32 * pos + 32], merge[384 * pos : 384 * pos + 384, :])
-    level1_out[...] = level1.astype(BF)
+    level1_near[...] = level1.astype(BF)
+    send_level1 = pltpu.make_async_copy(level1_near, level1_out, sent.at[1])
+    send_level1.start()
     grouped = jnp.concatenate([level1[8 * pos : 8 * pos + 8] for pos in range(4)], axis=1)
     band_out[...] = jnp.concatenate([grouped] * 8, axis=0).astype(BF)
+    send_resid.wait()
+    send_level1.wait()
 
 
 def middle_kernel(band, weight, mid_out, copies_out):
-    blocks = [
-        weight[((k * 8 + z) * 2 + yh) * 96 : ((k * 8 + z) * 2 + yh) * 96 + 96, :]
-        for yh in range(2)
-        for z in range(8)
-        for k in range(2)
-    ]
-    mid = dot(band[...], jnp.concatenate(blocks, axis=0)).astype(BF)
+    low = dot(band[:, 0:1536], weight[...])[:, 0:192]
+    high = dot(band[:, 1536:3072], weight[...])[:, 192:384]
+    mid = (low + high).astype(BF)
     mid_out[...] = mid
     copies_out[...] = jnp.concatenate([mid] * 8, axis=0)
 
 
-def project_kernel(mids, gain, wq, wk, wv, q_out, kv_out):
+def project_kernel(
+    where, mids, gain, wq, wk, wv, own, over_k, over_yh, over_both, q_out, kv_out, split_out
+):
+    split_out[...] = jnp.concatenate(ordered(where, own, over_k, over_yh, over_both), axis=0)
     parts = [mids[64 * i : 64 * i + 64, :].astype(F32) for i in range(8)]
     total = jnp.zeros((64, 1), F32)
     for part in parts:
@@ -158,7 +229,7 @@
     for i, part in enumerate(parts):
         normed = (part * inverse * gain[i : i + 1, :]).astype(BF)
         for j, weight in enumerate((wq, wk, wv)):
-            sums[j] += dot(normed, weight[192 * i : 192 * i + 192, :])
+            sums[j] += dot_nt(normed, weight[:, 192 * i : 192 * i + 192])
     queries, keys, values = sums
     q_out[...] = queries.astype(BF)
     both = jnp.concatenate([keys, values[:, 128:192], values[:, 0:128]], axis=1).astype(BF)
@@ -214,15 +285,12 @@
 
 
 def lift_kernel(parts, mid, weight, up_out):
-    total = mid[...].astype(F32)
-    sums = jnp.zeros((64, 192), F32)
+    sums = mid[...].astype(F32)
     for i in range(8):
         sums += parts[64 * i : 64 * i + 64, :].astype(F32)
-    lifted = (total + sums).astype(BF)
+    lifted = sums.astype(BF)
     for i in range(8):
-        up_out[:, 384 * i : 384 * i + 384] = dot(
-            lifted, weight[192 * i : 192 * i + 192, :]
-        ).astype(BF)
+        up_out[:, 384 * i : 384 * i + 384] = dot(lifted, weight[i]).astype(BF)
 
 
 def last_kernel(parts, level1, resid, split, out):
@@ -267,12 +335,32 @@
     shaped = jax.ShapeDtypeStruct
     left = lax.ppermute(tokens[:, 8:16], COL, shift(COL, 1))
     right = lax.ppermute(tokens[:, 0:8], COL, shift(COL, -1))
-    ext = jnp.concatenate([tokens, left, right], axis=1)
-    top = lax.ppermute(ext[8 - RADIUS : 8], ROW, shift(ROW, 1))
-    bottom = lax.ppermute(ext[0:RADIUS], ROW, shift(ROW, -1))
-
-    merge_block = exchange(copies(in_order(merge_two, "yh"), 8), "z")
-    merge_block = lax.all_gather(merge_block, "k", axis=0, tiled=True)
+    first, last = call(
+        rows_kernel, [shaped((RADIUS, 32, 384), BF)] * 2, (tokens, left, right), 1, name="rows"
+    )
+    top = lax.ppermute(last, ROW, shift(ROW, 1))
+    bottom = lax.ppermute(first, ROW, shift(ROW, -1))
+
+    condition = jnp.dot(
+        time_features(timestep, FREQ)[None, :], time_weight, precision=lax.Precision.HIGHEST
+    )
+    where = jnp.stack(
+        [
+            lax.axis_index(ROW) * 8,
+            lax.axis_index(COL) * 16,
+            jnp.int32(8 * lax.axis_size(ROW)),
+            jnp.int32(16 * lax.axis_size(COL)),
+            lax.axis_index("k"),
+            lax.axis_index("yh"),
+            lax.axis_index(COL),
+        ]
+    ).astype(jnp.int32)
+    def others(block):
+        return (
+            lax.ppermute(block, "k", swap("k")),
+            lax.ppermute(block, "yh", swap("yh")),
+            lax.ppermute(block, ("yh", "k"), [(0, 3), (1, 2), (2, 1), (3, 0)]),
+        )
 
     perm = []
     for row in range(32):
@@ -280,45 +368,78 @@
             yh, k = (row % 4) // 2, row % 2
             perm.append((row * 8 + col, ((yh * 8 + col) * 2 + k) * 8 + row // 4))
     split_block = lax.ppermute(split_two, ROW + COL, perm)
-    split_block = lax.all_gather(split_block, "k", axis=0, tiled=True)
-    split_block = in_order(split_block, "yh")
-    split_block = lax.all_gather(split_block, "z", axis=0, tiled=True)
-
-    condition = jnp.dot(
-        time_features(timestep, FREQ)[None, :], time_weight, precision=lax.Precision.HIGHEST
-    )
-    where = jnp.stack(
-        [
-            lax.axis_index(ROW) * 8,
-            lax.axis_index(COL) * 16,
-            jnp.int32(8 * lax.axis_size(ROW)),
-            jnp.int32(16 * lax.axis_size(COL)),
-        ]
-    ).astype(jnp.int32)
-    resid, level1, band = call(
+
+    weight = call(
+        join_kernel,
+        [shaped((2, 96, 384), BF)],
+        (where, merge_two, *others(merge_two)),
+        1,
+        smem=(0,),
+        name="join",
+    )
+    weight = lax.all_gather(weight.reshape(192, 384), "z", axis=0, tiled=True)
+
+    resid, level1, band, split_block = call(
         finest_kernel,
-        (shaped((128, 384), BF), shaped((32, 768), BF), shaped((64, 3072), BF)),
-        (where, ext, top, bottom, 1.0 + condition, query0, key0, value0, out0, merge_one),
+        (
+            shaped((128, 384), BF),
+            shaped((32, 768), BF),
+            shaped((64, 3072), BF),
+            shaped((48, 384), BF),
+        ),
+        (
+            where,
+            tokens,
+            left,
+            right,
+            top,
+            bottom,
+            1.0 + condition,
+            key0,
+            value0,
+            query0,
+            out0,
+            merge_one,
+            split_block,
+        ),
         6,
         smem=(0,),
+        out_far=(0, 1),
+        scratch=(
+            pltpu.VMEM((128, 384), BF),
+            pltpu.VMEM((32, 768), BF),
+            pltpu.SemaphoreType.DMA((2,)),
+        ),
         name="finest",
     )
     band = exchange(band, COL)
-    mid, mids = call(
+    mid, mids, split_block = call(
         middle_kernel,
         (shaped((64, 192), BF), shaped((512, 192), BF)),
-        (band, merge_block),
+        (band, weight),
         2,
+        through=(split_block,),
         name="middle",
     )
     mids = exchange(mids, COL)
-    q, kv = call(
+    q, kv, split_block = call(
         project_kernel,
-        (shaped((64, 192), BF), shaped((512, 384), BF)),
-        (mids, gain_two.reshape(8, 192), query2, key2, value2),
+        (shaped((64, 192), BF), shaped((512, 384), BF), shaped((192, 384), BF)),
+        (
+            where,
+            mids,
+            gain_two.reshape(8, 192),
+            query2.T,
+            key2.T,
+            value2.T,
+            split_block,
+            *others(split_block),
+        ),
         2,
+        smem=(0,),
         name="project",
     )
+    split_block = lax.all_gather(split_block, "z", axis=0, tiled=False)
     q_other = lax.ppermute(q, "yh", swap("yh"))
     kv = exchange(kv, "z")
     kv = lax.all_gather(kv, "k", axis=0, tiled=True)
@@ -330,12 +451,18 @@
         name="attend",
     )
     theirs = lax.ppermute(other, "yh", swap("yh"))
-    parts = call(combine_kernel, shaped((512, 192), BF), (own, theirs, out2), 1, name="combine")
+    parts = call(combine_kernel, [shaped((512, 192), BF)], (own, theirs, out2), 1, name="combine")
     parts = exchange(parts, COL)
-    up = call(lift_kernel, shaped((64, 3072), BF), (parts, mid, split_block), 1, name="lift")
+    up = call(
+        lift_kernel,
+        [shaped((64, 3072), BF)],
+        (parts, mid, split_block),
+        1,
+        name="lift",
+    )
     up = exchange(up, COL)
     return call(
-        last_kernel, shaped((8, 16, 384), BF), (up, level1, resid, split_one), 2, name="last"
+        last_kernel, [shaped((8, 16, 384), BF)], (up, level1, resid, split_one), 2, name="last"
     )
 
 

time: 160 us -> 143 us (0.89)
  blocking collectives: 19.1 us -> 40.2 us
  starting transfers between devices: 50 us -> 35.4 us
  waiting for transfers between devices: 48.4 us -> 33.9 us
  local copies, waits for them, and re-layouts: 12 us -> 3.73 us
  other arithmetic: 2.59 us -> 0.06 us
  Pallas kernels: 12.2 us -> 13.8 us
    all_to_all x1 -> x3, blocking collectives: 10.5 us -> 37.8 us  [exchange(): return lax.all_to_all(block, axis, split_axis=0, concat_axis=0, tiled=True)]
    all_to_all x5 -> x2, waiting for transfers between devices: 40.1 us -> 13.8 us  [exchange(): return lax.all_to_all(block, axis, split_axis=0, concat_axis=0, tiled=True)]
    all_to_all x5 -> x2, starting transfers between devices: 28.5 us -> 10.1 us  [exchange(): return lax.all_to_all(block, axis, split_axis=0, concat_axis=0, tiled=True)]
    ppermute x4 -> x8, waiting for transfers between devices: 3.52 us -> 13.6 us  [the longest x2 7.15 us: others(): lax.ppermute(block, 'yh', swap('yh'))]
    all_gather x1 -> x0, blocking collectives: 6.18 us -> none  [on_device(): split_block = lax.all_gather(split_block, 'k', axis=0, tiled=True)]
    unnamed x41 -> x38, local copies, waits for them, and re-layouts: 9.55 us -> 3.56 us
    ppermute x1, starting transfers between devices: 0.33 us -> 2.4 us  [on_device(): q_other = lax.ppermute(q, 'yh', swap('yh'))]
    select_n x2 -> x0, other arithmetic: 1.75 us -> none  [in_order(): low = jnp.where(first, block, other)]
  transfers between devices with their start and end apart: 16 -> 17, of which waited for: 7 -> 9; matrix products, arithmetic and copies ran while one was open for 5% -> 0% of each run, Pallas kernels for 7% -> 5%
where the time goes in v2:
time: 143 us; the launch traced here: 142 us
  blocking collectives  40.2 us (28%)
  starting transfers between devices  35.4 us (25%)
  waiting for transfers between devices  33.9 us (24%)
  between operations  14.3 us (10%)
  Pallas kernels  13.8 us (10%)
  local copies, waits for them, and re-layouts  3.73 us (3%)
    all_to_all x3, blocking collectives, exchange(): return lax.all_to_all(block, axis, split_axis=0, concat_axis=0, tiled=True)  37.8 us
    pallas_call x9, Pallas kernels, call(): pl.pallas_call(kernel, out_shape=out_shape, in_specs=specs, out_specs=out...  13.8 us
    all_to_all x2, waiting for transfers between devices, exchange(): return lax.all_to_all(block, axis, split_axis=0, concat_axis=0, tiled=True)  13.8 us
    all_to_all x2, starting transfers between devices, exchange(): return lax.all_to_all(block, axis, split_axis=0, concat_axis=0, tiled=True)  10.1 us
    ppermute x2, waiting for transfers between devices, others(): lax.ppermute(block, 'yh', swap('yh'))  7.15 us
    ppermute x2, starting transfers between devices, others(): lax.ppermute(block, 'k', swap('k'))  5.12 us
    ppermute x1, starting transfers between devices, on_device(): left = lax.ppermute(tokens[:, 8:16], COL, shift(COL, 1))  4.45 us
    ppermute x1, waiting for transfers between devices, on_device(): bottom = lax.ppermute(first, ROW, shift(ROW, -1))  3.8 us
  transfers between devices with their start and end apart: 17, of which 9 were waited for; matrix products, arithmetic and copies ran while one was open for 0% of the time, Pallas kernels for 5%

profile of v2, /device:TPU:8, one launch (start us, length us, event | category | flops | bytes accessed | tf_op | source)
XLA Modules:
  0.0 141.7 jit_solution(9604806434219095920)
XLA Ops:
  6.6 2.4 %collective-permute-start.6 = (bf16[96,192]{1,0:T(8,128)(2,1)}, bf16[96,192]{1,0:T(8,128)(2,1)S(1)}, u32[]{:S(2)}, u32[]{:S(2)}) collective-permute-start(bf16[96,192]{1,0:T(8,128)(2,1)} %refs_1_.3), channel_id=1, source_target_pairs={{0,128},{128,0},{1,129},{129,1},{2,130},{130,2},{3,131},{131,3},{4... | collective-permute-start | bytes 110600 | tf_op jit(solution)/shard_map/ppermute | solution.py:361
  10.0 2.4 %collective-permute-done.6.refs_3_ = bf16[96,192]{1,0:T(8,128)(2,1)S(1)} collective-permute-done((bf16[96,192]{1,0:T(8,128)(2,1)}, bf16[96,192]{1,0:T(8,128)(2,1)S(1)}, u32[]{:S(2)}, u32[]{:S(2)}) %collective-permute-start.6) | collective-permute-done | bytes 36896 | tf_op jit(solution)/shard_map/ppermute | solution.py:361
  12.4 1.9 %collective-permute-done.7.refs_4_ = bf16[96,192]{1,0:T(8,128)(2,1)S(1)} collective-permute-done((bf16[96,192]{1,0:T(8,128)(2,1)}, bf16[96,192]{1,0:T(8,128)(2,1)S(1)}, u32[]{:S(2)}, u32[]{:S(2)}) %collective-permute-start.7) | collective-permute-done | bytes 36896 | tf_op jit(solution)/shard_map/ppermute | solution.py:362
  16.6 4.4 %collective-permute-start = (bf16[8,8,384]{2,1,0:T(8,128)(2,1)S(1)}, bf16[8,8,384]{2,1,0:T(8,128)(2,1)S(1)}, u32[]{:S(2)}, u32[]{:S(2)}) collective-permute-start(bf16[8,8,384]{2,1,0:T(8,128)(2,1)S(1)} %get-tuple-element.34), channel_id=1, source_target_pairs={{0,1},{1,2},{2,3},{3,4},{4,5},{5,6},{6,7},{8,9},{9,10},{10,11},{11... | collective-permute-start | bytes 147464 | tf_op jit(solution)/shard_map/ppermute | solution.py:336
  21.0 1.9 %collective-permute-start.1 = (bf16[8,8,384]{2,1,0:T(8,128)(2,1)S(1)}, bf16[8,8,384]{2,1,0:T(8,128)(2,1)S(1)}, u32[]{:S(2)}, u32[]{:S(2)}) collective-permute-start(bf16[8,8,384]{2,1,0:T(8,128)(2,1)S(1)} %get-tuple-element.33), channel_id=1, source_target_pairs={{1,0},{2,1},{3,2},{4,3},{5,4},{6,5},{7,6},{9,8},{10,9},{11,10},{12... | collective-permute-start | bytes 147464 | tf_op jit(solution)/shard_map/ppermute | solution.py:337
  23.0 2.4 %collective-permute-start.4 = (bf16[48,384]{1,0:T(8,128)(2,1)S(1)}, bf16[48,384]{1,0:T(8,128)(2,1)S(1)}, u32[]{:S(2)}, u32[]{:S(2)}) collective-permute-start(bf16[48,384]{1,0:T(8,128)(2,1)S(1)} %copy-done.18), channel_id=1, source_target_pairs={{0,0},{1,16},{2,32},{3,48},{4,64},{5,80},{6,96},{7,112},{8,8},{9,2... | collective-permute-start | bytes 110600 | tf_op jit(solution)/shard_map/ppermute | solution.py:370
  26.4 1.7 %collective-permute-done.1.refs_2_.refs_3_ = bf16[8,8,384]{2,1,0:T(8,128)(2,1)S(1)} collective-permute-done((bf16[8,8,384]{2,1,0:T(8,128)(2,1)S(1)}, bf16[8,8,384]{2,1,0:T(8,128)(2,1)S(1)}, u32[]{:S(2)}, u32[]{:S(2)}) %collective-permute-start.1) | collective-permute-done | bytes 49184 | tf_op jit(solution)/shard_map/ppermute | solution.py:337
  30.7 3.8 %collective-permute-done.3.refs_5_ = bf16[3,32,384]{2,1,0:T(8,128)(2,1)S(1)} collective-permute-done((bf16[3,32,384]{2,1,0:T(8,128)(2,1)S(1)}, bf16[3,32,384]{2,1,0:T(8,128)(2,1)S(1)}, u32[]{:S(2)}, u32[]{:S(2)}) %collective-permute-start.3) | collective-permute-done | bytes 73760 | tf_op jit(solution)/shard_map/ppermute | solution.py:342
  34.6 5.3 %finest.1 = (bf16[128,384]{1,0:T(8,128)(2,1)}, bf16[32,768]{1,0:T(8,128)(2,1)}, bf16[64,3072]{1,0:T(8,128)(2,1)S(1)}, bf16[48,384]{1,0:T(8,128)(2,1)S(1)}) custom-call(s32[7]{0:T(128)S(1)} %stack.23.refs_0_, bf16[8,16,384]{2,1,0:T(8,128)(2,1)S(1)} %copy-done.1, bf16[8,8,384]{2,1,0:T(8,128)(2,1)S(1)} %collective-permute-done.refs_1_.refs_2_, ...), custom_call_target="tpu_custom_call" | custom-call | flops 6000000000 | bytes 18000000 | tf_op jit(solution)/shard_map/finest/pallas_call | solution.py:84
  39.9 16.0 %all_to_all.56 = bf16[8,8,3072]{2,1,0:T(8,128)(2,1)S(1)} all-to-all(bf16[8,8,3072]{2,1,0:T(8,128)(2,1)S(1)} %bitcast.24), channel_id=1, replica_groups=mesh['yh'=2,'z'=8,'k'=2,'x'=4,'yl'=2] {'x','yl'}, dimensions={0} | all-to-all | bytes 786432 | tf_op jit(solution)/shard_map/all_to_all | solution.py:35
  55.8 1.6 %all-gather.4.cloned.1.call-done.refs_1_ = bf16[1536,384]{1,0:T(8,128)(2,1)} async-done(((bf16[192,384]{1,0:T(8,128)(2,1)}), bf16[1536,384]{1,0:T(8,128)(2,1)}) %all-gather.4.cloned.1.call-update) | async-done | bytes 1179664 | tf_op jit(solution)/shard_map/all_gather | solution.py:380
  60.0 6.6 %all-to-all-start.1 = ((bf16[8,64,192]{2,1,0:T(8,128)(2,1)}), bf16[8,64,192]{2,1,0:T(8,128)(2,1)S(1)}, u32[]{:S(2)}, u32[]{:S(2)}) async-start(bf16[8,64,192]{2,1,0:T(8,128)(2,1)} %bitcast.10), calls=%async_computation.1 | async-start | bytes 524288 | tf_op jit(solution)/shard_map/all_to_all | solution.py:35
  67.0 5.1 %collective-permute-start.8 = (bf16[48,384]{1,0:T(8,128)(2,1)S(1)}, bf16[48,384]{1,0:T(8,128)(2,1)S(1)}, u32[]{:S(2)}, u32[]{:S(2)}) collective-permute-start(bf16[48,384]{1,0:T(8,128)(2,1)S(1)} %get-tuple-element.24.refs_6_), channel_id=1, source_target_pairs={{0,8},{8,0},{1,9},{9,1},{2,10},{10,2},{3,11},{11,3},{4,12},{12,4},... | collective-permute-start | bytes 110600 | tf_op jit(solution)/shard_map/ppermute | solution.py:360
  73.0 4.7 %collective-permute-done.9.refs_8_ = bf16[48,384]{1,0:T(8,128)(2,1)S(1)} collective-permute-done((bf16[48,384]{1,0:T(8,128)(2,1)S(1)}, bf16[48,384]{1,0:T(8,128)(2,1)S(1)}, u32[]{:S(2)}, u32[]{:S(2)}) %collective-permute-start.9) | collective-permute-done | bytes 36896 | tf_op jit(solution)/shard_map/ppermute | solution.py:361
  77.7 2.4 %project.1 = (bf16[64,192]{1,0:T(8,128)(2,1)S(1)}, bf16[512,384]{1,0:T(8,128)(2,1)}, bf16[192,384]{1,0:T(8,128)(2,1)}) custom-call(s32[7]{0:T(128)S(1)} %stack.23.refs_0_, bf16[512,192]{1,0:T(8,128)(2,1)S(1)} %bitcast.28, f32[8,192]{1,0:T(8,128)S(1)} %reshape.21.refs_2_, bf16[192,1536]{1,0:T(8,128)(2,1)S(1)} %bitcast.32, bf16[192,1536]{1,0:T(8,128)(2,1)S(1)} %bitcast.33, ...), custom_call_target="tpu_custom_call" | custom-call | flops 2000000000 | bytes 6000000 | tf_op jit(solution)/shard_map/project/pallas_call | solution.py:84
  80.1 3.5 %all-to-all-start.2 = ((bf16[8,64,384]{2,1,0:T(8,128)(2,1)}), bf16[8,64,384]{2,1,0:T(8,128)(2,1)S(1)}, u32[]{:S(2)}, u32[]{:S(2)}) async-start(bf16[8,64,384]{2,1,0:T(8,128)(2,1)} %bitcast.15), calls=%async_computation.2 | async-start | bytes 786432 | tf_op jit(solution)/shard_map/all_to_all | solution.py:35
  83.6 2.4 %collective-permute-start.11 = (bf16[64,192]{1,0:T(8,128)(2,1)S(1)}, bf16[64,192]{1,0:T(8,128)(2,1)S(1)}, u32[]{:S(2)}, u32[]{:S(2)}) collective-permute-start(bf16[64,192]{1,0:T(8,128)(2,1)S(1)} %get-tuple-element.25.refs_0_), channel_id=1, source_target_pairs={{0,128},{128,0},{1,129},{129,1},{2,130},{130,2},{3,131},{131,3},{4... | collective-permute-start | bytes 73736 | tf_op jit(solution)/shard_map/ppermute | solution.py:443
  86.0 13.8 %all-to-all-done.2 = bf16[8,64,384]{2,1,0:T(8,128)(2,1)S(1)} async-done(((bf16[8,64,384]{2,1,0:T(8,128)(2,1)}), bf16[8,64,384]{2,1,0:T(8,128)(2,1)S(1)}, u32[]{:S(2)}, u32[]{:S(2)}) %all-to-all-start.2) | async-done | bytes 393248 | tf_op jit(solution)/shard_map/all_to_all | solution.py:35
  99.8 2.4 %all_gather.13.refs_2_ = bf16[1024,384]{1,0:T(8,128)(2,1)S(1)} all-gather(bf16[512,384]{1,0:T(8,128)(2,1)S(1)} %bitcast.35), channel_id=1, replica_groups=mesh['yh'=2,'z'=8,'k'=2,'x'=4,'yl'=2] {'k'}, dimensions={0}, use_global_device_ids=true | all-gather | bytes 1179648 | tf_op jit(solution)/shard_map/all_gather | solution.py:445
  103.4 2.7 %collective-permute-start.12 = (f32[64,256]{1,0:T(8,128)S(1)}, f32[64,256]{1,0:T(8,128)S(1)}, u32[]{:S(2)}, u32[]{:S(2)}) collective-permute-start(f32[64,256]{1,0:T(8,128)S(1)} %get-tuple-element.28), channel_id=1, source_target_pairs={{0,128},{128,0},{1,129},{129,1},{2,130},{130,2},{3,131},{131,3},{4... | collective-permute-start | bytes 196616 | tf_op jit(solution)/shard_map/ppermute | solution.py:453
  106.1 3.2 %collective-permute-done.12.refs_1_ = f32[64,256]{1,0:T(8,128)S(1)} collective-permute-done((f32[64,256]{1,0:T(8,128)S(1)}, f32[64,256]{1,0:T(8,128)S(1)}, u32[]{:S(2)}, u32[]{:S(2)}) %collective-permute-start.12) | collective-permute-done | bytes 65568 | tf_op jit(solution)/shard_map/ppermute | solution.py:453
  109.9 11.3 %all_to_all.57 = bf16[8,64,192]{2,1,0:T(8,128)(2,1)S(1)} all-to-all(bf16[8,64,192]{2,1,0:T(8,128)(2,1)S(1)} %bitcast.30), channel_id=1, replica_groups=mesh['yh'=2,'z'=8,'k'=2,'x'=4,'yl'=2] {'x','yl'}, dimensions={0} | all-to-all | bytes 393216 | tf_op jit(solution)/shard_map/all_to_all | solution.py:35
  121.2 1.4 %copy-done.5 = bf16[1536,384]{1,0:T(8,128)(2,1)S(1)} copy-done((bf16[1536,384]{1,0:T(8,128)(2,1)S(1)}, bf16[1536,384]{1,0:T(8,128)(2,1)}, u32[]{:S(2)}) %copy-start.5) | copy-done | bytes 1179672
  123.0 10.5 %all_to_all.58 = bf16[8,8,3072]{2,1,0:T(8,128)(2,1)S(1)} all-to-all(bf16[8,8,3072]{2,1,0:T(8,128)(2,1)S(1)} %bitcast.27), channel_id=1, replica_groups=mesh['yh'=2,'z'=8,'k'=2,'x'=4,'yl'=2] {'x','yl'}, dimensions={0} | all-to-all | bytes 786432 | tf_op jit(solution)/shard_map/all_to_all | solution.py:35
  (71 shorter events, 13.6 us)
Async XLA Ops:
  6.5 19.5 %copy-start = (f32[256,384]{1,0:T(8,128)S(1)}, f32[256,384]{1,0:T(8,128)}, u32[]{:S(2)}) copy-start(f32[256,384]{1,0:T(8,128)} %param.18) | copy-start | bytes 1179652
  6.5 50.9 %all-gather.4.cloned.1.call-start = ((), (), s32[]{:S(2)}) async-start(), calls=%async_computation.5 | async-start | bytes 1327104 | tf_op jit(solution)/shard_map/all_gather | solution.py:380
  6.5 3.5 %collective-permute-start.5 = (bf16[96,192]{1,0:T(8,128)(2,1)}, bf16[96,192]{1,0:T(8,128)(2,1)S(1)}, u32[]{:S(2)}, u32[]{:S(2)}) collective-permute-start(bf16[96,192]{1,0:T(8,128)(2,1)} %refs_1_.3), channel_id=1, source_target_pairs={{0,8},{8,0},{1,9},{9,1},{2,10},{10,2},{3,11},{11,3},{4,12},{12,4},... | collective-permute-start | bytes 110600 | tf_op jit(solution)/shard_map/ppermute | solution.py:360
  6.6 5.9 %collective-permute-start.6 = (bf16[96,192]{1,0:T(8,128)(2,1)}, bf16[96,192]{1,0:T(8,128)(2,1)S(1)}, u32[]{:S(2)}, u32[]{:S(2)}) collective-permute-start(bf16[96,192]{1,0:T(8,128)(2,1)} %refs_1_.3), channel_id=1, source_target_pairs={{0,128},{128,0},{1,129},{129,1},{2,130},{130,2},{3,131},{131,3},{4... | collective-permute-start | bytes 110600 | tf_op jit(solution)/shard_map/ppermute | solution.py:361
  8.9 5.4 %collective-permute-start.7 = (bf16[96,192]{1,0:T(8,128)(2,1)}, bf16[96,192]{1,0:T(8,128)(2,1)S(1)}, u32[]{:S(2)}, u32[]{:S(2)}) collective-permute-start(bf16[96,192]{1,0:T(8,128)(2,1)} %refs_1_.3), channel_id=1, source_target_pairs={{0,136},{8,128},{128,8},{136,0},{1,137},{9,129},{129,9},{137,1},{2... | collective-permute-start | bytes 110600 | tf_op jit(solution)/shard_map/ppermute | solution.py:362
  16.5 18.1 %copy-start.11 = (bf16[384,384]{1,0:T(8,128)(2,1)S(1)}, bf16[384,384]{1,0:T(8,128)(2,1)}, u32[]{:S(2)}) copy-start(bf16[384,384]{1,0:T(8,128)(2,1)} %refs_8_.1) | copy-start | bytes 884740
  16.6 9.8 %collective-permute-start = (bf16[8,8,384]{2,1,0:T(8,128)(2,1)S(1)}, bf16[8,8,384]{2,1,0:T(8,128)(2,1)S(1)}, u32[]{:S(2)}, u32[]{:S(2)}) collective-permute-start(bf16[8,8,384]{2,1,0:T(8,128)(2,1)S(1)} %get-tuple-element.34), channel_id=1, source_target_pairs={{0,1},{1,2},{2,3},{3,4},{4,5},{5,6},{6,7},{8,9},{9,10},{10,11},{11... | collective-permute-start | bytes 147464 | tf_op jit(solution)/shard_map/ppermute | solution.py:336
  21.0 7.0 %collective-permute-start.1 = (bf16[8,8,384]{2,1,0:T(8,128)(2,1)S(1)}, bf16[8,8,384]{2,1,0:T(8,128)(2,1)S(1)}, u32[]{:S(2)}, u32[]{:S(2)}) collective-permute-start(bf16[8,8,384]{2,1,0:T(8,128)(2,1)S(1)} %get-tuple-element.33), channel_id=1, source_target_pairs={{1,0},{2,1},{3,2},{4,3},{5,4},{6,5},{7,6},{9,8},{10,9},{11,10},{12... | collective-permute-start | bytes 147464 | tf_op jit(solution)/shard_map/ppermute | solution.py:337
  23.0 7.8 %collective-permute-start.4 = (bf16[48,384]{1,0:T(8,128)(2,1)S(1)}, bf16[48,384]{1,0:T(8,128)(2,1)S(1)}, u32[]{:S(2)}, u32[]{:S(2)}) collective-permute-start(bf16[48,384]{1,0:T(8,128)(2,1)S(1)} %copy-done.18), channel_id=1, source_target_pairs={{0,0},{1,16},{2,32},{3,48},{4,64},{5,80},{6,96},{7,112},{8,8},{9,2... | collective-permute-start | bytes 110600 | tf_op jit(solution)/shard_map/ppermute | solution.py:370
  28.1 2.6 %collective-permute-start.2 = (bf16[3,32,384]{2,1,0:T(8,128)(2,1)S(1)}, bf16[3,32,384]{2,1,0:T(8,128)(2,1)S(1)}, u32[]{:S(2)}, u32[]{:S(2)}) collective-permute-start(bf16[3,32,384]{2,1,0:T(8,128)(2,1)S(1)} %get-tuple-element.19), channel_id=1, source_target_pairs={{0,8},{8,16},{16,24},{24,32},{32,40},{40,48},{48,56},{56,64},{64,7... | collective-permute-start | bytes 221192 | tf_op jit(solution)/shard_map/ppermute | solution.py:341
  29.4 5.1 %collective-permute-start.3 = (bf16[3,32,384]{2,1,0:T(8,128)(2,1)S(1)}, bf16[3,32,384]{2,1,0:T(8,128)(2,1)S(1)}, u32[]{:S(2)}, u32[]{:S(2)}) collective-permute-start(bf16[3,32,384]{2,1,0:T(8,128)(2,1)S(1)} %get-tuple-element.20), channel_id=1, source_target_pairs={{8,0},{16,8},{24,16},{32,24},{40,32},{48,40},{56,48},{64,56},{72,6... | collective-permute-start | bytes 221192 | tf_op jit(solution)/shard_map/ppermute | solution.py:342
  58.7 19.0 %copy-start.6 = (bf16[1536,192]{0,1:T(8,128)(2,1)S(1)}, bf16[1536,192]{0,1:T(8,128)(2,1)}, u32[]{:S(2)}) copy-start(bf16[1536,192]{0,1:T(8,128)(2,1)} %param.26) | copy-start | bytes 1769476
  58.7 19.0 %copy-start.7 = (bf16[1536,192]{0,1:T(8,128)(2,1)S(1)}, bf16[1536,192]{0,1:T(8,128)(2,1)}, u32[]{:S(2)}) copy-start(bf16[1536,192]{0,1:T(8,128)(2,1)} %param.27) | copy-start | bytes 1769476
  58.7 19.0 %copy-start.8 = (bf16[1536,192]{0,1:T(8,128)(2,1)S(1)}, bf16[1536,192]{0,1:T(8,128)(2,1)}, u32[]{:S(2)}) copy-start(bf16[1536,192]{0,1:T(8,128)(2,1)} %param.28) | copy-start | bytes 1769476
  60.0 17.7 %all-to-all-start.1 = ((bf16[8,64,192]{2,1,0:T(8,128)(2,1)}), bf16[8,64,192]{2,1,0:T(8,128)(2,1)S(1)}, u32[]{:S(2)}, u32[]{:S(2)}) async-start(bf16[8,64,192]{2,1,0:T(8,128)(2,1)} %bitcast.10), calls=%async_computation.1 | async-start | bytes 524288 | tf_op jit(solution)/shard_map/all_to_all | solution.py:35
  66.6 54.6 %all-gather.6.cloned.1.call-start = ((), (), s32[]{:S(2)}) async-start(), calls=%async_computation.6 | async-start | bytes 1327104 | tf_op jit(solution)/shard_map/all_gather | solution.py:442
  66.6 5.6 %collective-permute-start.10 = (bf16[48,384]{1,0:T(8,128)(2,1)S(1)}, bf16[48,384]{1,0:T(8,128)(2,1)S(1)}, u32[]{:S(2)}, u32[]{:S(2)}) collective-permute-start(bf16[48,384]{1,0:T(8,128)(2,1)S(1)} %get-tuple-element.24.refs_6_), channel_id=1, source_target_pairs={{0,136},{8,128},{128,8},{136,0},{1,137},{9,129},{129,9},{137,1},{2... | collective-permute-start | bytes 110600 | tf_op jit(solution)/shard_map/ppermute | solution.py:362
  67.0 6.0 %collective-permute-start.8 = (bf16[48,384]{1,0:T(8,128)(2,1)S(1)}, bf16[48,384]{1,0:T(8,128)(2,1)S(1)}, u32[]{:S(2)}, u32[]{:S(2)}) collective-permute-start(bf16[48,384]{1,0:T(8,128)(2,1)S(1)} %get-tuple-element.24.refs_6_), channel_id=1, source_target_pairs={{0,8},{8,0},{1,9},{9,1},{2,10},{10,2},{3,11},{11,3},{4,12},{12,4},... | collective-permute-start | bytes 110600 | tf_op jit(solution)/shard_map/ppermute | solution.py:360
  72.1 5.6 %collective-permute-start.9 = (bf16[48,384]{1,0:T(8,128)(2,1)S(1)}, bf16[48,384]{1,0:T(8,128)(2,1)S(1)}, u32[]{:S(2)}, u32[]{:S(2)}) collective-permute-start(bf16[48,384]{1,0:T(8,128)(2,1)S(1)} %get-tuple-element.24.refs_6_), channel_id=1, source_target_pairs={{0,128},{128,0},{1,129},{129,1},{2,130},{130,2},{3,131},{131,3},{4... | collective-permute-start | bytes 110600 | tf_op jit(solution)/shard_map/ppermute | solution.py:361
  80.1 19.6 %all-to-all-start.2 = ((bf16[8,64,384]{2,1,0:T(8,128)(2,1)}), bf16[8,64,384]{2,1,0:T(8,128)(2,1)S(1)}, u32[]{:S(2)}, u32[]{:S(2)}) async-start(bf16[8,64,384]{2,1,0:T(8,128)(2,1)} %bitcast.15), calls=%async_computation.2 | async-start | bytes 786432 | tf_op jit(solution)/shard_map/all_to_all | solution.py:35
  83.6 18.5 %collective-permute-start.11 = (bf16[64,192]{1,0:T(8,128)(2,1)S(1)}, bf16[64,192]{1,0:T(8,128)(2,1)S(1)}, u32[]{:S(2)}, u32[]{:S(2)}) collective-permute-start(bf16[64,192]{1,0:T(8,128)(2,1)S(1)} %get-tuple-element.25.refs_0_), channel_id=1, source_target_pairs={{0,128},{128,0},{1,129},{129,1},{2,130},{130,2},{3,131},{131,3},{4... | collective-permute-start | bytes 73736 | tf_op jit(solution)/shard_map/ppermute | solution.py:443
  103.4 5.9 %collective-permute-start.12 = (f32[64,256]{1,0:T(8,128)S(1)}, f32[64,256]{1,0:T(8,128)S(1)}, u32[]{:S(2)}, u32[]{:S(2)}) collective-permute-start(f32[64,256]{1,0:T(8,128)S(1)} %get-tuple-element.28), channel_id=1, source_target_pairs={{0,128},{128,0},{1,129},{129,1},{2,130},{130,2},{3,131},{131,3},{4... | collective-permute-start | bytes 196616 | tf_op jit(solution)/shard_map/ppermute | solution.py:453
  109.9 23.7 %copy-start.15 = (bf16[128,384]{1,0:T(8,128)(2,1)S(1)}, bf16[128,384]{1,0:T(8,128)(2,1)}, u32[]{:S(2)}) copy-start(bf16[128,384]{1,0:T(8,128)(2,1)} %get-tuple-element.32.refs_2_) | copy-start | bytes 294916
  109.9 23.7 %copy-start.16 = (bf16[32,768]{1,0:T(8,128)(2,1)S(1)}, bf16[32,768]{1,0:T(8,128)(2,1)}, u32[]{:S(2)}) copy-start(bf16[32,768]{1,0:T(8,128)(2,1)} %get-tuple-element.31.refs_1_) | copy-start | bytes 147460
  (12 other events, 126.3 us)
Sparse Core Ops, SparseCore 0:
  16.6 40.7 all-gather.3
  80.3 38.3 all-gather.5

commit v3 on v2

--- a/solution.py
+++ b/solution.py
@@ -114,22 +114,11 @@
     last_out[...] = wide[8 - RADIUS : 8].astype(BF)
 
 
-def ordered(where, own, over_k, over_yh, over_both):
-    blocks = [block[...] for block in (own, over_k, over_yh, over_both)]
-    here = where[5] * 2 + where[4]
-    result = []
-    for i in range(4):
-        row = blocks[3]
-        for j in range(3):
-            row = jnp.where(here == (i ^ j), blocks[j], row)
-        result.append(row)
-    return result
-
-
-def join_kernel(where, own, over_k, over_yh, over_both, out):
-    blocks = [block.astype(F32) for block in ordered(where, own, over_k, over_yh, over_both)]
-    for k in range(2):
-        out[k] = jnp.concatenate([blocks[k], blocks[2 + k]], axis=1).astype(BF)
+def copies_kernel(block, out):
+    floats = block[...].astype(F32)
+    packed = jnp.concatenate([floats[0:48], floats[48:96]], axis=1).astype(BF)
+    for i in range(8):
+        out[i] = packed
 
 
 def finest_kernel(
@@ -140,11 +129,11 @@
     top,
     bottom,
     scale,
-    wk,
-    wv,
-    wq,
-    wo,
-    merge,
+    wk_far,
+    wv_far,
+    wq_far,
+    wo_far,
+    merge_far,
     split,
     resid_out,
     level1_out,
@@ -152,8 +141,20 @@
     split_out,
     resid_near,
     level1_near,
+    wk,
+    wv,
+    wq,
+    wo,
+    merge,
     sent,
+    arrived,
 ):
+    pairs = ((wk_far, wk), (wv_far, wv), (wq_far, wq), (wo_far, wo), (merge_far, merge))
+    fetches = [
+        pltpu.make_async_copy(far, near, arrived.at[i]) for i, (far, near) in enumerate(pairs)
+    ]
+    for fetch in fetches:
+        fetch.start()
     split_out[...] = split[...]
     wide = widen(tokens[...], left[...], right[...])
     floats = jnp.concatenate(
@@ -161,7 +162,9 @@
     ).reshape(448, 384)
     mean = jnp.mean(floats * floats, axis=1, keepdims=True)
     normed = (floats * lax.rsqrt(mean + EPSILON) * scale[...]).astype(BF)
+    fetches[0].wait()
     keys = dot(normed, wk[...]).astype(BF)
+    fetches[1].wait()
     values = dot(normed, wv[...]).astype(BF)
 
     row, col = place_of(lax.broadcasted_iota(jnp.int32, (128, 448), 0))
@@ -170,6 +173,7 @@
     key_col = jnp.where(slot < 16, slot, jnp.where(slot < 24, slot - 24, slot - 8))
     pick = ((key_row == row) & (slot == col)).astype(F32).astype(BF)
     mine = dot(pick, floats.astype(BF))
+    fetches[2].wait()
     queries = dot(dot(pick, normed).astype(BF), wq[...]).astype(BF)
 
     global_row, global_col = key_row + where[0], key_col + where[1]
@@ -192,10 +196,12 @@
             outs.append(dot(weights, values[:, cut]))
         blocks.append(jnp.where(lane < HEAD, outs[0], outs[1]))
     attended = jnp.concatenate(blocks, axis=1).astype(BF)
+    fetches[3].wait()
     resid = (mine + dot(attended, wo[...])).astype(BF)
     resid_near[...] = resid
     send_resid = pltpu.make_async_copy(resid_near, resid_out, sent.at[0])
     send_resid.start()
+    fetches[4].wait()
     level1 = jnp.zeros((32, 768), F32)
     for pos in range(4):
         level1 += dot(resid[32 * pos : 32 * pos + 32], merge[384 * pos : 384 * pos + 384, :])
@@ -208,18 +214,23 @@
     send_level1.wait()
 
 
-def middle_kernel(band, weight, mid_out, copies_out):
-    low = dot(band[:, 0:1536], weight[...])[:, 0:192]
-    high = dot(band[:, 1536:3072], weight[...])[:, 192:384]
-    mid = (low + high).astype(BF)
+def middle_kernel(where, band, own, over_k, over_yh, over_both, mid_out, copies_out):
+    here = where[5] * 2 + where[4]
+    blocks = []
+    for yh in range(2):
+        for z in range(8):
+            for k in range(2):
+                block = over_both[z]
+                for j, ref in enumerate((own, over_k, over_yh)):
+                    block = jnp.where(here == ((yh * 2 + k) ^ j), ref[z], block)
+                blocks += [block[:, 0:192], block[:, 192:384]]
+    mid = dot(band[...], jnp.concatenate(blocks, axis=0)).astype(BF)
     mid_out[...] = mid
     copies_out[...] = jnp.concatenate([mid] * 8, axis=0)
 
 
-def project_kernel(
-    where, mids, gain, wq, wk, wv, own, over_k, over_yh, over_both, q_out, kv_out, split_out
-):
-    split_out[...] = jnp.concatenate(ordered(where, own, over_k, over_yh, over_both), axis=0)
+def project_kernel(mids, gain, wq, wk, wv, split, over_yh, q_out, kv_out, split_out):
+    split_out[...] = jnp.concatenate([split[...], over_yh[...]], axis=0)
     parts = [mids[64 * i : 64 * i + 64, :].astype(F32) for i in range(8)]
     total = jnp.zeros((64, 1), F32)
     for part in parts:
@@ -236,7 +247,10 @@
     kv_out[...] = jnp.concatenate([both] * 8, axis=0)
 
 
-def attend_kernel(q_own, q_other, kv, own_out, other_out):
+def attend_kernel(q_own, q_other, kv, *refs):
+    (own_out, other_out, stack_out), blocks = refs[8:], refs[:8]
+    for i, block in enumerate(blocks):
+        stack_out[i] = block[...]
     queries = jnp.concatenate([q_own[...], q_other[...]], axis=0)
     lane = lax.broadcasted_iota(jnp.int32, (1, 128), 1)
     low = (lane < HEAD).astype(F32).astype(BF)
@@ -284,13 +298,21 @@
     ).astype(BF)
 
 
-def lift_kernel(parts, mid, weight, up_out):
+def lift_kernel(where, parts, mid, weight, over_k, up_out):
     sums = mid[...].astype(F32)
     for i in range(8):
         sums += parts[64 * i : 64 * i + 64, :].astype(F32)
     lifted = sums.astype(BF)
+    here = where[5] * 2 + where[4]
+    source = lax.broadcasted_iota(jnp.int32, (192, 192), 0)
+    target = lax.broadcasted_iota(jnp.int32, (192, 192), 1)
+    turn = (target // 48) % 2 * 2 + target // 96
+    same = (source // 48 == turn ^ here) & (source % 48 == target % 48)
+    lifted = dot(lifted, same.astype(F32).astype(BF)).astype(BF)
     for i in range(8):
-        up_out[:, 384 * i : 384 * i + 384] = dot(lifted, weight[i]).astype(BF)
+        rows = jnp.concatenate([weight[i], over_k[i]], axis=0)
+        column = pl.multiple_of(lax.rem(where[6] + 8 - i, 8) * 384, 128)
+        up_out[:, pl.ds(column, 384)] = dot(lifted, rows).astype(BF)
 
 
 def last_kernel(parts, level1, resid, split, out):
@@ -352,7 +374,7 @@
             jnp.int32(16 * lax.axis_size(COL)),
             lax.axis_index("k"),
             lax.axis_index("yh"),
-            lax.axis_index(COL),
+            lax.axis_index("z"),
         ]
     ).astype(jnp.int32)
     def others(block):
@@ -369,16 +391,9 @@
             perm.append((row * 8 + col, ((yh * 8 + col) * 2 + k) * 8 + row // 4))
     split_block = lax.ppermute(split_two, ROW + COL, perm)
 
-    weight = call(
-        join_kernel,
-        [shaped((2, 96, 384), BF)],
-        (where, merge_two, *others(merge_two)),
-        1,
-        smem=(0,),
-        name="join",
-    )
-    weight = lax.all_gather(weight.reshape(192, 384), "z", axis=0, tiled=True)
-
+    merge_own = call(copies_kernel, [shaped((8, 48, 384), BF)], (merge_two,), 1, name="copies")
+    merge_own = exchange(merge_own, "z")
+    merge_yh = lax.ppermute(merge_own, "yh", swap("yh"))
     resid, level1, band, split_block = call(
         finest_kernel,
         (
@@ -408,56 +423,66 @@
         scratch=(
             pltpu.VMEM((128, 384), BF),
             pltpu.VMEM((32, 768), BF),
+            *[pltpu.VMEM((384, 384), BF) for _ in range(4)],
+            pltpu.VMEM((1536, 768), BF),
             pltpu.SemaphoreType.DMA((2,)),
+            pltpu.SemaphoreType.DMA((5,)),
         ),
+        far=(7, 8, 9, 10, 11),
+        vmem=60,
         name="finest",
     )
     band = exchange(band, COL)
-    mid, mids, split_block = call(
+    over_yh = lax.ppermute(split_block, "yh", swap("yh"))
+    merge_k, merge_both = [lax.ppermute(w, "k", swap("k")) for w in (merge_own, merge_yh)]
+    mid, mids = call(
         middle_kernel,
         (shaped((64, 192), BF), shaped((512, 192), BF)),
-        (band, weight),
+        (where, band, merge_own, merge_k, merge_yh, merge_both),
         2,
-        through=(split_block,),
+        smem=(0,),
         name="middle",
     )
     mids = exchange(mids, COL)
     q, kv, split_block = call(
         project_kernel,
-        (shaped((64, 192), BF), shaped((512, 384), BF), shaped((192, 384), BF)),
+        (shaped((64, 192), BF), shaped((512, 384), BF), shaped((96, 384), BF)),
         (
-            where,
             mids,
             gain_two.reshape(8, 192),
             query2.T,
             key2.T,
             value2.T,
             split_block,
-            *others(split_block),
+            over_yh,
         ),
         2,
-        smem=(0,),
         name="project",
     )
-    split_block = lax.all_gather(split_block, "z", axis=0, tiled=False)
+    split_blocks = [split_block] + [
+        lax.ppermute(split_block, "z", [(i, (i + step) % 8) for i in range(8)])
+        for step in range(1, 8)
+    ]
     q_other = lax.ppermute(q, "yh", swap("yh"))
     kv = exchange(kv, "z")
     kv = lax.all_gather(kv, "k", axis=0, tiled=True)
-    own, other = call(
+    own, other, split_block = call(
         attend_kernel,
-        (shaped((64, 256), F32), shaped((64, 256), F32)),
-        (q, q_other, kv),
+        (shaped((64, 256), F32), shaped((64, 256), F32), shaped((8, 96, 384), BF)),
+        (q, q_other, kv, *split_blocks),
         3,
         name="attend",
     )
     theirs = lax.ppermute(other, "yh", swap("yh"))
+    split_other = lax.ppermute(split_block, "k", swap("k"))
     parts = call(combine_kernel, [shaped((512, 192), BF)], (own, theirs, out2), 1, name="combine")
     parts = exchange(parts, COL)
     up = call(
         lift_kernel,
         [shaped((64, 3072), BF)],
-        (parts, mid, split_block),
+        (where, parts, mid, split_block, split_other),
         1,
+        smem=(0,),
         name="lift",
     )
     up = exchange(up, COL)

time: 143 us -> 137 us (0.958)
  starting transfers between devices: 35.4 us -> 58.5 us
  blocking collectives: 40.2 us -> 24.4 us
  between operations: 14.3 us -> 0.93 us
  waiting for transfers between devices: 33.9 us -> 28.8 us
  Pallas kernels: 13.8 us -> 16.8 us
  local copies, waits for them, and re-layouts: 3.73 us -> 5.87 us
    all_to_all x3 -> x2, blocking collectives: 37.8 us -> 22 us  [exchange(): return lax.all_to_all(block, axis, split_axis=0, concat_axis=0, tiled=True)]
    all_to_all x2 -> x4, starting transfers between devices: 10.1 us -> 21.9 us  [exchange(): return lax.all_to_all(block, axis, split_axis=0, concat_axis=0, tiled=True)]
    ppermute x6 -> x12, starting transfers between devices: 8.94 us -> 19.3 us  [the longest x7 13.8 us: on_device(): lax.ppermute(split_block, 'z', [(i, (i + step) % 8) for i in range(8)])]
    ppermute x1, waiting for transfers between devices: 3.8 us -> 0.01 us  [on_device(): bottom = lax.ppermute(first, ROW, shift(ROW, -1))]
    pallas_call x9, Pallas kernels: 13.8 us -> 16.8 us  [call(): pl.pallas_call(kernel, out_shape=out_shape, in_specs=specs, out_specs=out...]
    ppermute x1, waiting for transfers between devices: 1.66 us -> 0.01 us  [on_device(): right = lax.ppermute(tokens[:, 0:8], COL, shift(COL, -1))]
    all_gather x2 -> x0, waiting for transfers between devices: 1.65 us -> none  [the longest x1 1.64 us: on_device(): weight = lax.all_gather(weight.reshape(192, 384), 'z', axis=0, tiled=True)]
    ppermute x1, starting transfers between devices: 2.38 us -> 3.83 us  [on_device(): split_block = lax.ppermute(split_two, ROW + COL, perm)]
  transfers between devices with their start and end apart: 17 -> 23, of which waited for: 9 -> 10; matrix products, arithmetic and copies ran while one was open for 0% -> 2% of each run, Pallas kernels for 5% -> 7%
where the time goes in v3:
time: 137 us; the launch traced here: 136 us
  starting transfers between devices  58.5 us (43%)
  waiting for transfers between devices  28.8 us (21%)
  blocking collectives  24.4 us (18%)
  Pallas kernels  16.8 us (12%)
  local copies, waits for them, and re-layouts  5.87 us (4%)
    all_to_all x2, blocking collectives, exchange(): return lax.all_to_all(block, axis, split_axis=0, concat_axis=0, tiled=True)  22 us
    all_to_all x4, starting transfers between devices, exchange(): return lax.all_to_all(block, axis, split_axis=0, concat_axis=0, tiled=True)  21.9 us
    pallas_call x9, Pallas kernels, call(): pl.pallas_call(kernel, out_shape=out_shape, in_specs=specs, out_specs=out...  16.8 us
    all_to_all x4, waiting for transfers between devices, exchange(): return lax.all_to_all(block, axis, split_axis=0, concat_axis=0, tiled=True)  14.1 us
    ppermute x7, starting transfers between devices, on_device(): lax.ppermute(split_block, 'z', [(i, (i + step) % 8) for i in range(8)])  13.8 us
    ppermute x7, waiting for transfers between devices, on_device(): lax.ppermute(split_block, 'z', [(i, (i + step) % 8) for i in range(8)])  7.2 us
    ppermute x1, starting transfers between devices, on_device(): left = lax.ppermute(tokens[:, 8:16], COL, shift(COL, 1))  4.82 us
    ppermute x1, waiting for transfers between devices, on_device(): theirs = lax.ppermute(other, 'yh', swap('yh'))  4.29 us
  transfers between devices with their start and end apart: 23, of which 10 were waited for; matrix products, arithmetic and copies ran while one was open for 2% of the time, Pallas kernels for 7%

profile of v3, /device:TPU:8, one launch (start us, length us, event | category | flops | bytes accessed | tf_op | source)
XLA Modules:
  0.0 135.7 jit_solution(2578826654758942806)
XLA Ops:
  0.0 3.8 %collective-permute-start.4 = (bf16[48,384]{1,0:T(8,128)(2,1)}, bf16[48,384]{1,0:T(8,128)(2,1)S(1)}, u32[]{:S(2)}, u32[]{:S(2)}) collective-permute-start(bf16[48,384]{1,0:T(8,128)(2,1)} %param.30), channel_id=1, source_target_pairs={{0,0},{1,16},{2,32},{3,48},{4,64},{5,80},{6,96},{7,112},{8,8},{9,2... | collective-permute-start | bytes 110600 | tf_op jit(solution)/shard_map/ppermute | solution.py:392
  4.7 2.1 %collective-permute-start.1 = (bf16[8,8,384]{2,1,0:T(8,128)(2,1)S(1)}, bf16[8,8,384]{2,1,0:T(8,128)(2,1)S(1)}, u32[]{:S(2)}, u32[]{:S(2)}) collective-permute-start(bf16[8,8,384]{2,1,0:T(8,128)(2,1)S(1)} %get-tuple-element.33), channel_id=1, source_target_pairs={{1,0},{2,1},{3,2},{4,3},{5,4},{6,5},{7,6},{9,8},{10,9},{11,10},{12... | collective-permute-start | bytes 147464 | tf_op jit(solution)/shard_map/ppermute | solution.py:359
  6.8 4.8 %collective-permute-start = (bf16[8,8,384]{2,1,0:T(8,128)(2,1)S(1)}, bf16[8,8,384]{2,1,0:T(8,128)(2,1)S(1)}, u32[]{:S(2)}, u32[]{:S(2)}) collective-permute-start(bf16[8,8,384]{2,1,0:T(8,128)(2,1)S(1)} %get-tuple-element.34), channel_id=1, source_target_pairs={{0,1},{1,2},{2,3},{3,4},{4,5},{5,6},{6,7},{8,9},{9,10},{10,11},{11... | collective-permute-start | bytes 147464 | tf_op jit(solution)/shard_map/ppermute | solution.py:358
  13.2 7.8 %all-to-all-start.1 = ((bf16[8,48,384]{2,1,0:T(8,128)(2,1)}), bf16[8,48,384]{2,1,0:T(8,128)(2,1)S(1)}, u32[]{:S(2)}, u32[]{:S(2)}) async-start(bf16[8,48,384]{2,1,0:T(8,128)(2,1)} %copies.1), calls=%async_computation.1 | async-start | bytes 589824 | tf_op jit(solution)/shard_map/all_to_all | solution.py:35
  26.0 7.1 %all-to-all-done.1.refs_2_ = bf16[8,48,384]{2,1,0:T(8,128)(2,1)S(1)} async-done(((bf16[8,48,384]{2,1,0:T(8,128)(2,1)}), bf16[8,48,384]{2,1,0:T(8,128)(2,1)S(1)}, u32[]{:S(2)}, u32[]{:S(2)}) %all-to-all-start.1) | async-done | bytes 294944 | tf_op jit(solution)/shard_map/all_to_all | solution.py:35
  33.1 2.7 %collective-permute-start.6 = (bf16[8,48,384]{2,1,0:T(8,128)(2,1)S(1)}, bf16[8,48,384]{2,1,0:T(8,128)(2,1)S(1)}, u32[]{:S(2)}, u32[]{:S(2)}) collective-permute-start(bf16[8,48,384]{2,1,0:T(8,128)(2,1)S(1)} %all-to-all-done.1.refs_2_), channel_id=1, source_target_pairs={{0,128},{128,0},{1,129},{129,1},{2,130},{130,2},{3,131},{131,3},{4... | collective-permute-start | bytes 884744 | tf_op jit(solution)/shard_map/ppermute | solution.py:396
  37.1 8.0 %finest.1 = (bf16[128,384]{1,0:T(8,128)(2,1)}, bf16[32,768]{1,0:T(8,128)(2,1)}, bf16[64,3072]{1,0:T(8,128)(2,1)}, bf16[48,384]{1,0:T(8,128)(2,1)}) custom-call(s32[7]{0:T(128)} %stack.23.refs_0_, bf16[8,16,384]{2,1,0:T(8,128)(2,1)} %refs_1_.1, bf16[8,8,384]{2,1,0:T(8,128)(2,1)} %copy-done.12, bf16[8,8,384]{2,1,0:T(8,128)(2,1)} %copy-done.11, ...), custom_call_target="tpu_custom_call" | custom-call | flops 6000000000 | bytes 18000000 | tf_op jit(solution)/shard_map/finest/pallas_call | solution.py:84
  45.1 5.9 %all-to-all-start = ((bf16[8,8,3072]{2,1,0:T(8,128)(2,1)}), bf16[8,8,3072]{2,1,0:T(8,128)(2,1)S(1)}, u32[]{:S(2)}, u32[]{:S(2)}) async-start(bf16[8,8,3072]{2,1,0:T(8,128)(2,1)} %bitcast.32), calls=%async_computation | async-start | bytes 786432 | tf_op jit(solution)/shard_map/all_to_all | solution.py:35
  51.5 6.3 %all-to-all-done = bf16[8,8,3072]{2,1,0:T(8,128)(2,1)S(1)} async-done(((bf16[8,8,3072]{2,1,0:T(8,128)(2,1)}), bf16[8,8,3072]{2,1,0:T(8,128)(2,1)S(1)}, u32[]{:S(2)}, u32[]{:S(2)}) %all-to-all-start) | async-done | bytes 393248 | tf_op jit(solution)/shard_map/all_to_all | solution.py:35
  61.3 4.0 %all-to-all-start.2 = ((bf16[8,64,192]{2,1,0:T(8,128)(2,1)}), bf16[8,64,192]{2,1,0:T(8,128)(2,1)S(1)}, u32[]{:S(2)}, u32[]{:S(2)}) async-start(bf16[8,64,192]{2,1,0:T(8,128)(2,1)} %bitcast.9), calls=%async_computation.2 | async-start | bytes 524288 | tf_op jit(solution)/shard_map/all_to_all | solution.py:35
  65.2 2.2 %collective-permute-start.8 = (bf16[48,384]{1,0:T(8,128)(2,1)S(1)}, bf16[48,384]{1,0:T(8,128)(2,1)S(1)}, u32[]{:S(2)}, u32[]{:S(2)}) collective-permute-start(bf16[48,384]{1,0:T(8,128)(2,1)S(1)} %copy-done.13), channel_id=1, source_target_pairs={{0,128},{128,0},{1,129},{129,1},{2,130},{130,2},{3,131},{131,3},{4... | collective-permute-start | bytes 110600 | tf_op jit(solution)/shard_map/ppermute | solution.py:436
  67.6 3.1 %collective-permute-done.8.refs_6_ = bf16[48,384]{1,0:T(8,128)(2,1)S(1)} collective-permute-done((bf16[48,384]{1,0:T(8,128)(2,1)S(1)}, bf16[48,384]{1,0:T(8,128)(2,1)S(1)}, u32[]{:S(2)}, u32[]{:S(2)}) %collective-permute-start.8) | collective-permute-done | bytes 36896 | tf_op jit(solution)/shard_map/ppermute | solution.py:436
  73.3 4.3 %all-to-all-start.3 = ((bf16[8,64,384]{2,1,0:T(8,128)(2,1)}), bf16[8,64,384]{2,1,0:T(8,128)(2,1)S(1)}, u32[]{:S(2)}, u32[]{:S(2)}) async-start(bf16[8,64,384]{2,1,0:T(8,128)(2,1)} %bitcast.14), calls=%async_computation.3 | async-start | bytes 786432 | tf_op jit(solution)/shard_map/all_to_all | solution.py:35
  77.6 3.2 %collective-permute-start.16 = (bf16[96,384]{1,0:T(8,128)(2,1)S(1)}, bf16[96,384]{1,0:T(8,128)(2,1)S(1)}, u32[]{:S(2)}, u32[]{:S(2)}) collective-permute-start(bf16[96,384]{1,0:T(8,128)(2,1)S(1)} %get-tuple-element.26.refs_3_), channel_id=1, source_target_pairs={{0,112},{16,0},{32,16},{48,32},{64,48},{80,64},{96,80},{112,96},{1... | collective-permute-start | bytes 221192 | tf_op jit(solution)/shard_map/ppermute | solution.py:463
  80.8 2.4 %collective-permute-start.15 = (bf16[96,384]{1,0:T(8,128)(2,1)S(1)}, bf16[96,384]{1,0:T(8,128)(2,1)S(1)}, u32[]{:S(2)}, u32[]{:S(2)}) collective-permute-start(bf16[96,384]{1,0:T(8,128)(2,1)S(1)} %get-tuple-element.26.refs_3_), channel_id=1, source_target_pairs={{0,96},{16,112},{32,0},{48,16},{64,32},{80,48},{96,64},{112,80},{1... | collective-permute-start | bytes 221192 | tf_op jit(solution)/shard_map/ppermute | solution.py:463
  83.1 2.2 %collective-permute-start.9 = (bf16[64,192]{1,0:T(8,128)(2,1)S(1)}, bf16[64,192]{1,0:T(8,128)(2,1)S(1)}, u32[]{:S(2)}, u32[]{:S(2)}) collective-permute-start(bf16[64,192]{1,0:T(8,128)(2,1)S(1)} %get-tuple-element.24.refs_0_), channel_id=1, source_target_pairs={{0,128},{128,0},{1,129},{129,1},{2,130},{130,2},{3,131},{131,3},{4... | collective-permute-start | bytes 73736 | tf_op jit(solution)/shard_map/ppermute | solution.py:466
  86.8 3.6 %collective-permute-start.13 = (bf16[96,384]{1,0:T(8,128)(2,1)S(1)}, bf16[96,384]{1,0:T(8,128)(2,1)S(1)}, u32[]{:S(2)}, u32[]{:S(2)}) collective-permute-start(bf16[96,384]{1,0:T(8,128)(2,1)S(1)} %get-tuple-element.26.refs_3_), channel_id=1, source_target_pairs={{0,64},{16,80},{32,96},{48,112},{64,0},{80,16},{96,32},{112,48},{1... | collective-permute-start | bytes 221192 | tf_op jit(solution)/shard_map/ppermute | solution.py:463
  90.7 3.0 %collective-permute-done.16.refs_10_ = bf16[96,384]{1,0:T(8,128)(2,1)S(1)} collective-permute-done((bf16[96,384]{1,0:T(8,128)(2,1)S(1)}, bf16[96,384]{1,0:T(8,128)(2,1)S(1)}, u32[]{:S(2)}, u32[]{:S(2)}) %collective-permute-start.16) | collective-permute-done | bytes 73760 | tf_op jit(solution)/shard_map/ppermute | solution.py:463
  95.2 2.3 %collective-permute-start.10 = (bf16[96,384]{1,0:T(8,128)(2,1)S(1)}, bf16[96,384]{1,0:T(8,128)(2,1)S(1)}, u32[]{:S(2)}, u32[]{:S(2)}) collective-permute-start(bf16[96,384]{1,0:T(8,128)(2,1)S(1)} %get-tuple-element.26.refs_3_), channel_id=1, source_target_pairs={{0,16},{16,32},{32,48},{48,64},{64,80},{80,96},{96,112},{112,0},{1... | collective-permute-start | bytes 221192 | tf_op jit(solution)/shard_map/ppermute | solution.py:463
  97.5 2.4 %all_gather.3.refs_2_ = bf16[1024,384]{1,0:T(8,128)(2,1)S(1)} all-gather(bf16[512,384]{1,0:T(8,128)(2,1)S(1)} %bitcast.31), channel_id=1, replica_groups=mesh['yh'=2,'z'=8,'k'=2,'x'=4,'yl'=2] {'k'}, dimensions={0}, use_global_device_ids=true | all-gather | bytes 1179648 | tf_op jit(solution)/shard_map/all_gather | solution.py:468
  100.6 2.0 %collective-permute-done.11.refs_5_ = bf16[96,384]{1,0:T(8,128)(2,1)S(1)} collective-permute-done((bf16[96,384]{1,0:T(8,128)(2,1)S(1)}, bf16[96,384]{1,0:T(8,128)(2,1)S(1)}, u32[]{:S(2)}, u32[]{:S(2)}) %collective-permute-start.11) | collective-permute-done | bytes 73760 | tf_op jit(solution)/shard_map/ppermute | solution.py:463
  106.3 4.3 %collective-permute-done.17.refs_1_ = f32[64,256]{1,0:T(8,128)S(1)} collective-permute-done((f32[64,256]{1,0:T(8,128)S(1)}, f32[64,256]{1,0:T(8,128)S(1)}, u32[]{:S(2)}, u32[]{:S(2)}) %collective-permute-start.17) | collective-permute-done | bytes 65568 | tf_op jit(solution)/shard_map/ppermute | solution.py:476
  111.2 11.5 %all_to_all.61 = bf16[8,64,192]{2,1,0:T(8,128)(2,1)S(1)} all-to-all(bf16[8,64,192]{2,1,0:T(8,128)(2,1)S(1)} %bitcast.27), channel_id=1, replica_groups=mesh['yh'=2,'z'=8,'k'=2,'x'=4,'yl'=2] {'x','yl'}, dimensions={0} | all-to-all | bytes 393216 | tf_op jit(solution)/shard_map/all_to_all | solution.py:35
  123.9 10.5 %all_to_all.62 = bf16[8,8,3072]{2,1,0:T(8,128)(2,1)S(1)} all-to-all(bf16[8,8,3072]{2,1,0:T(8,128)(2,1)S(1)} %bitcast.23), channel_id=1, replica_groups=mesh['yh'=2,'z'=8,'k'=2,'x'=4,'yl'=2] {'x','yl'}, dimensions={0} | all-to-all | bytes 786432 | tf_op jit(solution)/shard_map/all_to_all | solution.py:35
  (82 shorter events, 25.2 us)
Async XLA Ops:
  0.0 35.8 %collective-permute-start.4 = (bf16[48,384]{1,0:T(8,128)(2,1)}, bf16[48,384]{1,0:T(8,128)(2,1)S(1)}, u32[]{:S(2)}, u32[]{:S(2)}) collective-permute-start(bf16[48,384]{1,0:T(8,128)(2,1)} %param.30), channel_id=1, source_target_pairs={{0,0},{1,16},{2,32},{3,48},{4,64},{5,80},{6,96},{7,112},{8,8},{9,2... | collective-permute-start | bytes 110600 | tf_op jit(solution)/shard_map/ppermute | solution.py:392
  4.7 17.4 %collective-permute-start.1 = (bf16[8,8,384]{2,1,0:T(8,128)(2,1)S(1)}, bf16[8,8,384]{2,1,0:T(8,128)(2,1)S(1)}, u32[]{:S(2)}, u32[]{:S(2)}) collective-permute-start(bf16[8,8,384]{2,1,0:T(8,128)(2,1)S(1)} %get-tuple-element.33), channel_id=1, source_target_pairs={{1,0},{2,1},{3,2},{4,3},{5,4},{6,5},{7,6},{9,8},{10,9},{11,10},{12... | collective-permute-start | bytes 147464 | tf_op jit(solution)/shard_map/ppermute | solution.py:359
  6.8 15.3 %collective-permute-start = (bf16[8,8,384]{2,1,0:T(8,128)(2,1)S(1)}, bf16[8,8,384]{2,1,0:T(8,128)(2,1)S(1)}, u32[]{:S(2)}, u32[]{:S(2)}) collective-permute-start(bf16[8,8,384]{2,1,0:T(8,128)(2,1)S(1)} %get-tuple-element.34), channel_id=1, source_target_pairs={{0,1},{1,2},{2,3},{3,4},{4,5},{5,6},{6,7},{8,9},{9,10},{10,11},{11... | collective-permute-start | bytes 147464 | tf_op jit(solution)/shard_map/ppermute | solution.py:358
  13.2 19.9 %all-to-all-start.1 = ((bf16[8,48,384]{2,1,0:T(8,128)(2,1)}), bf16[8,48,384]{2,1,0:T(8,128)(2,1)S(1)}, u32[]{:S(2)}, u32[]{:S(2)}) async-start(bf16[8,48,384]{2,1,0:T(8,128)(2,1)} %copies.1), calls=%async_computation.1 | async-start | bytes 589824 | tf_op jit(solution)/shard_map/all_to_all | solution.py:35
  22.1 13.7 %collective-permute-start.2 = (bf16[3,32,384]{2,1,0:T(8,128)(2,1)S(1)}, bf16[3,32,384]{2,1,0:T(8,128)(2,1)S(1)}, u32[]{:S(2)}, u32[]{:S(2)}) collective-permute-start(bf16[3,32,384]{2,1,0:T(8,128)(2,1)S(1)} %get-tuple-element.19), channel_id=1, source_target_pairs={{0,8},{8,16},{16,24},{24,32},{32,40},{40,48},{48,56},{56,64},{64,7... | collective-permute-start | bytes 221192 | tf_op jit(solution)/shard_map/ppermute | solution.py:363
  23.4 12.4 %collective-permute-start.3 = (bf16[3,32,384]{2,1,0:T(8,128)(2,1)S(1)}, bf16[3,32,384]{2,1,0:T(8,128)(2,1)S(1)}, u32[]{:S(2)}, u32[]{:S(2)}) collective-permute-start(bf16[3,32,384]{2,1,0:T(8,128)(2,1)S(1)} %get-tuple-element.20), channel_id=1, source_target_pairs={{8,0},{16,8},{24,16},{32,24},{40,32},{48,40},{56,48},{64,56},{72,6... | collective-permute-start | bytes 221192 | tf_op jit(solution)/shard_map/ppermute | solution.py:364
  26.0 32.6 %copy-start.2 = (s32[7]{0:T(128)S(1)}, s32[7]{0:T(128)}, u32[]{:S(2)}) copy-start(s32[7]{0:T(128)} %stack.23.refs_0_) | copy-start | bytes 88
  33.1 17.9 %collective-permute-start.6 = (bf16[8,48,384]{2,1,0:T(8,128)(2,1)S(1)}, bf16[8,48,384]{2,1,0:T(8,128)(2,1)S(1)}, u32[]{:S(2)}, u32[]{:S(2)}) collective-permute-start(bf16[8,48,384]{2,1,0:T(8,128)(2,1)S(1)} %all-to-all-done.1.refs_2_), channel_id=1, source_target_pairs={{0,128},{128,0},{1,129},{129,1},{2,130},{130,2},{3,131},{131,3},{4... | collective-permute-start | bytes 884744 | tf_op jit(solution)/shard_map/ppermute | solution.py:396
  45.1 12.7 %all-to-all-start = ((bf16[8,8,3072]{2,1,0:T(8,128)(2,1)}), bf16[8,8,3072]{2,1,0:T(8,128)(2,1)S(1)}, u32[]{:S(2)}, u32[]{:S(2)}) async-start(bf16[8,8,3072]{2,1,0:T(8,128)(2,1)} %bitcast.32), calls=%async_computation | async-start | bytes 786432 | tf_op jit(solution)/shard_map/all_to_all | solution.py:35
  51.0 6.8 %collective-permute-start.5 = (bf16[8,48,384]{2,1,0:T(8,128)(2,1)S(1)}, bf16[8,48,384]{2,1,0:T(8,128)(2,1)S(1)}, u32[]{:S(2)}, u32[]{:S(2)}) collective-permute-start(bf16[8,48,384]{2,1,0:T(8,128)(2,1)S(1)} %all-to-all-done.1.refs_2_), channel_id=1, source_target_pairs={{0,8},{8,0},{1,9},{9,1},{2,10},{10,2},{3,11},{11,3},{4,12},{12,4},... | collective-permute-start | bytes 884744 | tf_op jit(solution)/shard_map/ppermute | solution.py:437
  51.0 6.8 %collective-permute-start.7 = (bf16[8,48,384]{2,1,0:T(8,128)(2,1)S(1)}, bf16[8,48,384]{2,1,0:T(8,128)(2,1)S(1)}, u32[]{:S(2)}, u32[]{:S(2)}) collective-permute-start(bf16[8,48,384]{2,1,0:T(8,128)(2,1)S(1)} %collective-permute-done.6.refs_4_), channel_id=1, source_target_pairs={{0,8},{8,0},{1,9},{9,1},{2,10},{10,2},{3,11},{11,3},{4,12},{12,4},... | collective-permute-start | bytes 884744 | tf_op jit(solution)/shard_map/ppermute | solution.py:437
  61.3 10.1 %all-to-all-start.2 = ((bf16[8,64,192]{2,1,0:T(8,128)(2,1)}), bf16[8,64,192]{2,1,0:T(8,128)(2,1)S(1)}, u32[]{:S(2)}, u32[]{:S(2)}) async-start(bf16[8,64,192]{2,1,0:T(8,128)(2,1)} %bitcast.9), calls=%async_computation.2 | async-start | bytes 524288 | tf_op jit(solution)/shard_map/all_to_all | solution.py:35
  65.2 5.5 %collective-permute-start.8 = (bf16[48,384]{1,0:T(8,128)(2,1)S(1)}, bf16[48,384]{1,0:T(8,128)(2,1)S(1)}, u32[]{:S(2)}, u32[]{:S(2)}) collective-permute-start(bf16[48,384]{1,0:T(8,128)(2,1)S(1)} %copy-done.13), channel_id=1, source_target_pairs={{0,128},{128,0},{1,129},{129,1},{2,130},{130,2},{3,131},{131,3},{4... | collective-permute-start | bytes 110600 | tf_op jit(solution)/shard_map/ppermute | solution.py:436
  73.3 24.2 %all-to-all-start.3 = ((bf16[8,64,384]{2,1,0:T(8,128)(2,1)}), bf16[8,64,384]{2,1,0:T(8,128)(2,1)S(1)}, u32[]{:S(2)}, u32[]{:S(2)}) async-start(bf16[8,64,384]{2,1,0:T(8,128)(2,1)} %bitcast.14), calls=%async_computation.3 | async-start | bytes 786432 | tf_op jit(solution)/shard_map/all_to_all | solution.py:35
  77.6 16.1 %collective-permute-start.16 = (bf16[96,384]{1,0:T(8,128)(2,1)S(1)}, bf16[96,384]{1,0:T(8,128)(2,1)S(1)}, u32[]{:S(2)}, u32[]{:S(2)}) collective-permute-start(bf16[96,384]{1,0:T(8,128)(2,1)S(1)} %get-tuple-element.26.refs_3_), channel_id=1, source_target_pairs={{0,112},{16,0},{32,16},{48,32},{64,48},{80,64},{96,80},{112,96},{1... | collective-permute-start | bytes 221192 | tf_op jit(solution)/shard_map/ppermute | solution.py:463
  80.8 14.4 %collective-permute-start.15 = (bf16[96,384]{1,0:T(8,128)(2,1)S(1)}, bf16[96,384]{1,0:T(8,128)(2,1)S(1)}, u32[]{:S(2)}, u32[]{:S(2)}) collective-permute-start(bf16[96,384]{1,0:T(8,128)(2,1)S(1)} %get-tuple-element.26.refs_3_), channel_id=1, source_target_pairs={{0,96},{16,112},{32,0},{48,16},{64,32},{80,48},{96,64},{112,80},{1... | collective-permute-start | bytes 221192 | tf_op jit(solution)/shard_map/ppermute | solution.py:463
  83.1 7.3 %collective-permute-start.9 = (bf16[64,192]{1,0:T(8,128)(2,1)S(1)}, bf16[64,192]{1,0:T(8,128)(2,1)S(1)}, u32[]{:S(2)}, u32[]{:S(2)}) collective-permute-start(bf16[64,192]{1,0:T(8,128)(2,1)S(1)} %get-tuple-element.24.refs_0_), channel_id=1, source_target_pairs={{0,128},{128,0},{1,129},{129,1},{2,130},{130,2},{3,131},{131,3},{4... | collective-permute-start | bytes 73736 | tf_op jit(solution)/shard_map/ppermute | solution.py:466
  85.4 14.5 %collective-permute-start.14 = (bf16[96,384]{1,0:T(8,128)(2,1)S(1)}, bf16[96,384]{1,0:T(8,128)(2,1)S(1)}, u32[]{:S(2)}, u32[]{:S(2)}) collective-permute-start(bf16[96,384]{1,0:T(8,128)(2,1)S(1)} %get-tuple-element.26.refs_3_), channel_id=1, source_target_pairs={{0,80},{16,96},{32,112},{48,0},{64,16},{80,32},{96,48},{112,64},{1... | collective-permute-start | bytes 221192 | tf_op jit(solution)/shard_map/ppermute | solution.py:463
  86.8 13.0 %collective-permute-start.13 = (bf16[96,384]{1,0:T(8,128)(2,1)S(1)}, bf16[96,384]{1,0:T(8,128)(2,1)S(1)}, u32[]{:S(2)}, u32[]{:S(2)}) collective-permute-start(bf16[96,384]{1,0:T(8,128)(2,1)S(1)} %get-tuple-element.26.refs_3_), channel_id=1, source_target_pairs={{0,64},{16,80},{32,96},{48,112},{64,0},{80,16},{96,32},{112,48},{1... | collective-permute-start | bytes 221192 | tf_op jit(solution)/shard_map/ppermute | solution.py:463
  90.4 10.2 %collective-permute-start.12 = (bf16[96,384]{1,0:T(8,128)(2,1)S(1)}, bf16[96,384]{1,0:T(8,128)(2,1)S(1)}, u32[]{:S(2)}, u32[]{:S(2)}) collective-permute-start(bf16[96,384]{1,0:T(8,128)(2,1)S(1)} %get-tuple-element.26.refs_3_), channel_id=1, source_target_pairs={{0,48},{16,64},{32,80},{48,96},{64,112},{80,0},{96,16},{112,32},{1... | collective-permute-start | bytes 221192 | tf_op jit(solution)/shard_map/ppermute | solution.py:463
  93.7 8.9 %collective-permute-start.11 = (bf16[96,384]{1,0:T(8,128)(2,1)S(1)}, bf16[96,384]{1,0:T(8,128)(2,1)S(1)}, u32[]{:S(2)}, u32[]{:S(2)}) collective-permute-start(bf16[96,384]{1,0:T(8,128)(2,1)S(1)} %get-tuple-element.26.refs_3_), channel_id=1, source_target_pairs={{0,32},{16,48},{32,64},{48,80},{64,96},{80,112},{96,0},{112,16},{1... | collective-permute-start | bytes 221192 | tf_op jit(solution)/shard_map/ppermute | solution.py:463
  95.2 7.9 %collective-permute-start.10 = (bf16[96,384]{1,0:T(8,128)(2,1)S(1)}, bf16[96,384]{1,0:T(8,128)(2,1)S(1)}, u32[]{:S(2)}, u32[]{:S(2)}) collective-permute-start(bf16[96,384]{1,0:T(8,128)(2,1)S(1)} %get-tuple-element.26.refs_3_), channel_id=1, source_target_pairs={{0,16},{16,32},{32,48},{48,64},{64,80},{80,96},{96,112},{112,0},{1... | collective-permute-start | bytes 221192 | tf_op jit(solution)/shard_map/ppermute | solution.py:463
  104.4 18.3 %collective-permute-start.18 = (bf16[8,96,384]{2,1,0:T(8,128)(2,1)S(1)}, bf16[8,96,384]{2,1,0:T(8,128)(2,1)S(1)}, u32[]{:S(2)}, u32[]{:S(2)}) collective-permute-start(bf16[8,96,384]{2,1,0:T(8,128)(2,1)S(1)} %get-tuple-element.30.refs_3_), channel_id=1, source_target_pairs={{0,8},{8,0},{1,9},{9,1},{2,10},{10,2},{3,11},{11,3},{4,12},{12,4},... | collective-permute-start | bytes 1769480 | tf_op jit(solution)/shard_map/ppermute | solution.py:477
  104.5 6.0 %collective-permute-start.17 = (f32[64,256]{1,0:T(8,128)S(1)}, f32[64,256]{1,0:T(8,128)S(1)}, u32[]{:S(2)}, u32[]{:S(2)}) collective-permute-start(f32[64,256]{1,0:T(8,128)S(1)} %get-tuple-element.28), channel_id=1, source_target_pairs={{0,128},{128,0},{1,129},{129,1},{2,130},{130,2},{3,131},{131,3},{4... | collective-permute-start | bytes 196616 | tf_op jit(solution)/shard_map/ppermute | solution.py:476
  (19 other events, 166.1 us)

commit v4 on v3

--- a/solution.py
+++ b/solution.py
@@ -135,6 +135,7 @@
     wo_far,
     merge_far,
     split,
+    split_yh,
     resid_out,
     level1_out,
     band_out,
@@ -155,7 +156,7 @@
     ]
     for fetch in fetches:
         fetch.start()
-    split_out[...] = split[...]
+    split_out[...] = jnp.concatenate([split[...], split_yh[...]], axis=0)
     wide = widen(tokens[...], left[...], right[...])
     floats = jnp.concatenate(
         [top[...].astype(F32), wide, bottom[...].astype(F32)], axis=0
@@ -214,7 +215,8 @@
     send_level1.wait()
 
 
-def middle_kernel(where, band, own, over_k, over_yh, over_both, mid_out, copies_out):
+def middle_kernel(where, band, own, over_k, over_yh, over_both, *refs):
+    mid_out, copies_out = refs[3:]
     here = where[5] * 2 + where[4]
     blocks = []
     for yh in range(2):
@@ -229,8 +231,8 @@
     copies_out[...] = jnp.concatenate([mid] * 8, axis=0)
 
 
-def project_kernel(mids, gain, wq, wk, wv, split, over_yh, q_out, kv_out, split_out):
-    split_out[...] = jnp.concatenate([split[...], over_yh[...]], axis=0)
+def project_kernel(mids, gain, wq, wk, wv, *refs):
+    q_out, kv_out = refs[4:]
     parts = [mids[64 * i : 64 * i + 64, :].astype(F32) for i in range(8)]
     total = jnp.zeros((64, 1), F32)
     for part in parts:
@@ -400,7 +402,7 @@
             shaped((128, 384), BF),
             shaped((32, 768), BF),
             shaped((64, 3072), BF),
-            shaped((48, 384), BF),
+            shaped((96, 384), BF),
         ),
         (
             where,
@@ -416,6 +418,7 @@
             out0,
             merge_one,
             split_block,
+            lax.ppermute(split_block, "yh", swap("yh")),
         ),
         6,
         smem=(0,),
@@ -433,36 +436,30 @@
         name="finest",
     )
     band = exchange(band, COL)
-    over_yh = lax.ppermute(split_block, "yh", swap("yh"))
+    split_blocks = [split_block] + [
+        lax.ppermute(split_block, "z", [(i, (i + step) % 8) for i in range(8)])
+        for step in range(1, 8)
+    ]
     merge_k, merge_both = [lax.ppermute(w, "k", swap("k")) for w in (merge_own, merge_yh)]
     mid, mids = call(
         middle_kernel,
         (shaped((64, 192), BF), shaped((512, 192), BF)),
-        (where, band, merge_own, merge_k, merge_yh, merge_both),
+        (where, band, merge_own, merge_k, merge_yh, merge_both)
+        + tuple(split_blocks[i] for i in (1, 2, 7)),
         2,
         smem=(0,),
+        far=(6, 7, 8),
         name="middle",
     )
     mids = exchange(mids, COL)
-    q, kv, split_block = call(
+    q, kv = call(
         project_kernel,
-        (shaped((64, 192), BF), shaped((512, 384), BF), shaped((96, 384), BF)),
-        (
-            mids,
-            gain_two.reshape(8, 192),
-            query2.T,
-            key2.T,
-            value2.T,
-            split_block,
-            over_yh,
-        ),
+        (shaped((64, 192), BF), shaped((512, 384), BF)),
+        (mids, gain_two.reshape(8, 192), query2.T, key2.T, value2.T, *split_blocks[3:7]),
         2,
+        far=(5, 6, 7, 8),
         name="project",
     )
-    split_blocks = [split_block] + [
-        lax.ppermute(split_block, "z", [(i, (i + step) % 8) for i in range(8)])
-        for step in range(1, 8)
-    ]
     q_other = lax.ppermute(q, "yh", swap("yh"))
     kv = exchange(kv, "z")
     kv = lax.all_gather(kv, "k", axis=0, tiled=True)

time: 137 us -> 149 us (1.088)
  waiting for transfers between devices: 28.8 us -> 36.7 us
  local copies, waits for them, and re-layouts: 5.87 us -> 11.1 us
    ppermute x7, waiting for transfers between devices: 7.2 us -> 14.5 us  [on_device(): lax.ppermute(split_block, 'z', [(i, (i + step) % 8) for i in range(8)])]
    all_to_all x4, starting transfers between devices: 21.9 us -> 26.9 us  [exchange(): return lax.all_to_all(block, axis, split_axis=0, concat_axis=0, tiled=True)]
    unnamed x40 -> x58, local copies, waits for them, and re-layouts: 3.75 us -> 8.31 us
    ppermute x7, starting transfers between devices: 13.8 us -> 10.3 us  [on_device(): lax.ppermute(split_block, 'z', [(i, (i + step) % 8) for i in range(8)])]
    all_to_all x4, waiting for transfers between devices: 14.1 us -> 17.5 us  [exchange(): return lax.all_to_all(block, axis, split_axis=0, concat_axis=0, tiled=True)]
    ppermute x1, waiting for transfers between devices: 3.15 us -> 0.01 us  [on_device(): lax.ppermute(split_block, 'yh', swap('yh'))]
  transfers between devices with their start and end apart: 23 -> 23, of which waited for: 10 -> 7; matrix products, arithmetic and copies ran while one was open for 2% -> 2% of each run, Pallas kernels for 7% -> 6%
where the time goes in v4:
time: 149 us; the launch traced here: 148 us
  starting transfers between devices  57.5 us (39%)
  waiting for transfers between devices  36.7 us (25%)
  blocking collectives  24.5 us (16%)
  Pallas kernels  16.9 us (11%)
  local copies, waits for them, and re-layouts  11.1 us (7%)
    all_to_all x4, starting transfers between devices, exchange(): return lax.all_to_all(block, axis, split_axis=0, concat_axis=0, tiled=True)  26.9 us
    all_to_all x2, blocking collectives, exchange(): return lax.all_to_all(block, axis, split_axis=0, concat_axis=0, tiled=True)  22.1 us
    all_to_all x4, waiting for transfers between devices, exchange(): return lax.all_to_all(block, axis, split_axis=0, concat_axis=0, tiled=True)  17.5 us
    pallas_call x9, Pallas kernels, call(): pl.pallas_call(kernel, out_shape=out_shape, in_specs=specs, out_specs=out...  16.9 us
    ppermute x7, waiting for transfers between devices, on_device(): lax.ppermute(split_block, 'z', [(i, (i + step) % 8) for i in range(8)])  14.5 us
    ppermute x7, starting transfers between devices, on_device(): lax.ppermute(split_block, 'z', [(i, (i + step) % 8) for i in range(8)])  10.3 us
    unnamed x58, local copies, waits for them, and re-layouts  8.31 us
    ppermute x1, waiting for transfers between devices, on_device(): theirs = lax.ppermute(other, 'yh', swap('yh'))  4.65 us
  transfers between devices with their start and end apart: 23, of which 7 were waited for; matrix products, arithmetic and copies ran while one was open for 2% of the time, Pallas kernels for 6%

profile of v4, /device:TPU:8, one launch (start us, length us, event | category | flops | bytes accessed | tf_op | source)
XLA Modules:
  0.0 148.1 jit_solution(12807502062058850867)
XLA Ops:
  0.9 3.4 %collective-permute-start = (bf16[8,8,384]{2,1,0:T(8,128)(2,1)S(1)}, bf16[8,8,384]{2,1,0:T(8,128)(2,1)S(1)}, u32[]{:S(2)}, u32[]{:S(2)}) collective-permute-start(bf16[8,8,384]{2,1,0:T(8,128)(2,1)S(1)} %get-tuple-element.32), channel_id=1, source_target_pairs={{0,1},{1,2},{2,3},{3,4},{4,5},{5,6},{6,7},{8,9},{9,10},{10,11},{11... | collective-permute-start | bytes 147464 | tf_op jit(solution)/shard_map/ppermute | solution.py:360
  4.3 2.6 %collective-permute-start.1 = (bf16[8,8,384]{2,1,0:T(8,128)(2,1)S(1)}, bf16[8,8,384]{2,1,0:T(8,128)(2,1)S(1)}, u32[]{:S(2)}, u32[]{:S(2)}) collective-permute-start(bf16[8,8,384]{2,1,0:T(8,128)(2,1)S(1)} %get-tuple-element.31), channel_id=1, source_target_pairs={{1,0},{2,1},{3,2},{4,3},{5,4},{6,5},{7,6},{9,8},{10,9},{11,10},{12... | collective-permute-start | bytes 147464 | tf_op jit(solution)/shard_map/ppermute | solution.py:361
  6.9 2.6 %collective-permute-start.4 = (bf16[48,384]{1,0:T(8,128)(2,1)}, bf16[48,384]{1,0:T(8,128)(2,1)S(1)}, u32[]{:S(2)}, u32[]{:S(2)}) collective-permute-start(bf16[48,384]{1,0:T(8,128)(2,1)} %param.30), channel_id=1, source_target_pairs={{0,0},{1,16},{2,32},{3,48},{4,64},{5,80},{6,96},{7,112},{8,8},{9,2... | collective-permute-start | bytes 110600 | tf_op jit(solution)/shard_map/ppermute | solution.py:394
  11.2 9.8 %all-to-all-start.1 = ((bf16[8,48,384]{2,1,0:T(8,128)(2,1)}), bf16[8,48,384]{2,1,0:T(8,128)(2,1)S(1)}, u32[]{:S(2)}, u32[]{:S(2)}) async-start(bf16[8,48,384]{2,1,0:T(8,128)(2,1)} %copies.1), calls=%async_computation.1 | async-start | bytes 589824 | tf_op jit(solution)/shard_map/all_to_all | solution.py:35
  22.0 2.8 %collective-permute-start.5 = (bf16[48,384]{1,0:T(8,128)(2,1)S(1)}, bf16[48,384]{1,0:T(8,128)(2,1)S(1)}, u32[]{:S(2)}, u32[]{:S(2)}) collective-permute-start(bf16[48,384]{1,0:T(8,128)(2,1)S(1)} %collective-permute-done.4.refs_12_), channel_id=1, source_target_pairs={{0,128},{128,0},{1,129},{129,1},{2,130},{130,2},{3,131},{131,3},{4... | collective-permute-start | bytes 110600 | tf_op jit(solution)/shard_map/ppermute | solution.py:421
  28.7 4.0 %all-to-all-done.1.refs_2_ = bf16[8,48,384]{2,1,0:T(8,128)(2,1)S(1)} async-done(((bf16[8,48,384]{2,1,0:T(8,128)(2,1)}), bf16[8,48,384]{2,1,0:T(8,128)(2,1)S(1)}, u32[]{:S(2)}, u32[]{:S(2)}) %all-to-all-start.1) | async-done | bytes 294944 | tf_op jit(solution)/shard_map/all_to_all | solution.py:35
  32.7 3.4 %collective-permute-start.7 = (bf16[8,48,384]{2,1,0:T(8,128)(2,1)S(1)}, bf16[8,48,384]{2,1,0:T(8,128)(2,1)S(1)}, u32[]{:S(2)}, u32[]{:S(2)}) collective-permute-start(bf16[8,48,384]{2,1,0:T(8,128)(2,1)S(1)} %all-to-all-done.1.refs_2_), channel_id=1, source_target_pairs={{0,128},{128,0},{1,129},{129,1},{2,130},{130,2},{3,131},{131,3},{4... | collective-permute-start | bytes 884744 | tf_op jit(solution)/shard_map/ppermute | solution.py:398
  37.4 8.0 %finest.1 = (bf16[128,384]{1,0:T(8,128)(2,1)}, bf16[32,768]{1,0:T(8,128)(2,1)}, bf16[64,3072]{1,0:T(8,128)(2,1)}, bf16[96,384]{1,0:T(8,128)(2,1)}) custom-call(s32[7]{0:T(128)} %stack.23.refs_0_, bf16[8,16,384]{2,1,0:T(8,128)(2,1)} %refs_1_.1, bf16[8,8,384]{2,1,0:T(8,128)(2,1)} %copy-done.21, bf16[8,8,384]{2,1,0:T(8,128)(2,1)} %copy-done.22, ...), custom_call_target="tpu_custom_call" | custom-call | flops 6000000000 | bytes 18000000 | tf_op jit(solution)/shard_map/finest/pallas_call | solution.py:84
  45.4 7.4 %all-to-all-start = ((bf16[8,8,3072]{2,1,0:T(8,128)(2,1)}), bf16[8,8,3072]{2,1,0:T(8,128)(2,1)S(1)}, u32[]{:S(2)}, u32[]{:S(2)}) async-start(bf16[8,8,3072]{2,1,0:T(8,128)(2,1)} %bitcast.32), calls=%async_computation | async-start | bytes 786432 | tf_op jit(solution)/shard_map/all_to_all | solution.py:35
  53.3 2.1 %collective-permute-start.11 = (bf16[96,384]{1,0:T(8,128)(2,1)}, bf16[96,384]{1,0:T(8,128)(2,1)S(1)}, u32[]{:S(2)}, u32[]{:S(2)}) collective-permute-start(bf16[96,384]{1,0:T(8,128)(2,1)} %get-tuple-element.21.refs_3_), channel_id=1, source_target_pairs={{0,112},{16,0},{32,16},{48,32},{64,48},{80,64},{96,80},{112,96},{1... | collective-permute-start | bytes 221192 | tf_op jit(solution)/shard_map/ppermute | solution.py:440
  55.4 6.7 %collective-permute-done.10.refs_7_.refs_5_ = bf16[96,384]{1,0:T(8,128)(2,1)S(1)} collective-permute-done((bf16[96,384]{1,0:T(8,128)(2,1)}, bf16[96,384]{1,0:T(8,128)(2,1)S(1)}, u32[]{:S(2)}, u32[]{:S(2)}) %collective-permute-start.10) | collective-permute-done | bytes 73760 | tf_op jit(solution)/shard_map/ppermute | solution.py:440
  70.2 5.7 %all-to-all-start.2 = ((bf16[8,64,192]{2,1,0:T(8,128)(2,1)}), bf16[8,64,192]{2,1,0:T(8,128)(2,1)S(1)}, u32[]{:S(2)}, u32[]{:S(2)}) async-start(bf16[8,64,192]{2,1,0:T(8,128)(2,1)} %bitcast.9), calls=%async_computation.2 | async-start | bytes 524288 | tf_op jit(solution)/shard_map/all_to_all | solution.py:35
  76.9 2.6 %collective-permute-start.13 = (bf16[96,384]{1,0:T(8,128)(2,1)S(1)}, bf16[96,384]{1,0:T(8,128)(2,1)S(1)}, u32[]{:S(2)}, u32[]{:S(2)}) collective-permute-start(bf16[96,384]{1,0:T(8,128)(2,1)S(1)} %copy-done.10), channel_id=1, source_target_pairs={{0,64},{16,80},{32,96},{48,112},{64,0},{80,16},{96,32},{112,48},{1... | collective-permute-start | bytes 221192 | tf_op jit(solution)/shard_map/ppermute | solution.py:440
  79.4 4.6 %collective-permute-start.14 = (bf16[96,384]{1,0:T(8,128)(2,1)S(1)}, bf16[96,384]{1,0:T(8,128)(2,1)S(1)}, u32[]{:S(2)}, u32[]{:S(2)}) collective-permute-start(bf16[96,384]{1,0:T(8,128)(2,1)S(1)} %copy-done.10), channel_id=1, source_target_pairs={{0,80},{16,96},{32,112},{48,0},{64,16},{80,32},{96,48},{112,64},{1... | collective-permute-start | bytes 221192 | tf_op jit(solution)/shard_map/ppermute | solution.py:440
  84.8 2.7 %collective-permute-done.12.refs_5_.refs_6_ = bf16[96,384]{1,0:T(8,128)(2,1)S(1)} collective-permute-done((bf16[96,384]{1,0:T(8,128)(2,1)S(1)}, bf16[96,384]{1,0:T(8,128)(2,1)S(1)}, u32[]{:S(2)}, u32[]{:S(2)}) %collective-permute-start.12) | collective-permute-done | bytes 73760 | tf_op jit(solution)/shard_map/ppermute | solution.py:440
  87.5 2.1 %collective-permute-done.14.refs_7_.refs_8_ = bf16[96,384]{1,0:T(8,128)(2,1)S(1)} collective-permute-done((bf16[96,384]{1,0:T(8,128)(2,1)S(1)}, bf16[96,384]{1,0:T(8,128)(2,1)S(1)}, u32[]{:S(2)}, u32[]{:S(2)}) %collective-permute-start.14) | collective-permute-done | bytes 73760 | tf_op jit(solution)/shard_map/ppermute | solution.py:440
  89.6 3.0 %collective-permute-done.15.refs_8_.refs_9_ = bf16[96,384]{1,0:T(8,128)(2,1)S(1)} collective-permute-done((bf16[96,384]{1,0:T(8,128)(2,1)S(1)}, bf16[96,384]{1,0:T(8,128)(2,1)S(1)}, u32[]{:S(2)}, u32[]{:S(2)}) %collective-permute-start.15) | collective-permute-done | bytes 73760 | tf_op jit(solution)/shard_map/ppermute | solution.py:440
  92.6 1.9 %project.1 = (bf16[64,192]{1,0:T(8,128)(2,1)S(1)}, bf16[512,384]{1,0:T(8,128)(2,1)}) custom-call(bf16[512,192]{1,0:T(8,128)(2,1)S(1)} %bitcast.25, f32[8,192]{1,0:T(8,128)S(1)} %reshape.17.refs_1_, bf16[192,1536]{1,0:T(8,128)(2,1)S(1)} %bitcast.28, bf16[192,1536]{1,0:T(8,128)(2,1)S(1)} %bitcast.29, bf16[192,1536]{1,0:T(8,128)(2,1)S(1)} %bitcast.30, ...), custom_call_target="tpu_custom_call" | custom-call | flops 2000000000 | bytes 6000000 | tf_op jit(solution)/shard_map/project/pallas_call | solution.py:84
  94.5 4.1 %all-to-all-start.3 = ((bf16[8,64,384]{2,1,0:T(8,128)(2,1)}), bf16[8,64,384]{2,1,0:T(8,128)(2,1)S(1)}, u32[]{:S(2)}, u32[]{:S(2)}) async-start(bf16[8,64,384]{2,1,0:T(8,128)(2,1)} %bitcast.14), calls=%async_computation.3 | async-start | bytes 786432 | tf_op jit(solution)/shard_map/all_to_all | solution.py:35
  99.5 13.5 %all-to-all-done.3 = bf16[8,64,384]{2,1,0:T(8,128)(2,1)S(1)} async-done(((bf16[8,64,384]{2,1,0:T(8,128)(2,1)}), bf16[8,64,384]{2,1,0:T(8,128)(2,1)S(1)}, u32[]{:S(2)}, u32[]{:S(2)}) %all-to-all-start.3) | async-done | bytes 393248 | tf_op jit(solution)/shard_map/all_to_all | solution.py:35
  113.1 2.4 %all_gather.3.refs_2_ = bf16[1024,384]{1,0:T(8,128)(2,1)S(1)} all-gather(bf16[512,384]{1,0:T(8,128)(2,1)S(1)} %bitcast.31), channel_id=1, replica_groups=mesh['yh'=2,'z'=8,'k'=2,'x'=4,'yl'=2] {'k'}, dimensions={0}, use_global_device_ids=true | all-gather | bytes 1179648 | tf_op jit(solution)/shard_map/all_gather | solution.py:465
  118.2 4.6 %collective-permute-done.17.refs_1_ = f32[64,256]{1,0:T(8,128)S(1)} collective-permute-done((f32[64,256]{1,0:T(8,128)S(1)}, f32[64,256]{1,0:T(8,128)S(1)}, u32[]{:S(2)}, u32[]{:S(2)}) %collective-permute-start.17) | collective-permute-done | bytes 65568 | tf_op jit(solution)/shard_map/ppermute | solution.py:473
  123.5 11.6 %all_to_all.61 = bf16[8,64,192]{2,1,0:T(8,128)(2,1)S(1)} all-to-all(bf16[8,64,192]{2,1,0:T(8,128)(2,1)S(1)} %bitcast.27), channel_id=1, replica_groups=mesh['yh'=2,'z'=8,'k'=2,'x'=4,'yl'=2] {'x','yl'}, dimensions={0} | all-to-all | bytes 393216 | tf_op jit(solution)/shard_map/all_to_all | solution.py:35
  136.2 10.5 %all_to_all.62 = bf16[8,8,3072]{2,1,0:T(8,128)(2,1)S(1)} all-to-all(bf16[8,8,3072]{2,1,0:T(8,128)(2,1)S(1)} %bitcast.23), channel_id=1, replica_groups=mesh['yh'=2,'z'=8,'k'=2,'x'=4,'yl'=2] {'x','yl'}, dimensions={0} | all-to-all | bytes 786432 | tf_op jit(solution)/shard_map/all_to_all | solution.py:35
  (100 shorter events, 25.0 us)
Async XLA Ops:
  0.9 23.9 %collective-permute-start = (bf16[8,8,384]{2,1,0:T(8,128)(2,1)S(1)}, bf16[8,8,384]{2,1,0:T(8,128)(2,1)S(1)}, u32[]{:S(2)}, u32[]{:S(2)}) collective-permute-start(bf16[8,8,384]{2,1,0:T(8,128)(2,1)S(1)} %get-tuple-element.32), channel_id=1, source_target_pairs={{0,1},{1,2},{2,3},{3,4},{4,5},{5,6},{6,7},{8,9},{9,10},{10,11},{11... | collective-permute-start | bytes 147464 | tf_op jit(solution)/shard_map/ppermute | solution.py:360
  4.3 20.5 %collective-permute-start.1 = (bf16[8,8,384]{2,1,0:T(8,128)(2,1)S(1)}, bf16[8,8,384]{2,1,0:T(8,128)(2,1)S(1)}, u32[]{:S(2)}, u32[]{:S(2)}) collective-permute-start(bf16[8,8,384]{2,1,0:T(8,128)(2,1)S(1)} %get-tuple-element.31), channel_id=1, source_target_pairs={{1,0},{2,1},{3,2},{4,3},{5,4},{6,5},{7,6},{9,8},{10,9},{11,10},{12... | collective-permute-start | bytes 147464 | tf_op jit(solution)/shard_map/ppermute | solution.py:361
  6.9 15.1 %collective-permute-start.4 = (bf16[48,384]{1,0:T(8,128)(2,1)}, bf16[48,384]{1,0:T(8,128)(2,1)S(1)}, u32[]{:S(2)}, u32[]{:S(2)}) collective-permute-start(bf16[48,384]{1,0:T(8,128)(2,1)} %param.30), channel_id=1, source_target_pairs={{0,0},{1,16},{2,32},{3,48},{4,64},{5,80},{6,96},{7,112},{8,8},{9,2... | collective-permute-start | bytes 110600 | tf_op jit(solution)/shard_map/ppermute | solution.py:394
  11.2 21.5 %all-to-all-start.1 = ((bf16[8,48,384]{2,1,0:T(8,128)(2,1)}), bf16[8,48,384]{2,1,0:T(8,128)(2,1)S(1)}, u32[]{:S(2)}, u32[]{:S(2)}) async-start(bf16[8,48,384]{2,1,0:T(8,128)(2,1)} %copies.1), calls=%async_computation.1 | async-start | bytes 589824 | tf_op jit(solution)/shard_map/all_to_all | solution.py:35
  22.0 14.1 %collective-permute-start.5 = (bf16[48,384]{1,0:T(8,128)(2,1)S(1)}, bf16[48,384]{1,0:T(8,128)(2,1)S(1)}, u32[]{:S(2)}, u32[]{:S(2)}) collective-permute-start(bf16[48,384]{1,0:T(8,128)(2,1)S(1)} %collective-permute-done.4.refs_12_), channel_id=1, source_target_pairs={{0,128},{128,0},{1,129},{129,1},{2,130},{130,2},{3,131},{131,3},{4... | collective-permute-start | bytes 110600 | tf_op jit(solution)/shard_map/ppermute | solution.py:421
  24.9 11.2 %collective-permute-start.2 = (bf16[3,32,384]{2,1,0:T(8,128)(2,1)S(1)}, bf16[3,32,384]{2,1,0:T(8,128)(2,1)S(1)}, u32[]{:S(2)}, u32[]{:S(2)}) collective-permute-start(bf16[3,32,384]{2,1,0:T(8,128)(2,1)S(1)} %get-tuple-element.18), channel_id=1, source_target_pairs={{0,8},{8,16},{16,24},{24,32},{32,40},{40,48},{48,56},{56,64},{64,7... | collective-permute-start | bytes 221192 | tf_op jit(solution)/shard_map/ppermute | solution.py:365
  26.2 9.9 %collective-permute-start.3 = (bf16[3,32,384]{2,1,0:T(8,128)(2,1)S(1)}, bf16[3,32,384]{2,1,0:T(8,128)(2,1)S(1)}, u32[]{:S(2)}, u32[]{:S(2)}) collective-permute-start(bf16[3,32,384]{2,1,0:T(8,128)(2,1)S(1)} %get-tuple-element.19), channel_id=1, source_target_pairs={{8,0},{16,8},{24,16},{32,24},{40,32},{48,40},{56,48},{64,56},{72,6... | collective-permute-start | bytes 221192 | tf_op jit(solution)/shard_map/ppermute | solution.py:366
  28.7 36.1 %copy-start.2 = (s32[7]{0:T(128)S(1)}, s32[7]{0:T(128)}, u32[]{:S(2)}) copy-start(s32[7]{0:T(128)} %stack.23.refs_0_) | copy-start | bytes 88
  32.7 20.1 %collective-permute-start.7 = (bf16[8,48,384]{2,1,0:T(8,128)(2,1)S(1)}, bf16[8,48,384]{2,1,0:T(8,128)(2,1)S(1)}, u32[]{:S(2)}, u32[]{:S(2)}) collective-permute-start(bf16[8,48,384]{2,1,0:T(8,128)(2,1)S(1)} %all-to-all-done.1.refs_2_), channel_id=1, source_target_pairs={{0,128},{128,0},{1,129},{129,1},{2,130},{130,2},{3,131},{131,3},{4... | collective-permute-start | bytes 884744 | tf_op jit(solution)/shard_map/ppermute | solution.py:398
  45.4 18.6 %all-to-all-start = ((bf16[8,8,3072]{2,1,0:T(8,128)(2,1)}), bf16[8,8,3072]{2,1,0:T(8,128)(2,1)S(1)}, u32[]{:S(2)}, u32[]{:S(2)}) async-start(bf16[8,8,3072]{2,1,0:T(8,128)(2,1)} %bitcast.32), calls=%async_computation | async-start | bytes 786432 | tf_op jit(solution)/shard_map/all_to_all | solution.py:35
  52.8 11.2 %collective-permute-start.6 = (bf16[8,48,384]{2,1,0:T(8,128)(2,1)S(1)}, bf16[8,48,384]{2,1,0:T(8,128)(2,1)S(1)}, u32[]{:S(2)}, u32[]{:S(2)}) collective-permute-start(bf16[8,48,384]{2,1,0:T(8,128)(2,1)S(1)} %all-to-all-done.1.refs_2_), channel_id=1, source_target_pairs={{0,8},{8,0},{1,9},{9,1},{2,10},{10,2},{3,11},{11,3},{4,12},{12,4},... | collective-permute-start | bytes 884744 | tf_op jit(solution)/shard_map/ppermute | solution.py:443
  52.8 11.2 %collective-permute-start.8 = (bf16[8,48,384]{2,1,0:T(8,128)(2,1)S(1)}, bf16[8,48,384]{2,1,0:T(8,128)(2,1)S(1)}, u32[]{:S(2)}, u32[]{:S(2)}) collective-permute-start(bf16[8,48,384]{2,1,0:T(8,128)(2,1)S(1)} %collective-permute-done.7.refs_4_), channel_id=1, source_target_pairs={{0,8},{8,0},{1,9},{9,1},{2,10},{10,2},{3,11},{11,3},{4,12},{12,4},... | collective-permute-start | bytes 884744 | tf_op jit(solution)/shard_map/ppermute | solution.py:443
  53.3 8.8 %collective-permute-start.10 = (bf16[96,384]{1,0:T(8,128)(2,1)}, bf16[96,384]{1,0:T(8,128)(2,1)S(1)}, u32[]{:S(2)}, u32[]{:S(2)}) collective-permute-start(bf16[96,384]{1,0:T(8,128)(2,1)} %get-tuple-element.21.refs_3_), channel_id=1, source_target_pairs={{0,32},{16,48},{32,64},{48,80},{64,96},{80,112},{96,0},{112,16},{1... | collective-permute-start | bytes 221192 | tf_op jit(solution)/shard_map/ppermute | solution.py:440
  53.3 9.5 %collective-permute-start.11 = (bf16[96,384]{1,0:T(8,128)(2,1)}, bf16[96,384]{1,0:T(8,128)(2,1)S(1)}, u32[]{:S(2)}, u32[]{:S(2)}) collective-permute-start(bf16[96,384]{1,0:T(8,128)(2,1)} %get-tuple-element.21.refs_3_), channel_id=1, source_target_pairs={{0,112},{16,0},{32,16},{48,32},{64,48},{80,64},{96,80},{112,96},{1... | collective-permute-start | bytes 221192 | tf_op jit(solution)/shard_map/ppermute | solution.py:440
  55.4 8.0 %collective-permute-start.9 = (bf16[96,384]{1,0:T(8,128)(2,1)}, bf16[96,384]{1,0:T(8,128)(2,1)S(1)}, u32[]{:S(2)}, u32[]{:S(2)}) collective-permute-start(bf16[96,384]{1,0:T(8,128)(2,1)} %get-tuple-element.21.refs_3_), channel_id=1, source_target_pairs={{0,16},{16,32},{32,48},{48,64},{64,80},{80,96},{96,112},{112,0},{1... | collective-permute-start | bytes 221192 | tf_op jit(solution)/shard_map/ppermute | solution.py:440
  70.2 22.4 %all-to-all-start.2 = ((bf16[8,64,192]{2,1,0:T(8,128)(2,1)}), bf16[8,64,192]{2,1,0:T(8,128)(2,1)S(1)}, u32[]{:S(2)}, u32[]{:S(2)}) async-start(bf16[8,64,192]{2,1,0:T(8,128)(2,1)} %bitcast.9), calls=%async_computation.2 | async-start | bytes 524288 | tf_op jit(solution)/shard_map/all_to_all | solution.py:35
  75.9 11.6 %collective-permute-start.12 = (bf16[96,384]{1,0:T(8,128)(2,1)S(1)}, bf16[96,384]{1,0:T(8,128)(2,1)S(1)}, u32[]{:S(2)}, u32[]{:S(2)}) collective-permute-start(bf16[96,384]{1,0:T(8,128)(2,1)S(1)} %copy-done.10), channel_id=1, source_target_pairs={{0,48},{16,64},{32,80},{48,96},{64,112},{80,0},{96,16},{112,32},{1... | collective-permute-start | bytes 221192 | tf_op jit(solution)/shard_map/ppermute | solution.py:440
  76.9 10.6 %collective-permute-start.13 = (bf16[96,384]{1,0:T(8,128)(2,1)S(1)}, bf16[96,384]{1,0:T(8,128)(2,1)S(1)}, u32[]{:S(2)}, u32[]{:S(2)}) collective-permute-start(bf16[96,384]{1,0:T(8,128)(2,1)S(1)} %copy-done.10), channel_id=1, source_target_pairs={{0,64},{16,80},{32,96},{48,112},{64,0},{80,16},{96,32},{112,48},{1... | collective-permute-start | bytes 221192 | tf_op jit(solution)/shard_map/ppermute | solution.py:440
  79.4 10.1 %collective-permute-start.14 = (bf16[96,384]{1,0:T(8,128)(2,1)S(1)}, bf16[96,384]{1,0:T(8,128)(2,1)S(1)}, u32[]{:S(2)}, u32[]{:S(2)}) collective-permute-start(bf16[96,384]{1,0:T(8,128)(2,1)S(1)} %copy-done.10), channel_id=1, source_target_pairs={{0,80},{16,96},{32,112},{48,0},{64,16},{80,32},{96,48},{112,64},{1... | collective-permute-start | bytes 221192 | tf_op jit(solution)/shard_map/ppermute | solution.py:440
  84.0 8.5 %collective-permute-start.15 = (bf16[96,384]{1,0:T(8,128)(2,1)S(1)}, bf16[96,384]{1,0:T(8,128)(2,1)S(1)}, u32[]{:S(2)}, u32[]{:S(2)}) collective-permute-start(bf16[96,384]{1,0:T(8,128)(2,1)S(1)} %copy-done.10), channel_id=1, source_target_pairs={{0,96},{16,112},{32,0},{48,16},{64,32},{80,48},{96,64},{112,80},{1... | collective-permute-start | bytes 221192 | tf_op jit(solution)/shard_map/ppermute | solution.py:440
  94.5 18.6 %all-to-all-start.3 = ((bf16[8,64,384]{2,1,0:T(8,128)(2,1)}), bf16[8,64,384]{2,1,0:T(8,128)(2,1)S(1)}, u32[]{:S(2)}, u32[]{:S(2)}) async-start(bf16[8,64,384]{2,1,0:T(8,128)(2,1)} %bitcast.14), calls=%async_computation.3 | async-start | bytes 786432 | tf_op jit(solution)/shard_map/all_to_all | solution.py:35
  98.6 16.8 %collective-permute-start.16 = (bf16[64,192]{1,0:T(8,128)(2,1)S(1)}, bf16[64,192]{1,0:T(8,128)(2,1)S(1)}, u32[]{:S(2)}, u32[]{:S(2)}) collective-permute-start(bf16[64,192]{1,0:T(8,128)(2,1)S(1)} %get-tuple-element.23.refs_0_), channel_id=1, source_target_pairs={{0,128},{128,0},{1,129},{129,1},{2,130},{130,2},{3,131},{131,3},{4... | collective-permute-start | bytes 73736 | tf_op jit(solution)/shard_map/ppermute | solution.py:463
  116.7 18.3 %collective-permute-start.18 = (bf16[8,96,384]{2,1,0:T(8,128)(2,1)S(1)}, bf16[8,96,384]{2,1,0:T(8,128)(2,1)S(1)}, u32[]{:S(2)}, u32[]{:S(2)}) collective-permute-start(bf16[8,96,384]{2,1,0:T(8,128)(2,1)S(1)} %get-tuple-element.28.refs_3_), channel_id=1, source_target_pairs={{0,8},{8,0},{1,9},{9,1},{2,10},{10,2},{3,11},{11,3},{4,12},{12,4},... | collective-permute-start | bytes 1769480 | tf_op jit(solution)/shard_map/ppermute | solution.py:474
  117.0 5.9 %collective-permute-start.17 = (f32[64,256]{1,0:T(8,128)S(1)}, f32[64,256]{1,0:T(8,128)S(1)}, u32[]{:S(2)}, u32[]{:S(2)}) collective-permute-start(f32[64,256]{1,0:T(8,128)S(1)} %get-tuple-element.26), channel_id=1, source_target_pairs={{0,128},{128,0},{1,129},{129,1},{2,130},{130,2},{3,131},{131,3},{4... | collective-permute-start | bytes 196616 | tf_op jit(solution)/shard_map/ppermute | solution.py:473
  (28 other events, 282.2 us)

commit v5 on v3

--- a/solution.py
+++ b/solution.py
@@ -229,8 +229,7 @@
     copies_out[...] = jnp.concatenate([mid] * 8, axis=0)
 
 
-def project_kernel(mids, gain, wq, wk, wv, split, over_yh, q_out, kv_out, split_out):
-    split_out[...] = jnp.concatenate([split[...], over_yh[...]], axis=0)
+def project_kernel(mids, gain, wq, wk, wv, split, over_yh, q_out, kv_out):
     parts = [mids[64 * i : 64 * i + 64, :].astype(F32) for i in range(8)]
     total = jnp.zeros((64, 1), F32)
     for part in parts:
@@ -244,13 +243,13 @@
     queries, keys, values = sums
     q_out[...] = queries.astype(BF)
     both = jnp.concatenate([keys, values[:, 128:192], values[:, 0:128]], axis=1).astype(BF)
-    kv_out[...] = jnp.concatenate([both] * 8, axis=0)
-
-
-def attend_kernel(q_own, q_other, kv, *refs):
-    (own_out, other_out, stack_out), blocks = refs[8:], refs[:8]
-    for i, block in enumerate(blocks):
-        stack_out[i] = block[...]
+    rows = jnp.concatenate([both, split[...], over_yh[...]], axis=0)
+    for i in range(8):
+        kv_out[i] = rows
+
+
+def attend_kernel(q_own, q_other, blocks, others, own_out, other_out):
+    kv = jnp.concatenate([ref[i, 0:64, :] for ref in (blocks, others) for i in range(8)], axis=0)
     queries = jnp.concatenate([q_own[...], q_other[...]], axis=0)
     lane = lax.broadcasted_iota(jnp.int32, (1, 128), 1)
     low = (lane < HEAD).astype(F32).astype(BF)
@@ -298,21 +297,19 @@
     ).astype(BF)
 
 
-def lift_kernel(where, parts, mid, weight, over_k, up_out):
+def lift_kernel(where, parts, mid, blocks, others, up_out):
     sums = mid[...].astype(F32)
     for i in range(8):
         sums += parts[64 * i : 64 * i + 64, :].astype(F32)
     lifted = sums.astype(BF)
-    here = where[5] * 2 + where[4]
     source = lax.broadcasted_iota(jnp.int32, (192, 192), 0)
     target = lax.broadcasted_iota(jnp.int32, (192, 192), 1)
-    turn = (target // 48) % 2 * 2 + target // 96
-    same = (source // 48 == turn ^ here) & (source % 48 == target % 48)
+    owner = (((target // 48) % 2) ^ where[5]) * 2 + ((target // 96) ^ where[4])
+    same = (source // 48 == owner) & (source % 48 == target % 48)
     lifted = dot(lifted, same.astype(F32).astype(BF)).astype(BF)
     for i in range(8):
-        rows = jnp.concatenate([weight[i], over_k[i]], axis=0)
-        column = pl.multiple_of(lax.rem(where[6] + 8 - i, 8) * 384, 128)
-        up_out[:, pl.ds(column, 384)] = dot(lifted, rows).astype(BF)
+        rows = jnp.concatenate([blocks[i, 64:160, :], others[i, 64:160, :]], axis=0)
+        up_out[:, 384 * i : 384 * i + 384] = dot(lifted, rows).astype(BF)
 
 
 def last_kernel(parts, level1, resid, split, out):
@@ -444,9 +441,9 @@
         name="middle",
     )
     mids = exchange(mids, COL)
-    q, kv, split_block = call(
+    q, kv = call(
         project_kernel,
-        (shaped((64, 192), BF), shaped((512, 384), BF), shaped((96, 384), BF)),
+        (shaped((64, 192), BF), shaped((8, 160, 384), BF)),
         (
             mids,
             gain_two.reshape(8, 192),
@@ -459,28 +456,23 @@
         2,
         name="project",
     )
-    split_blocks = [split_block] + [
-        lax.ppermute(split_block, "z", [(i, (i + step) % 8) for i in range(8)])
-        for step in range(1, 8)
-    ]
     q_other = lax.ppermute(q, "yh", swap("yh"))
     kv = exchange(kv, "z")
-    kv = lax.all_gather(kv, "k", axis=0, tiled=True)
-    own, other, split_block = call(
+    kv_other = lax.ppermute(kv, "k", swap("k"))
+    own, other = call(
         attend_kernel,
-        (shaped((64, 256), F32), shaped((64, 256), F32), shaped((8, 96, 384), BF)),
-        (q, q_other, kv, *split_blocks),
+        (shaped((64, 256), F32), shaped((64, 256), F32)),
+        (q, q_other, kv, kv_other),
         3,
         name="attend",
     )
     theirs = lax.ppermute(other, "yh", swap("yh"))
-    split_other = lax.ppermute(split_block, "k", swap("k"))
     parts = call(combine_kernel, [shaped((512, 192), BF)], (own, theirs, out2), 1, name="combine")
     parts = exchange(parts, COL)
     up = call(
         lift_kernel,
         [shaped((64, 3072), BF)],
-        (where, parts, mid, split_block, split_other),
+        (where, parts, mid, kv, kv_other),
         1,
         smem=(0,),
         name="lift",

time: 137 us -> 142 us (1.036)
  blocking collectives: 24.4 us -> 52.7 us
  starting transfers between devices: 58.5 us -> 39.7 us
  waiting for transfers between devices: 28.8 us -> 25.3 us
    all_to_all x2 -> x3, blocking collectives: 22 us -> 52.7 us  [exchange(): return lax.all_to_all(block, axis, split_axis=0, concat_axis=0, tiled=True)]
    ppermute x8 -> x1, starting transfers between devices: 13.9 us -> 0.01 us  [on_device(): kv_other = lax.ppermute(kv, 'k', swap('k'))]
    ppermute x8 -> x1, waiting for transfers between devices: 7.2 us -> 0.01 us  [on_device(): kv_other = lax.ppermute(kv, 'k', swap('k'))]
    all_to_all x4 -> x3, starting transfers between devices: 21.9 us -> 17.6 us  [exchange(): return lax.all_to_all(block, axis, split_axis=0, concat_axis=0, tiled=True)]
    ppermute x1, waiting for transfers between devices: 0.01 us -> 3.83 us  [on_device(): q_other = lax.ppermute(q, 'yh', swap('yh'))]
    all_gather x1 -> x0, blocking collectives: 2.36 us -> none  [on_device(): kv = lax.all_gather(kv, 'k', axis=0, tiled=True)]
    all_to_all x4 -> x3, waiting for transfers between devices: 14.1 us -> 14.1 us  [exchange(): return lax.all_to_all(block, axis, split_axis=0, concat_axis=0, tiled=True)]
  transfers between devices with their start and end apart: 23 -> 15, of which waited for: 10 -> 6; matrix products, arithmetic and copies ran while one was open for 2% -> 2% of each run, Pallas kernels for 7% -> 6%
where the time goes in v5:
time: 142 us; the launch traced here: 141 us
  blocking collectives  52.7 us (37%)
  starting transfers between devices  39.7 us (28%)
  waiting for transfers between devices  25.3 us (18%)
  Pallas kernels  16 us (11%)
  local copies, waits for them, and re-layouts  5.85 us (4%)
    all_to_all x3, blocking collectives, exchange(): return lax.all_to_all(block, axis, split_axis=0, concat_axis=0, tiled=True)  52.7 us
    all_to_all x3, starting transfers between devices, exchange(): return lax.all_to_all(block, axis, split_axis=0, concat_axis=0, tiled=True)  17.6 us
    pallas_call x9, Pallas kernels, call(): pl.pallas_call(kernel, out_shape=out_shape, in_specs=specs, out_specs=out...  16 us
    all_to_all x3, waiting for transfers between devices, exchange(): return lax.all_to_all(block, axis, split_axis=0, concat_axis=0, tiled=True)  14.1 us
    ppermute x1, starting transfers between devices, on_device(): left = lax.ppermute(tokens[:, 8:16], COL, shift(COL, 1))  4.82 us
    ppermute x1, waiting for transfers between devices, on_device(): theirs = lax.ppermute(other, 'yh', swap('yh'))  4.18 us
    ppermute x1, starting transfers between devices, on_device(): split_block = lax.ppermute(split_two, ROW + COL, perm)  3.83 us
    ppermute x1, waiting for transfers between devices, on_device(): q_other = lax.ppermute(q, 'yh', swap('yh'))  3.83 us
  transfers between devices with their start and end apart: 15, of which 6 were waited for; matrix products, arithmetic and copies ran while one was open for 2% of the time, Pallas kernels for 6%

profile of v5, /device:TPU:8, one launch (start us, length us, event | category | flops | bytes accessed | tf_op | source)
XLA Modules:
  0.0 140.8 jit_solution(16081270045795512323)
XLA Ops:
  0.0 3.8 %collective-permute-start.4 = (bf16[48,384]{1,0:T(8,128)(2,1)}, bf16[48,384]{1,0:T(8,128)(2,1)S(1)}, u32[]{:S(2)}, u32[]{:S(2)}) collective-permute-start(bf16[48,384]{1,0:T(8,128)(2,1)} %param.30), channel_id=1, source_target_pairs={{0,0},{1,16},{2,32},{3,48},{4,64},{5,80},{6,96},{7,112},{8,8},{9,2... | collective-permute-start | bytes 110600 | tf_op jit(solution)/shard_map/ppermute | solution.py:389
  4.7 2.1 %collective-permute-start.1 = (bf16[8,8,384]{2,1,0:T(8,128)(2,1)S(1)}, bf16[8,8,384]{2,1,0:T(8,128)(2,1)S(1)}, u32[]{:S(2)}, u32[]{:S(2)}) collective-permute-start(bf16[8,8,384]{2,1,0:T(8,128)(2,1)S(1)} %get-tuple-element.29), channel_id=1, source_target_pairs={{1,0},{2,1},{3,2},{4,3},{5,4},{6,5},{7,6},{9,8},{10,9},{11,10},{12... | collective-permute-start | bytes 147464 | tf_op jit(solution)/shard_map/ppermute | solution.py:356
  6.8 4.8 %collective-permute-start = (bf16[8,8,384]{2,1,0:T(8,128)(2,1)S(1)}, bf16[8,8,384]{2,1,0:T(8,128)(2,1)S(1)}, u32[]{:S(2)}, u32[]{:S(2)}) collective-permute-start(bf16[8,8,384]{2,1,0:T(8,128)(2,1)S(1)} %get-tuple-element.30), channel_id=1, source_target_pairs={{0,1},{1,2},{2,3},{3,4},{4,5},{5,6},{6,7},{8,9},{9,10},{10,11},{11... | collective-permute-start | bytes 147464 | tf_op jit(solution)/shard_map/ppermute | solution.py:355
  13.2 7.8 %all-to-all-start.1 = ((bf16[8,48,384]{2,1,0:T(8,128)(2,1)}), bf16[8,48,384]{2,1,0:T(8,128)(2,1)S(1)}, u32[]{:S(2)}, u32[]{:S(2)}) async-start(bf16[8,48,384]{2,1,0:T(8,128)(2,1)} %copies.1), calls=%async_computation.1 | async-start | bytes 589824 | tf_op jit(solution)/shard_map/all_to_all | solution.py:35
  22.1 1.3 collective-permute-start.2
  23.4 1.3 collective-permute-start.3
  26.0 7.1 %all-to-all-done.1.refs_2_ = bf16[8,48,384]{2,1,0:T(8,128)(2,1)S(1)} async-done(((bf16[8,48,384]{2,1,0:T(8,128)(2,1)}), bf16[8,48,384]{2,1,0:T(8,128)(2,1)S(1)}, u32[]{:S(2)}, u32[]{:S(2)}) %all-to-all-start.1) | async-done | bytes 294944 | tf_op jit(solution)/shard_map/all_to_all | solution.py:35
  33.1 2.7 %collective-permute-start.6 = (bf16[8,48,384]{2,1,0:T(8,128)(2,1)S(1)}, bf16[8,48,384]{2,1,0:T(8,128)(2,1)S(1)}, u32[]{:S(2)}, u32[]{:S(2)}) collective-permute-start(bf16[8,48,384]{2,1,0:T(8,128)(2,1)S(1)} %all-to-all-done.1.refs_2_), channel_id=1, source_target_pairs={{0,128},{128,0},{1,129},{129,1},{2,130},{130,2},{3,131},{131,3},{4... | collective-permute-start | bytes 884744 | tf_op jit(solution)/shard_map/ppermute | solution.py:393
  37.1 8.0 %finest.1 = (bf16[128,384]{1,0:T(8,128)(2,1)}, bf16[32,768]{1,0:T(8,128)(2,1)}, bf16[64,3072]{1,0:T(8,128)(2,1)}, bf16[48,384]{1,0:T(8,128)(2,1)}) custom-call(s32[7]{0:T(128)} %stack.23.refs_0_, bf16[8,16,384]{2,1,0:T(8,128)(2,1)} %refs_1_.1, bf16[8,8,384]{2,1,0:T(8,128)(2,1)} %copy-done.12, bf16[8,8,384]{2,1,0:T(8,128)(2,1)} %copy-done.11, ...), custom_call_target="tpu_custom_call" | custom-call | flops 6000000000 | bytes 18000000 | tf_op jit(solution)/shard_map/finest/pallas_call | solution.py:84
  45.1 5.9 %all-to-all-start = ((bf16[8,8,3072]{2,1,0:T(8,128)(2,1)}), bf16[8,8,3072]{2,1,0:T(8,128)(2,1)S(1)}, u32[]{:S(2)}, u32[]{:S(2)}) async-start(bf16[8,8,3072]{2,1,0:T(8,128)(2,1)} %bitcast.29), calls=%async_computation | async-start | bytes 786432 | tf_op jit(solution)/shard_map/all_to_all | solution.py:35
  51.5 6.3 %all-to-all-done = bf16[8,8,3072]{2,1,0:T(8,128)(2,1)S(1)} async-done(((bf16[8,8,3072]{2,1,0:T(8,128)(2,1)}), bf16[8,8,3072]{2,1,0:T(8,128)(2,1)S(1)}, u32[]{:S(2)}, u32[]{:S(2)}) %all-to-all-start) | async-done | bytes 393248 | tf_op jit(solution)/shard_map/all_to_all | solution.py:35
  59.5 1.8 %middle.1 = (bf16[64,192]{1,0:T(8,128)(2,1)S(1)}, bf16[512,192]{1,0:T(8,128)(2,1)}) custom-call(s32[7]{0:T(128)S(1)} %copy-done.2, bf16[64,3072]{1,0:T(8,128)(2,1)S(1)} %bitcast.20, bf16[8,48,384]{2,1,0:T(8,128)(2,1)S(1)} %all-to-all-done.1.refs_2_, bf16[8,48,384]{2,1,0:T(8,128)(2,1)S(1)} %collective-permute-done.5.refs_3_, ...), custom_call_target="tpu_custom_call" | custom-call | flops 2000000000 | bytes 6000000 | tf_op jit(solution)/shard_map/middle/pallas_call | solution.py:84
  61.3 3.9 %all-to-all-start.2 = ((bf16[8,64,192]{2,1,0:T(8,128)(2,1)}), bf16[8,64,192]{2,1,0:T(8,128)(2,1)S(1)}, u32[]{:S(2)}, u32[]{:S(2)}) async-start(bf16[8,64,192]{2,1,0:T(8,128)(2,1)} %bitcast.9), calls=%async_computation.2 | async-start | bytes 524288 | tf_op jit(solution)/shard_map/all_to_all | solution.py:35
  65.2 2.2 %collective-permute-start.8 = (bf16[48,384]{1,0:T(8,128)(2,1)S(1)}, bf16[48,384]{1,0:T(8,128)(2,1)S(1)}, u32[]{:S(2)}, u32[]{:S(2)}) collective-permute-start(bf16[48,384]{1,0:T(8,128)(2,1)S(1)} %copy-done.13), channel_id=1, source_target_pairs={{0,128},{128,0},{1,129},{129,1},{2,130},{130,2},{3,131},{131,3},{4... | collective-permute-start | bytes 110600 | tf_op jit(solution)/shard_map/ppermute | solution.py:433
  67.5 3.1 %collective-permute-done.8.refs_6_ = bf16[48,384]{1,0:T(8,128)(2,1)S(1)} collective-permute-done((bf16[48,384]{1,0:T(8,128)(2,1)S(1)}, bf16[48,384]{1,0:T(8,128)(2,1)S(1)}, u32[]{:S(2)}, u32[]{:S(2)}) %collective-permute-start.8) | collective-permute-done | bytes 36896 | tf_op jit(solution)/shard_map/ppermute | solution.py:433
  72.5 30.7 %all_to_all.54.refs_2_.refs_3_ = bf16[8,160,384]{2,1,0:T(8,128)(2,1)S(1)} all-to-all(bf16[8,160,384]{2,1,0:T(8,128)(2,1)S(1)} %get-tuple-element.23), channel_id=1, replica_groups=mesh['yh'=2,'z'=8,'k'=2,'x'=4,'yl'=2] {'z'}, dimensions={0} | all-to-all | bytes 1966080 | tf_op jit(solution)/shard_map/all_to_all | solution.py:35
  103.2 1.6 %collective-permute-start.9 = (bf16[64,192]{1,0:T(8,128)(2,1)S(1)}, bf16[64,192]{1,0:T(8,128)(2,1)S(1)}, u32[]{:S(2)}, u32[]{:S(2)}) collective-permute-start(bf16[64,192]{1,0:T(8,128)(2,1)S(1)} %get-tuple-element.22.refs_0_), channel_id=1, source_target_pairs={{0,128},{128,0},{1,129},{129,1},{2,130},{130,2},{3,131},{131,3},{4... | collective-permute-start | bytes 73736 | tf_op jit(solution)/shard_map/ppermute | solution.py:459
  104.8 3.8 %collective-permute-done.9.refs_1_ = bf16[64,192]{1,0:T(8,128)(2,1)S(1)} collective-permute-done((bf16[64,192]{1,0:T(8,128)(2,1)S(1)}, bf16[64,192]{1,0:T(8,128)(2,1)S(1)}, u32[]{:S(2)}, u32[]{:S(2)}) %collective-permute-start.9) | collective-permute-done | bytes 24608 | tf_op jit(solution)/shard_map/ppermute | solution.py:459
  108.6 1.2 attend.1
  109.9 1.7 %collective-permute-start.11 = (f32[64,256]{1,0:T(8,128)S(1)}, f32[64,256]{1,0:T(8,128)S(1)}, u32[]{:S(2)}, u32[]{:S(2)}) collective-permute-start(f32[64,256]{1,0:T(8,128)S(1)} %get-tuple-element.25), channel_id=1, source_target_pairs={{0,128},{128,0},{1,129},{129,1},{2,130},{130,2},{3,131},{131,3},{4... | collective-permute-start | bytes 196616 | tf_op jit(solution)/shard_map/ppermute | solution.py:469
  111.6 4.2 %collective-permute-done.11.refs_1_ = f32[64,256]{1,0:T(8,128)S(1)} collective-permute-done((f32[64,256]{1,0:T(8,128)S(1)}, f32[64,256]{1,0:T(8,128)S(1)}, u32[]{:S(2)}, u32[]{:S(2)}) %collective-permute-start.11) | collective-permute-done | bytes 65568 | tf_op jit(solution)/shard_map/ppermute | solution.py:469
  116.3 11.5 %all_to_all.55 = bf16[8,64,192]{2,1,0:T(8,128)(2,1)S(1)} all-to-all(bf16[8,64,192]{2,1,0:T(8,128)(2,1)S(1)} %bitcast.25), channel_id=1, replica_groups=mesh['yh'=2,'z'=8,'k'=2,'x'=4,'yl'=2] {'x','yl'}, dimensions={0} | all-to-all | bytes 393216 | tf_op jit(solution)/shard_map/all_to_all | solution.py:35
  129.0 10.5 %all_to_all.56 = bf16[8,8,3072]{2,1,0:T(8,128)(2,1)S(1)} all-to-all(bf16[8,8,3072]{2,1,0:T(8,128)(2,1)S(1)} %bitcast.21), channel_id=1, replica_groups=mesh['yh'=2,'z'=8,'k'=2,'x'=4,'yl'=2] {'x','yl'}, dimensions={0} | all-to-all | bytes 786432 | tf_op jit(solution)/shard_map/all_to_all | solution.py:35
  139.5 1.3 last.1
  (66 shorter events, 11.1 us)
Async XLA Ops:
  0.0 21.7 %copy-start = (f32[256,384]{1,0:T(8,128)S(1)}, f32[256,384]{1,0:T(8,128)}, u32[]{:S(2)}) copy-start(f32[256,384]{1,0:T(8,128)} %param.18) | copy-start | bytes 1179652
  0.0 35.8 %collective-permute-start.4 = (bf16[48,384]{1,0:T(8,128)(2,1)}, bf16[48,384]{1,0:T(8,128)(2,1)S(1)}, u32[]{:S(2)}, u32[]{:S(2)}) collective-permute-start(bf16[48,384]{1,0:T(8,128)(2,1)} %param.30), channel_id=1, source_target_pairs={{0,0},{1,16},{2,32},{3,48},{4,64},{5,80},{6,96},{7,112},{8,8},{9,2... | collective-permute-start | bytes 110600 | tf_op jit(solution)/shard_map/ppermute | solution.py:389
  4.7 17.4 %copy-start.1 = (bf16[8,16,384]{2,1,0:T(8,128)(2,1)S(1)}, bf16[8,16,384]{2,1,0:T(8,128)(2,1)}, u32[]{:S(2)}) copy-start(bf16[8,16,384]{2,1,0:T(8,128)(2,1)} %refs_1_.1) | copy-start | bytes 294916
  4.7 17.4 %collective-permute-start.1 = (bf16[8,8,384]{2,1,0:T(8,128)(2,1)S(1)}, bf16[8,8,384]{2,1,0:T(8,128)(2,1)S(1)}, u32[]{:S(2)}, u32[]{:S(2)}) collective-permute-start(bf16[8,8,384]{2,1,0:T(8,128)(2,1)S(1)} %get-tuple-element.29), channel_id=1, source_target_pairs={{1,0},{2,1},{3,2},{4,3},{5,4},{6,5},{7,6},{9,8},{10,9},{11,10},{12... | collective-permute-start | bytes 147464 | tf_op jit(solution)/shard_map/ppermute | solution.py:356
  6.8 15.3 %collective-permute-start = (bf16[8,8,384]{2,1,0:T(8,128)(2,1)S(1)}, bf16[8,8,384]{2,1,0:T(8,128)(2,1)S(1)}, u32[]{:S(2)}, u32[]{:S(2)}) collective-permute-start(bf16[8,8,384]{2,1,0:T(8,128)(2,1)S(1)} %get-tuple-element.30), channel_id=1, source_target_pairs={{0,1},{1,2},{2,3},{3,4},{4,5},{5,6},{6,7},{8,9},{9,10},{10,11},{11... | collective-permute-start | bytes 147464 | tf_op jit(solution)/shard_map/ppermute | solution.py:355
  13.2 19.9 %all-to-all-start.1 = ((bf16[8,48,384]{2,1,0:T(8,128)(2,1)}), bf16[8,48,384]{2,1,0:T(8,128)(2,1)S(1)}, u32[]{:S(2)}, u32[]{:S(2)}) async-start(bf16[8,48,384]{2,1,0:T(8,128)(2,1)} %copies.1), calls=%async_computation.1 | async-start | bytes 589824 | tf_op jit(solution)/shard_map/all_to_all | solution.py:35
  22.1 13.8 %copy-start.11 = (bf16[8,8,384]{2,1,0:T(8,128)(2,1)}, bf16[8,8,384]{2,1,0:T(8,128)(2,1)S(1)}, u32[]{:S(2)}) copy-start(bf16[8,8,384]{2,1,0:T(8,128)(2,1)S(1)} %collective-permute-done.1.refs_2_.refs_3_) | copy-start | bytes 147460
  22.1 13.8 %copy-start.12 = (bf16[8,8,384]{2,1,0:T(8,128)(2,1)}, bf16[8,8,384]{2,1,0:T(8,128)(2,1)S(1)}, u32[]{:S(2)}) copy-start(bf16[8,8,384]{2,1,0:T(8,128)(2,1)S(1)} %collective-permute-done.refs_1_.refs_2_) | copy-start | bytes 147460
  22.1 13.7 %collective-permute-start.2 = (bf16[3,32,384]{2,1,0:T(8,128)(2,1)S(1)}, bf16[3,32,384]{2,1,0:T(8,128)(2,1)S(1)}, u32[]{:S(2)}, u32[]{:S(2)}) collective-permute-start(bf16[3,32,384]{2,1,0:T(8,128)(2,1)S(1)} %get-tuple-element.17), channel_id=1, source_target_pairs={{0,8},{8,16},{16,24},{24,32},{32,40},{40,48},{48,56},{56,64},{64,7... | collective-permute-start | bytes 221192 | tf_op jit(solution)/shard_map/ppermute | solution.py:360
  23.4 12.4 %collective-permute-start.3 = (bf16[3,32,384]{2,1,0:T(8,128)(2,1)S(1)}, bf16[3,32,384]{2,1,0:T(8,128)(2,1)S(1)}, u32[]{:S(2)}, u32[]{:S(2)}) collective-permute-start(bf16[3,32,384]{2,1,0:T(8,128)(2,1)S(1)} %get-tuple-element.18), channel_id=1, source_target_pairs={{8,0},{16,8},{24,16},{32,24},{40,32},{48,40},{56,48},{64,56},{72,6... | collective-permute-start | bytes 221192 | tf_op jit(solution)/shard_map/ppermute | solution.py:361
  25.9 32.6 %copy-start.2 = (s32[7]{0:T(128)S(1)}, s32[7]{0:T(128)}, u32[]{:S(2)}) copy-start(s32[7]{0:T(128)} %stack.23.refs_0_) | copy-start | bytes 88
  33.1 17.9 %collective-permute-start.6 = (bf16[8,48,384]{2,1,0:T(8,128)(2,1)S(1)}, bf16[8,48,384]{2,1,0:T(8,128)(2,1)S(1)}, u32[]{:S(2)}, u32[]{:S(2)}) collective-permute-start(bf16[8,48,384]{2,1,0:T(8,128)(2,1)S(1)} %all-to-all-done.1.refs_2_), channel_id=1, source_target_pairs={{0,128},{128,0},{1,129},{129,1},{2,130},{130,2},{3,131},{131,3},{4... | collective-permute-start | bytes 884744 | tf_op jit(solution)/shard_map/ppermute | solution.py:393
  45.1 12.7 %all-to-all-start = ((bf16[8,8,3072]{2,1,0:T(8,128)(2,1)}), bf16[8,8,3072]{2,1,0:T(8,128)(2,1)S(1)}, u32[]{:S(2)}, u32[]{:S(2)}) async-start(bf16[8,8,3072]{2,1,0:T(8,128)(2,1)} %bitcast.29), calls=%async_computation | async-start | bytes 786432 | tf_op jit(solution)/shard_map/all_to_all | solution.py:35
  51.0 6.8 %collective-permute-start.5 = (bf16[8,48,384]{2,1,0:T(8,128)(2,1)S(1)}, bf16[8,48,384]{2,1,0:T(8,128)(2,1)S(1)}, u32[]{:S(2)}, u32[]{:S(2)}) collective-permute-start(bf16[8,48,384]{2,1,0:T(8,128)(2,1)S(1)} %all-to-all-done.1.refs_2_), channel_id=1, source_target_pairs={{0,8},{8,0},{1,9},{9,1},{2,10},{10,2},{3,11},{11,3},{4,12},{12,4},... | collective-permute-start | bytes 884744 | tf_op jit(solution)/shard_map/ppermute | solution.py:434
  51.0 6.8 %collective-permute-start.7 = (bf16[8,48,384]{2,1,0:T(8,128)(2,1)S(1)}, bf16[8,48,384]{2,1,0:T(8,128)(2,1)S(1)}, u32[]{:S(2)}, u32[]{:S(2)}) collective-permute-start(bf16[8,48,384]{2,1,0:T(8,128)(2,1)S(1)} %collective-permute-done.6.refs_4_), channel_id=1, source_target_pairs={{0,8},{8,0},{1,9},{9,1},{2,10},{10,2},{3,11},{11,3},{4,12},{12,4},... | collective-permute-start | bytes 884744 | tf_op jit(solution)/shard_map/ppermute | solution.py:434
  59.5 11.9 %copy-start.4 = (bf16[1536,192]{0,1:T(8,128)(2,1)S(1)}, bf16[1536,192]{0,1:T(8,128)(2,1)}, u32[]{:S(2)}) copy-start(bf16[1536,192]{0,1:T(8,128)(2,1)} %param.26) | copy-start | bytes 1769476
  59.5 11.9 %copy-start.5 = (bf16[1536,192]{0,1:T(8,128)(2,1)S(1)}, bf16[1536,192]{0,1:T(8,128)(2,1)}, u32[]{:S(2)}) copy-start(bf16[1536,192]{0,1:T(8,128)(2,1)} %param.27) | copy-start | bytes 1769476
  59.5 11.9 %copy-start.6 = (bf16[1536,192]{0,1:T(8,128)(2,1)S(1)}, bf16[1536,192]{0,1:T(8,128)(2,1)}, u32[]{:S(2)}) copy-start(bf16[1536,192]{0,1:T(8,128)(2,1)} %param.28) | copy-start | bytes 1769476
  61.3 10.1 %all-to-all-start.2 = ((bf16[8,64,192]{2,1,0:T(8,128)(2,1)}), bf16[8,64,192]{2,1,0:T(8,128)(2,1)S(1)}, u32[]{:S(2)}, u32[]{:S(2)}) async-start(bf16[8,64,192]{2,1,0:T(8,128)(2,1)} %bitcast.9), calls=%async_computation.2 | async-start | bytes 524288 | tf_op jit(solution)/shard_map/all_to_all | solution.py:35
  65.2 5.5 %collective-permute-start.8 = (bf16[48,384]{1,0:T(8,128)(2,1)S(1)}, bf16[48,384]{1,0:T(8,128)(2,1)S(1)}, u32[]{:S(2)}, u32[]{:S(2)}) collective-permute-start(bf16[48,384]{1,0:T(8,128)(2,1)S(1)} %copy-done.13), channel_id=1, source_target_pairs={{0,128},{128,0},{1,129},{129,1},{2,130},{130,2},{3,131},{131,3},{4... | collective-permute-start | bytes 110600 | tf_op jit(solution)/shard_map/ppermute | solution.py:433
  103.2 5.4 %collective-permute-start.10 = (bf16[8,160,384]{2,1,0:T(8,128)(2,1)S(1)}, bf16[8,160,384]{2,1,0:T(8,128)(2,1)S(1)}, u32[]{:S(2)}, u32[]{:S(2)}) collective-permute-start(bf16[8,160,384]{2,1,0:T(8,128)(2,1)S(1)} %all_to_all.54.refs_2_.refs_3_), channel_id=1, source_target_pairs={{0,8},{8,0},{1,9},{9,1},{2,10},{10,2},{3,11},{11,3},{4,12},{12,4},... | collective-permute-start | bytes 2949128 | tf_op jit(solution)/shard_map/ppermute | solution.py:461
  103.2 12.5 %copy-start.7 = (bf16[192,1536]{1,0:T(8,128)(2,1)S(1)}, bf16[192,1536]{1,0:T(8,128)(2,1)}, u32[]{:S(2)}) copy-start(bf16[192,1536]{1,0:T(8,128)(2,1)} %refs_2_.1) | copy-start | bytes 1769476
  103.2 5.4 %collective-permute-start.9 = (bf16[64,192]{1,0:T(8,128)(2,1)S(1)}, bf16[64,192]{1,0:T(8,128)(2,1)S(1)}, u32[]{:S(2)}, u32[]{:S(2)}) collective-permute-start(bf16[64,192]{1,0:T(8,128)(2,1)S(1)} %get-tuple-element.22.refs_0_), channel_id=1, source_target_pairs={{0,128},{128,0},{1,129},{129,1},{2,130},{130,2},{3,131},{131,3},{4... | collective-permute-start | bytes 73736 | tf_op jit(solution)/shard_map/ppermute | solution.py:459
  109.9 5.9 %collective-permute-start.11 = (f32[64,256]{1,0:T(8,128)S(1)}, f32[64,256]{1,0:T(8,128)S(1)}, u32[]{:S(2)}, u32[]{:S(2)}) collective-permute-start(f32[64,256]{1,0:T(8,128)S(1)} %get-tuple-element.25), channel_id=1, source_target_pairs={{0,128},{128,0},{1,129},{129,1},{2,130},{130,2},{3,131},{131,3},{4... | collective-permute-start | bytes 196616 | tf_op jit(solution)/shard_map/ppermute | solution.py:469
  (11 other events, 53.0 us)

commit v6 on v3

--- a/solution.py
+++ b/solution.py
@@ -247,10 +247,7 @@
     kv_out[...] = jnp.concatenate([both] * 8, axis=0)
 
 
-def attend_kernel(q_own, q_other, kv, *refs):
-    (own_out, other_out, stack_out), blocks = refs[8:], refs[:8]
-    for i, block in enumerate(blocks):
-        stack_out[i] = block[...]
+def attend_kernel(q_own, q_other, kv, own_out, other_out):
     queries = jnp.concatenate([q_own[...], q_other[...]], axis=0)
     lane = lax.broadcasted_iota(jnp.int32, (1, 128), 1)
     low = (lane < HEAD).astype(F32).astype(BF)
@@ -277,7 +274,10 @@
     other_out[...] = result[64:128]
 
 
-def combine_kernel(mine, theirs, out2, parts_out):
+def combine_kernel(mine, theirs, out2, *refs):
+    (parts_out, stack_out), blocks = refs[8:], refs[:8]
+    for i, block in enumerate(blocks):
+        stack_out[i] = block[...]
     a, b = mine[...], theirs[...]
     factors = []
     for head in range(3):
@@ -466,16 +466,22 @@
     q_other = lax.ppermute(q, "yh", swap("yh"))
     kv = exchange(kv, "z")
     kv = lax.all_gather(kv, "k", axis=0, tiled=True)
-    own, other, split_block = call(
+    own, other = call(
         attend_kernel,
-        (shaped((64, 256), F32), shaped((64, 256), F32), shaped((8, 96, 384), BF)),
-        (q, q_other, kv, *split_blocks),
+        (shaped((64, 256), F32), shaped((64, 256), F32)),
+        (q, q_other, kv),
         3,
         name="attend",
     )
     theirs = lax.ppermute(other, "yh", swap("yh"))
+    parts, split_block = call(
+        combine_kernel,
+        [shaped((512, 192), BF), shaped((8, 96, 384), BF)],
+        (own, theirs, out2, *split_blocks),
+        1,
+        name="combine",
+    )
     split_other = lax.ppermute(split_block, "k", swap("k"))
-    parts = call(combine_kernel, [shaped((512, 192), BF)], (own, theirs, out2), 1, name="combine")
     parts = exchange(parts, COL)
     up = call(
         lift_kernel,

time: 137 us -> 134 us (0.978)
  waiting for transfers between devices: 28.8 us -> 24.9 us
    ppermute x7, waiting for transfers between devices: 7.2 us -> 2.61 us  [on_device(): lax.ppermute(split_block, 'z', [(i, (i + step) % 8) for i in range(8)])]
    ppermute x1, waiting for transfers between devices: 4.29 us -> 1.04 us  [on_device(): theirs = lax.ppermute(other, 'yh', swap('yh'))]
    all_to_all x4, waiting for transfers between devices: 14.1 us -> 17.2 us  [exchange(): return lax.all_to_all(block, axis, split_axis=0, concat_axis=0, tiled=True)]
    all_to_all x4, starting transfers between devices: 21.9 us -> 24 us  [exchange(): return lax.all_to_all(block, axis, split_axis=0, concat_axis=0, tiled=True)]
    ppermute x1, starting transfers between devices: 4.82 us -> 3.42 us  [on_device(): left = lax.ppermute(tokens[:, 8:16], COL, shift(COL, 1))]
  transfers between devices with their start and end apart: 23 -> 23, of which waited for: 10 -> 8; matrix products, arithmetic and copies ran while one was open for 2% -> 1% of each run, Pallas kernels for 7% -> 8%
where the time goes in v6:
time: 134 us; the launch traced here: 133 us
  starting transfers between devices  59.1 us (44%)
  blocking collectives  25.1 us (19%)
  waiting for transfers between devices  24.9 us (19%)
  Pallas kernels  16.8 us (13%)
  local copies, waits for them, and re-layouts  5.97 us (4%)
    all_to_all x4, starting transfers between devices, exchange(): return lax.all_to_all(block, axis, split_axis=0, concat_axis=0, tiled=True)  24 us
    all_to_all x2, blocking collectives, exchange(): return lax.all_to_all(block, axis, split_axis=0, concat_axis=0, tiled=True)  22.7 us
    all_to_all x4, waiting for transfers between devices, exchange(): return lax.all_to_all(block, axis, split_axis=0, concat_axis=0, tiled=True)  17.2 us
    pallas_call x9, Pallas kernels, call(): pl.pallas_call(kernel, out_shape=out_shape, in_specs=specs, out_specs=out...  16.8 us
    ppermute x7, starting transfers between devices, on_device(): lax.ppermute(split_block, 'z', [(i, (i + step) % 8) for i in range(8)])  14.5 us
    ppermute x1, waiting for transfers between devices, on_device(): over_yh = lax.ppermute(split_block, 'yh', swap('yh'))  4.01 us
    unnamed x40, local copies, waits for them, and re-layouts  3.75 us
    ppermute x1, starting transfers between devices, on_device(): left = lax.ppermute(tokens[:, 8:16], COL, shift(COL, 1))  3.42 us
  transfers between devices with their start and end apart: 23, of which 8 were waited for; matrix products, arithmetic and copies ran while one was open for 1% of the time, Pallas kernels for 8%

profile of v6, /device:TPU:8, one launch (start us, length us, event | category | flops | bytes accessed | tf_op | source)
XLA Modules:
  0.0 133.2 jit_solution(8172438990454610785)
XLA Ops:
  0.9 3.4 %collective-permute-start = (bf16[8,8,384]{2,1,0:T(8,128)(2,1)S(1)}, bf16[8,8,384]{2,1,0:T(8,128)(2,1)S(1)}, u32[]{:S(2)}, u32[]{:S(2)}) collective-permute-start(bf16[8,8,384]{2,1,0:T(8,128)(2,1)S(1)} %get-tuple-element.36), channel_id=1, source_target_pairs={{0,1},{1,2},{2,3},{3,4},{4,5},{5,6},{6,7},{8,9},{9,10},{10,11},{11... | collective-permute-start | bytes 147464 | tf_op jit(solution)/shard_map/ppermute | solution.py:358
  4.3 2.6 %collective-permute-start.1 = (bf16[8,8,384]{2,1,0:T(8,128)(2,1)S(1)}, bf16[8,8,384]{2,1,0:T(8,128)(2,1)S(1)}, u32[]{:S(2)}, u32[]{:S(2)}) collective-permute-start(bf16[8,8,384]{2,1,0:T(8,128)(2,1)S(1)} %get-tuple-element.35), channel_id=1, source_target_pairs={{1,0},{2,1},{3,2},{4,3},{5,4},{6,5},{7,6},{9,8},{10,9},{11,10},{12... | collective-permute-start | bytes 147464 | tf_op jit(solution)/shard_map/ppermute | solution.py:359
  6.9 2.6 %collective-permute-start.4 = (bf16[48,384]{1,0:T(8,128)(2,1)}, bf16[48,384]{1,0:T(8,128)(2,1)S(1)}, u32[]{:S(2)}, u32[]{:S(2)}) collective-permute-start(bf16[48,384]{1,0:T(8,128)(2,1)} %param.30), channel_id=1, source_target_pairs={{0,0},{1,16},{2,32},{3,48},{4,64},{5,80},{6,96},{7,112},{8,8},{9,2... | collective-permute-start | bytes 110600 | tf_op jit(solution)/shard_map/ppermute | solution.py:392
  11.2 9.8 %all-to-all-start.1 = ((bf16[8,48,384]{2,1,0:T(8,128)(2,1)}), bf16[8,48,384]{2,1,0:T(8,128)(2,1)S(1)}, u32[]{:S(2)}, u32[]{:S(2)}) async-start(bf16[8,48,384]{2,1,0:T(8,128)(2,1)} %copies.1), calls=%async_computation.1 | async-start | bytes 589824 | tf_op jit(solution)/shard_map/all_to_all | solution.py:35
  25.9 7.1 %all-to-all-done.1.refs_2_ = bf16[8,48,384]{2,1,0:T(8,128)(2,1)S(1)} async-done(((bf16[8,48,384]{2,1,0:T(8,128)(2,1)}), bf16[8,48,384]{2,1,0:T(8,128)(2,1)S(1)}, u32[]{:S(2)}, u32[]{:S(2)}) %all-to-all-start.1) | async-done | bytes 294944 | tf_op jit(solution)/shard_map/all_to_all | solution.py:35
  33.0 2.7 %collective-permute-start.6 = (bf16[8,48,384]{2,1,0:T(8,128)(2,1)S(1)}, bf16[8,48,384]{2,1,0:T(8,128)(2,1)S(1)}, u32[]{:S(2)}, u32[]{:S(2)}) collective-permute-start(bf16[8,48,384]{2,1,0:T(8,128)(2,1)S(1)} %all-to-all-done.1.refs_2_), channel_id=1, source_target_pairs={{0,128},{128,0},{1,129},{129,1},{2,130},{130,2},{3,131},{131,3},{4... | collective-permute-start | bytes 884744 | tf_op jit(solution)/shard_map/ppermute | solution.py:396
  37.0 8.0 %finest.1 = (bf16[128,384]{1,0:T(8,128)(2,1)}, bf16[32,768]{1,0:T(8,128)(2,1)}, bf16[64,3072]{1,0:T(8,128)(2,1)}, bf16[48,384]{1,0:T(8,128)(2,1)}) custom-call(s32[7]{0:T(128)} %stack.23.refs_0_, bf16[8,16,384]{2,1,0:T(8,128)(2,1)} %refs_1_.1, bf16[8,8,384]{2,1,0:T(8,128)(2,1)} %copy-done.11, bf16[8,8,384]{2,1,0:T(8,128)(2,1)} %copy-done.12, ...), custom_call_target="tpu_custom_call" | custom-call | flops 6000000000 | bytes 18000000 | tf_op jit(solution)/shard_map/finest/pallas_call | solution.py:84
  45.0 6.3 %all-to-all-start = ((bf16[8,8,3072]{2,1,0:T(8,128)(2,1)}), bf16[8,8,3072]{2,1,0:T(8,128)(2,1)S(1)}, u32[]{:S(2)}, u32[]{:S(2)}) async-start(bf16[8,8,3072]{2,1,0:T(8,128)(2,1)} %bitcast.32), calls=%async_computation | async-start | bytes 786432 | tf_op jit(solution)/shard_map/all_to_all | solution.py:35
  51.9 6.3 %all-to-all-done = bf16[8,8,3072]{2,1,0:T(8,128)(2,1)S(1)} async-done(((bf16[8,8,3072]{2,1,0:T(8,128)(2,1)}), bf16[8,8,3072]{2,1,0:T(8,128)(2,1)S(1)}, u32[]{:S(2)}, u32[]{:S(2)}) %all-to-all-start) | async-done | bytes 393248 | tf_op jit(solution)/shard_map/all_to_all | solution.py:35
  61.7 3.9 %all-to-all-start.2 = ((bf16[8,64,192]{2,1,0:T(8,128)(2,1)}), bf16[8,64,192]{2,1,0:T(8,128)(2,1)S(1)}, u32[]{:S(2)}, u32[]{:S(2)}) async-start(bf16[8,64,192]{2,1,0:T(8,128)(2,1)} %bitcast.9), calls=%async_computation.2 | async-start | bytes 524288 | tf_op jit(solution)/shard_map/all_to_all | solution.py:35
  67.4 4.0 %collective-permute-done.8.refs_6_ = bf16[48,384]{1,0:T(8,128)(2,1)S(1)} collective-permute-done((bf16[48,384]{1,0:T(8,128)(2,1)S(1)}, bf16[48,384]{1,0:T(8,128)(2,1)S(1)}, u32[]{:S(2)}, u32[]{:S(2)}) %collective-permute-start.8) | collective-permute-done | bytes 36896 | tf_op jit(solution)/shard_map/ppermute | solution.py:436
  73.7 3.9 %all-to-all-start.3 = ((bf16[8,64,384]{2,1,0:T(8,128)(2,1)}), bf16[8,64,384]{2,1,0:T(8,128)(2,1)S(1)}, u32[]{:S(2)}, u32[]{:S(2)}) async-start(bf16[8,64,384]{2,1,0:T(8,128)(2,1)} %bitcast.14), calls=%async_computation.3 | async-start | bytes 786432 | tf_op jit(solution)/shard_map/all_to_all | solution.py:35
  77.6 2.0 %collective-permute-start.11 = (bf16[96,384]{1,0:T(8,128)(2,1)S(1)}, bf16[96,384]{1,0:T(8,128)(2,1)S(1)}, u32[]{:S(2)}, u32[]{:S(2)}) collective-permute-start(bf16[96,384]{1,0:T(8,128)(2,1)S(1)} %get-tuple-element.29.refs_3_), channel_id=1, source_target_pairs={{0,16},{16,32},{32,48},{48,64},{64,80},{80,96},{96,112},{112,0},{1... | collective-permute-start | bytes 221192 | tf_op jit(solution)/shard_map/ppermute | solution.py:463
  79.6 2.4 %collective-permute-start.12 = (bf16[96,384]{1,0:T(8,128)(2,1)S(1)}, bf16[96,384]{1,0:T(8,128)(2,1)S(1)}, u32[]{:S(2)}, u32[]{:S(2)}) collective-permute-start(bf16[96,384]{1,0:T(8,128)(2,1)S(1)} %get-tuple-element.29.refs_3_), channel_id=1, source_target_pairs={{0,32},{16,48},{32,64},{48,80},{64,96},{80,112},{96,0},{112,16},{1... | collective-permute-start | bytes 221192 | tf_op jit(solution)/shard_map/ppermute | solution.py:463
  82.0 2.7 %collective-permute-start.13 = (bf16[96,384]{1,0:T(8,128)(2,1)S(1)}, bf16[96,384]{1,0:T(8,128)(2,1)S(1)}, u32[]{:S(2)}, u32[]{:S(2)}) collective-permute-start(bf16[96,384]{1,0:T(8,128)(2,1)S(1)} %get-tuple-element.29.refs_3_), channel_id=1, source_target_pairs={{0,48},{16,64},{32,80},{48,96},{64,112},{80,0},{96,16},{112,32},{1... | collective-permute-start | bytes 221192 | tf_op jit(solution)/shard_map/ppermute | solution.py:463
  84.7 2.4 %collective-permute-start.14 = (bf16[96,384]{1,0:T(8,128)(2,1)S(1)}, bf16[96,384]{1,0:T(8,128)(2,1)S(1)}, u32[]{:S(2)}, u32[]{:S(2)}) collective-permute-start(bf16[96,384]{1,0:T(8,128)(2,1)S(1)} %get-tuple-element.29.refs_3_), channel_id=1, source_target_pairs={{0,64},{16,80},{32,96},{48,112},{64,0},{80,16},{96,32},{112,48},{1... | collective-permute-start | bytes 221192 | tf_op jit(solution)/shard_map/ppermute | solution.py:463
  87.0 2.1 %collective-permute-start.9 = (bf16[64,192]{1,0:T(8,128)(2,1)S(1)}, bf16[64,192]{1,0:T(8,128)(2,1)S(1)}, u32[]{:S(2)}, u32[]{:S(2)}) collective-permute-start(bf16[64,192]{1,0:T(8,128)(2,1)S(1)} %get-tuple-element.25.refs_0_), channel_id=1, source_target_pairs={{0,128},{128,0},{1,129},{129,1},{2,130},{130,2},{3,131},{131,3},{4... | collective-permute-start | bytes 73736 | tf_op jit(solution)/shard_map/ppermute | solution.py:466
  89.2 3.5 %all-to-all-done.3 = bf16[8,64,384]{2,1,0:T(8,128)(2,1)S(1)} async-done(((bf16[8,64,384]{2,1,0:T(8,128)(2,1)}), bf16[8,64,384]{2,1,0:T(8,128)(2,1)S(1)}, u32[]{:S(2)}, u32[]{:S(2)}) %all-to-all-start.3) | async-done | bytes 393248 | tf_op jit(solution)/shard_map/all_to_all | solution.py:35
  92.7 2.4 %all_gather.3.refs_2_ = bf16[1024,384]{1,0:T(8,128)(2,1)S(1)} all-gather(bf16[512,384]{1,0:T(8,128)(2,1)S(1)} %bitcast.31), channel_id=1, replica_groups=mesh['yh'=2,'z'=8,'k'=2,'x'=4,'yl'=2] {'k'}, dimensions={0}, use_global_device_ids=true | all-gather | bytes 1179648 | tf_op jit(solution)/shard_map/all_gather | solution.py:468
  95.3 3.4 %collective-permute-start.16 = (bf16[96,384]{1,0:T(8,128)(2,1)S(1)}, bf16[96,384]{1,0:T(8,128)(2,1)S(1)}, u32[]{:S(2)}, u32[]{:S(2)}) collective-permute-start(bf16[96,384]{1,0:T(8,128)(2,1)S(1)} %get-tuple-element.29.refs_3_), channel_id=1, source_target_pairs={{0,96},{16,112},{32,0},{48,16},{64,32},{80,48},{96,64},{112,80},{1... | collective-permute-start | bytes 221192 | tf_op jit(solution)/shard_map/ppermute | solution.py:463
  101.4 2.2 %collective-permute-start.10 = (f32[64,256]{1,0:T(8,128)S(1)}, f32[64,256]{1,0:T(8,128)S(1)}, u32[]{:S(2)}, u32[]{:S(2)}) collective-permute-start(f32[64,256]{1,0:T(8,128)S(1)} %get-tuple-element.28), channel_id=1, source_target_pairs={{0,128},{128,0},{1,129},{129,1},{2,130},{130,2},{3,131},{131,3},{4... | collective-permute-start | bytes 196616 | tf_op jit(solution)/shard_map/ppermute | solution.py:476
  104.2 2.0 %collective-permute-done.17.refs_10_ = bf16[96,384]{1,0:T(8,128)(2,1)S(1)} collective-permute-done((bf16[96,384]{1,0:T(8,128)(2,1)S(1)}, bf16[96,384]{1,0:T(8,128)(2,1)S(1)}, u32[]{:S(2)}, u32[]{:S(2)}) %collective-permute-start.17) | collective-permute-done | bytes 73760 | tf_op jit(solution)/shard_map/ppermute | solution.py:463
  108.0 12.0 %all_to_all.61 = bf16[8,64,192]{2,1,0:T(8,128)(2,1)S(1)} all-to-all(bf16[8,64,192]{2,1,0:T(8,128)(2,1)S(1)} %bitcast.26), channel_id=1, replica_groups=mesh['yh'=2,'z'=8,'k'=2,'x'=4,'yl'=2] {'x','yl'}, dimensions={0} | all-to-all | bytes 393216 | tf_op jit(solution)/shard_map/all_to_all | solution.py:35
  121.1 10.8 %all_to_all.62 = bf16[8,8,3072]{2,1,0:T(8,128)(2,1)S(1)} all-to-all(bf16[8,8,3072]{2,1,0:T(8,128)(2,1)S(1)} %bitcast.23), channel_id=1, replica_groups=mesh['yh'=2,'z'=8,'k'=2,'x'=4,'yl'=2] {'x','yl'}, dimensions={0} | all-to-all | bytes 786432 | tf_op jit(solution)/shard_map/all_to_all | solution.py:35
  (82 shorter events, 23.7 us)
Async XLA Ops:
  0.9 21.1 %collective-permute-start = (bf16[8,8,384]{2,1,0:T(8,128)(2,1)S(1)}, bf16[8,8,384]{2,1,0:T(8,128)(2,1)S(1)}, u32[]{:S(2)}, u32[]{:S(2)}) collective-permute-start(bf16[8,8,384]{2,1,0:T(8,128)(2,1)S(1)} %get-tuple-element.36), channel_id=1, source_target_pairs={{0,1},{1,2},{2,3},{3,4},{4,5},{5,6},{6,7},{8,9},{9,10},{10,11},{11... | collective-permute-start | bytes 147464 | tf_op jit(solution)/shard_map/ppermute | solution.py:358
  4.3 17.7 %collective-permute-start.1 = (bf16[8,8,384]{2,1,0:T(8,128)(2,1)S(1)}, bf16[8,8,384]{2,1,0:T(8,128)(2,1)S(1)}, u32[]{:S(2)}, u32[]{:S(2)}) collective-permute-start(bf16[8,8,384]{2,1,0:T(8,128)(2,1)S(1)} %get-tuple-element.35), channel_id=1, source_target_pairs={{1,0},{2,1},{3,2},{4,3},{5,4},{6,5},{7,6},{9,8},{10,9},{11,10},{12... | collective-permute-start | bytes 147464 | tf_op jit(solution)/shard_map/ppermute | solution.py:359
  6.9 28.8 %collective-permute-start.4 = (bf16[48,384]{1,0:T(8,128)(2,1)}, bf16[48,384]{1,0:T(8,128)(2,1)S(1)}, u32[]{:S(2)}, u32[]{:S(2)}) collective-permute-start(bf16[48,384]{1,0:T(8,128)(2,1)} %param.30), channel_id=1, source_target_pairs={{0,0},{1,16},{2,32},{3,48},{4,64},{5,80},{6,96},{7,112},{8,8},{9,2... | collective-permute-start | bytes 110600 | tf_op jit(solution)/shard_map/ppermute | solution.py:392
  11.2 21.8 %all-to-all-start.1 = ((bf16[8,48,384]{2,1,0:T(8,128)(2,1)}), bf16[8,48,384]{2,1,0:T(8,128)(2,1)S(1)}, u32[]{:S(2)}, u32[]{:S(2)}) async-start(bf16[8,48,384]{2,1,0:T(8,128)(2,1)} %copies.1), calls=%async_computation.1 | async-start | bytes 589824 | tf_op jit(solution)/shard_map/all_to_all | solution.py:35
  22.1 13.7 %collective-permute-start.2 = (bf16[3,32,384]{2,1,0:T(8,128)(2,1)S(1)}, bf16[3,32,384]{2,1,0:T(8,128)(2,1)S(1)}, u32[]{:S(2)}, u32[]{:S(2)}) collective-permute-start(bf16[3,32,384]{2,1,0:T(8,128)(2,1)S(1)} %get-tuple-element.20), channel_id=1, source_target_pairs={{0,8},{8,16},{16,24},{24,32},{32,40},{40,48},{48,56},{56,64},{64,7... | collective-permute-start | bytes 221192 | tf_op jit(solution)/shard_map/ppermute | solution.py:363
  23.4 12.4 %collective-permute-start.3 = (bf16[3,32,384]{2,1,0:T(8,128)(2,1)S(1)}, bf16[3,32,384]{2,1,0:T(8,128)(2,1)S(1)}, u32[]{:S(2)}, u32[]{:S(2)}) collective-permute-start(bf16[3,32,384]{2,1,0:T(8,128)(2,1)S(1)} %get-tuple-element.21), channel_id=1, source_target_pairs={{8,0},{16,8},{24,16},{32,24},{40,32},{48,40},{56,48},{64,56},{72,6... | collective-permute-start | bytes 221192 | tf_op jit(solution)/shard_map/ppermute | solution.py:364
  25.9 33.0 %copy-start.2 = (s32[7]{0:T(128)S(1)}, s32[7]{0:T(128)}, u32[]{:S(2)}) copy-start(s32[7]{0:T(128)} %stack.23.refs_0_) | copy-start | bytes 88
  33.0 18.4 %collective-permute-start.6 = (bf16[8,48,384]{2,1,0:T(8,128)(2,1)S(1)}, bf16[8,48,384]{2,1,0:T(8,128)(2,1)S(1)}, u32[]{:S(2)}, u32[]{:S(2)}) collective-permute-start(bf16[8,48,384]{2,1,0:T(8,128)(2,1)S(1)} %all-to-all-done.1.refs_2_), channel_id=1, source_target_pairs={{0,128},{128,0},{1,129},{129,1},{2,130},{130,2},{3,131},{131,3},{4... | collective-permute-start | bytes 884744 | tf_op jit(solution)/shard_map/ppermute | solution.py:396
  45.0 13.2 %all-to-all-start = ((bf16[8,8,3072]{2,1,0:T(8,128)(2,1)}), bf16[8,8,3072]{2,1,0:T(8,128)(2,1)S(1)}, u32[]{:S(2)}, u32[]{:S(2)}) async-start(bf16[8,8,3072]{2,1,0:T(8,128)(2,1)} %bitcast.32), calls=%async_computation | async-start | bytes 786432 | tf_op jit(solution)/shard_map/all_to_all | solution.py:35
  51.4 6.8 %collective-permute-start.5 = (bf16[8,48,384]{2,1,0:T(8,128)(2,1)S(1)}, bf16[8,48,384]{2,1,0:T(8,128)(2,1)S(1)}, u32[]{:S(2)}, u32[]{:S(2)}) collective-permute-start(bf16[8,48,384]{2,1,0:T(8,128)(2,1)S(1)} %all-to-all-done.1.refs_2_), channel_id=1, source_target_pairs={{0,8},{8,0},{1,9},{9,1},{2,10},{10,2},{3,11},{11,3},{4,12},{12,4},... | collective-permute-start | bytes 884744 | tf_op jit(solution)/shard_map/ppermute | solution.py:437
  51.4 6.8 %collective-permute-start.7 = (bf16[8,48,384]{2,1,0:T(8,128)(2,1)S(1)}, bf16[8,48,384]{2,1,0:T(8,128)(2,1)S(1)}, u32[]{:S(2)}, u32[]{:S(2)}) collective-permute-start(bf16[8,48,384]{2,1,0:T(8,128)(2,1)S(1)} %collective-permute-done.6.refs_4_), channel_id=1, source_target_pairs={{0,8},{8,0},{1,9},{9,1},{2,10},{10,2},{3,11},{11,3},{4,12},{12,4},... | collective-permute-start | bytes 884744 | tf_op jit(solution)/shard_map/ppermute | solution.py:437
  61.7 10.1 %all-to-all-start.2 = ((bf16[8,64,192]{2,1,0:T(8,128)(2,1)}), bf16[8,64,192]{2,1,0:T(8,128)(2,1)S(1)}, u32[]{:S(2)}, u32[]{:S(2)}) async-start(bf16[8,64,192]{2,1,0:T(8,128)(2,1)} %bitcast.9), calls=%async_computation.2 | async-start | bytes 524288 | tf_op jit(solution)/shard_map/all_to_all | solution.py:35
  65.6 5.8 %collective-permute-start.8 = (bf16[48,384]{1,0:T(8,128)(2,1)S(1)}, bf16[48,384]{1,0:T(8,128)(2,1)S(1)}, u32[]{:S(2)}, u32[]{:S(2)}) collective-permute-start(bf16[48,384]{1,0:T(8,128)(2,1)S(1)} %copy-done.13), channel_id=1, source_target_pairs={{0,128},{128,0},{1,129},{129,1},{2,130},{130,2},{3,131},{131,3},{4... | collective-permute-start | bytes 110600 | tf_op jit(solution)/shard_map/ppermute | solution.py:436
  73.7 19.0 %all-to-all-start.3 = ((bf16[8,64,384]{2,1,0:T(8,128)(2,1)}), bf16[8,64,384]{2,1,0:T(8,128)(2,1)S(1)}, u32[]{:S(2)}, u32[]{:S(2)}) async-start(bf16[8,64,384]{2,1,0:T(8,128)(2,1)} %bitcast.14), calls=%async_computation.3 | async-start | bytes 786432 | tf_op jit(solution)/shard_map/all_to_all | solution.py:35
  77.6 17.7 %collective-permute-start.11 = (bf16[96,384]{1,0:T(8,128)(2,1)S(1)}, bf16[96,384]{1,0:T(8,128)(2,1)S(1)}, u32[]{:S(2)}, u32[]{:S(2)}) collective-permute-start(bf16[96,384]{1,0:T(8,128)(2,1)S(1)} %get-tuple-element.29.refs_3_), channel_id=1, source_target_pairs={{0,16},{16,32},{32,48},{48,64},{64,80},{80,96},{96,112},{112,0},{1... | collective-permute-start | bytes 221192 | tf_op jit(solution)/shard_map/ppermute | solution.py:463
  79.6 19.1 %collective-permute-start.12 = (bf16[96,384]{1,0:T(8,128)(2,1)S(1)}, bf16[96,384]{1,0:T(8,128)(2,1)S(1)}, u32[]{:S(2)}, u32[]{:S(2)}) collective-permute-start(bf16[96,384]{1,0:T(8,128)(2,1)S(1)} %get-tuple-element.29.refs_3_), channel_id=1, source_target_pairs={{0,32},{16,48},{32,64},{48,80},{64,96},{80,112},{96,0},{112,16},{1... | collective-permute-start | bytes 221192 | tf_op jit(solution)/shard_map/ppermute | solution.py:463
  82.0 19.4 %collective-permute-start.13 = (bf16[96,384]{1,0:T(8,128)(2,1)S(1)}, bf16[96,384]{1,0:T(8,128)(2,1)S(1)}, u32[]{:S(2)}, u32[]{:S(2)}) collective-permute-start(bf16[96,384]{1,0:T(8,128)(2,1)S(1)} %get-tuple-element.29.refs_3_), channel_id=1, source_target_pairs={{0,48},{16,64},{32,80},{48,96},{64,112},{80,0},{96,16},{112,32},{1... | collective-permute-start | bytes 221192 | tf_op jit(solution)/shard_map/ppermute | solution.py:463
  84.7 19.0 %collective-permute-start.14 = (bf16[96,384]{1,0:T(8,128)(2,1)S(1)}, bf16[96,384]{1,0:T(8,128)(2,1)S(1)}, u32[]{:S(2)}, u32[]{:S(2)}) collective-permute-start(bf16[96,384]{1,0:T(8,128)(2,1)S(1)} %get-tuple-element.29.refs_3_), channel_id=1, source_target_pairs={{0,64},{16,80},{32,96},{48,112},{64,0},{80,16},{96,32},{112,48},{1... | collective-permute-start | bytes 221192 | tf_op jit(solution)/shard_map/ppermute | solution.py:463
  87.0 8.0 %collective-permute-start.9 = (bf16[64,192]{1,0:T(8,128)(2,1)S(1)}, bf16[64,192]{1,0:T(8,128)(2,1)S(1)}, u32[]{:S(2)}, u32[]{:S(2)}) collective-permute-start(bf16[64,192]{1,0:T(8,128)(2,1)S(1)} %get-tuple-element.25.refs_0_), channel_id=1, source_target_pairs={{0,128},{128,0},{1,129},{129,1},{2,130},{130,2},{3,131},{131,3},{4... | collective-permute-start | bytes 73736 | tf_op jit(solution)/shard_map/ppermute | solution.py:466
  95.1 8.6 %collective-permute-start.15 = (bf16[96,384]{1,0:T(8,128)(2,1)S(1)}, bf16[96,384]{1,0:T(8,128)(2,1)S(1)}, u32[]{:S(2)}, u32[]{:S(2)}) collective-permute-start(bf16[96,384]{1,0:T(8,128)(2,1)S(1)} %get-tuple-element.29.refs_3_), channel_id=1, source_target_pairs={{0,80},{16,96},{32,112},{48,0},{64,16},{80,32},{96,48},{112,64},{1... | collective-permute-start | bytes 221192 | tf_op jit(solution)/shard_map/ppermute | solution.py:463
  95.3 8.9 %collective-permute-start.16 = (bf16[96,384]{1,0:T(8,128)(2,1)S(1)}, bf16[96,384]{1,0:T(8,128)(2,1)S(1)}, u32[]{:S(2)}, u32[]{:S(2)}) collective-permute-start(bf16[96,384]{1,0:T(8,128)(2,1)S(1)} %get-tuple-element.29.refs_3_), channel_id=1, source_target_pairs={{0,96},{16,112},{32,0},{48,16},{64,32},{80,48},{96,64},{112,80},{1... | collective-permute-start | bytes 221192 | tf_op jit(solution)/shard_map/ppermute | solution.py:463
  98.7 7.5 %collective-permute-start.17 = (bf16[96,384]{1,0:T(8,128)(2,1)S(1)}, bf16[96,384]{1,0:T(8,128)(2,1)S(1)}, u32[]{:S(2)}, u32[]{:S(2)}) collective-permute-start(bf16[96,384]{1,0:T(8,128)(2,1)S(1)} %get-tuple-element.29.refs_3_), channel_id=1, source_target_pairs={{0,112},{16,0},{32,16},{48,32},{64,48},{80,64},{96,80},{112,96},{1... | collective-permute-start | bytes 221192 | tf_op jit(solution)/shard_map/ppermute | solution.py:463
  101.4 5.9 %collective-permute-start.10 = (f32[64,256]{1,0:T(8,128)S(1)}, f32[64,256]{1,0:T(8,128)S(1)}, u32[]{:S(2)}, u32[]{:S(2)}) collective-permute-start(f32[64,256]{1,0:T(8,128)S(1)} %get-tuple-element.28), channel_id=1, source_target_pairs={{0,128},{128,0},{1,129},{129,1},{2,130},{130,2},{3,131},{131,3},{4... | collective-permute-start | bytes 196616 | tf_op jit(solution)/shard_map/ppermute | solution.py:476
  107.9 12.1 %collective-permute-start.18 = (bf16[8,96,384]{2,1,0:T(8,128)(2,1)S(1)}, bf16[8,96,384]{2,1,0:T(8,128)(2,1)S(1)}, u32[]{:S(2)}, u32[]{:S(2)}) collective-permute-start(bf16[8,96,384]{2,1,0:T(8,128)(2,1)S(1)} %get-tuple-element.32.refs_3_), channel_id=1, source_target_pairs={{0,8},{8,0},{1,9},{9,1},{2,10},{10,2},{3,11},{11,3},{4,12},{12,4},... | collective-permute-start | bytes 1769480 | tf_op jit(solution)/shard_map/ppermute | solution.py:484
  (19 other events, 171.5 us)

commit v7 on v6

--- a/solution.py
+++ b/solution.py
@@ -153,7 +153,7 @@
     fetches = [
         pltpu.make_async_copy(far, near, arrived.at[i]) for i, (far, near) in enumerate(pairs)
     ]
-    for fetch in fetches:
+    for fetch in fetches[:3]:
         fetch.start()
     split_out[...] = split[...]
     wide = widen(tokens[...], left[...], right[...])
@@ -165,6 +165,8 @@
     fetches[0].wait()
     keys = dot(normed, wk[...]).astype(BF)
     fetches[1].wait()
+    for fetch in fetches[3:]:
+        fetch.start()
     values = dot(normed, wv[...]).astype(BF)
 
     row, col = place_of(lax.broadcasted_iota(jnp.int32, (128, 448), 0))

time: 134 us -> 134 us (level)
  no operation moved by 1% of the time
where the time goes in v7:
time: 134 us; the launch traced here: 133 us
  starting transfers between devices  59.1 us (44%)
  blocking collectives  25.1 us (19%)
  waiting for transfers between devices  24.9 us (19%)
  Pallas kernels  16.8 us (13%)
  local copies, waits for them, and re-layouts  5.97 us (4%)
    all_to_all x4, starting transfers between devices, exchange(): return lax.all_to_all(block, axis, split_axis=0, concat_axis=0, tiled=True)  24 us
    all_to_all x2, blocking collectives, exchange(): return lax.all_to_all(block, axis, split_axis=0, concat_axis=0, tiled=True)  22.7 us
    all_to_all x4, waiting for transfers between devices, exchange(): return lax.all_to_all(block, axis, split_axis=0, concat_axis=0, tiled=True)  17.2 us
    pallas_call x9, Pallas kernels, call(): pl.pallas_call(kernel, out_shape=out_shape, in_specs=specs, out_specs=out...  16.8 us
    ppermute x7, starting transfers between devices, on_device(): lax.ppermute(split_block, 'z', [(i, (i + step) % 8) for i in range(8)])  14.5 us
    ppermute x1, waiting for transfers between devices, on_device(): over_yh = lax.ppermute(split_block, 'yh', swap('yh'))  4.01 us
    unnamed x40, local copies, waits for them, and re-layouts  3.75 us
    ppermute x1, starting transfers between devices, on_device(): left = lax.ppermute(tokens[:, 8:16], COL, shift(COL, 1))  3.42 us
  transfers between devices with their start and end apart: 23, of which 8 were waited for; matrix products, arithmetic and copies ran while one was open for 1% of the time, Pallas kernels for 8%

profile of v7, /device:TPU:8, one launch (start us, length us, event | category | flops | bytes accessed | tf_op | source)
XLA Modules:
  0.0 133.2 jit_solution(17750784709617199431)
XLA Ops:
  0.9 3.4 %collective-permute-start = (bf16[8,8,384]{2,1,0:T(8,128)(2,1)S(1)}, bf16[8,8,384]{2,1,0:T(8,128)(2,1)S(1)}, u32[]{:S(2)}, u32[]{:S(2)}) collective-permute-start(bf16[8,8,384]{2,1,0:T(8,128)(2,1)S(1)} %get-tuple-element.36), channel_id=1, source_target_pairs={{0,1},{1,2},{2,3},{3,4},{4,5},{5,6},{6,7},{8,9},{9,10},{10,11},{11... | collective-permute-start | bytes 147464 | tf_op jit(solution)/shard_map/ppermute | solution.py:360
  4.3 2.6 %collective-permute-start.1 = (bf16[8,8,384]{2,1,0:T(8,128)(2,1)S(1)}, bf16[8,8,384]{2,1,0:T(8,128)(2,1)S(1)}, u32[]{:S(2)}, u32[]{:S(2)}) collective-permute-start(bf16[8,8,384]{2,1,0:T(8,128)(2,1)S(1)} %get-tuple-element.35), channel_id=1, source_target_pairs={{1,0},{2,1},{3,2},{4,3},{5,4},{6,5},{7,6},{9,8},{10,9},{11,10},{12... | collective-permute-start | bytes 147464 | tf_op jit(solution)/shard_map/ppermute | solution.py:361
  6.9 2.6 %collective-permute-start.4 = (bf16[48,384]{1,0:T(8,128)(2,1)}, bf16[48,384]{1,0:T(8,128)(2,1)S(1)}, u32[]{:S(2)}, u32[]{:S(2)}) collective-permute-start(bf16[48,384]{1,0:T(8,128)(2,1)} %param.30), channel_id=1, source_target_pairs={{0,0},{1,16},{2,32},{3,48},{4,64},{5,80},{6,96},{7,112},{8,8},{9,2... | collective-permute-start | bytes 110600 | tf_op jit(solution)/shard_map/ppermute | solution.py:394
  11.2 9.8 %all-to-all-start.1 = ((bf16[8,48,384]{2,1,0:T(8,128)(2,1)}), bf16[8,48,384]{2,1,0:T(8,128)(2,1)S(1)}, u32[]{:S(2)}, u32[]{:S(2)}) async-start(bf16[8,48,384]{2,1,0:T(8,128)(2,1)} %copies.1), calls=%async_computation.1 | async-start | bytes 589824 | tf_op jit(solution)/shard_map/all_to_all | solution.py:35
  25.9 7.1 %all-to-all-done.1.refs_2_ = bf16[8,48,384]{2,1,0:T(8,128)(2,1)S(1)} async-done(((bf16[8,48,384]{2,1,0:T(8,128)(2,1)}), bf16[8,48,384]{2,1,0:T(8,128)(2,1)S(1)}, u32[]{:S(2)}, u32[]{:S(2)}) %all-to-all-start.1) | async-done | bytes 294944 | tf_op jit(solution)/shard_map/all_to_all | solution.py:35
  33.0 2.7 %collective-permute-start.6 = (bf16[8,48,384]{2,1,0:T(8,128)(2,1)S(1)}, bf16[8,48,384]{2,1,0:T(8,128)(2,1)S(1)}, u32[]{:S(2)}, u32[]{:S(2)}) collective-permute-start(bf16[8,48,384]{2,1,0:T(8,128)(2,1)S(1)} %all-to-all-done.1.refs_2_), channel_id=1, source_target_pairs={{0,128},{128,0},{1,129},{129,1},{2,130},{130,2},{3,131},{131,3},{4... | collective-permute-start | bytes 884744 | tf_op jit(solution)/shard_map/ppermute | solution.py:398
  37.0 8.0 %finest.1 = (bf16[128,384]{1,0:T(8,128)(2,1)}, bf16[32,768]{1,0:T(8,128)(2,1)}, bf16[64,3072]{1,0:T(8,128)(2,1)}, bf16[48,384]{1,0:T(8,128)(2,1)}) custom-call(s32[7]{0:T(128)} %stack.23.refs_0_, bf16[8,16,384]{2,1,0:T(8,128)(2,1)} %refs_1_.1, bf16[8,8,384]{2,1,0:T(8,128)(2,1)} %copy-done.11, bf16[8,8,384]{2,1,0:T(8,128)(2,1)} %copy-done.12, ...), custom_call_target="tpu_custom_call" | custom-call | flops 6000000000 | bytes 18000000 | tf_op jit(solution)/shard_map/finest/pallas_call | solution.py:84
  45.0 6.3 %all-to-all-start = ((bf16[8,8,3072]{2,1,0:T(8,128)(2,1)}), bf16[8,8,3072]{2,1,0:T(8,128)(2,1)S(1)}, u32[]{:S(2)}, u32[]{:S(2)}) async-start(bf16[8,8,3072]{2,1,0:T(8,128)(2,1)} %bitcast.32), calls=%async_computation | async-start | bytes 786432 | tf_op jit(solution)/shard_map/all_to_all | solution.py:35
  51.9 6.3 %all-to-all-done = bf16[8,8,3072]{2,1,0:T(8,128)(2,1)S(1)} async-done(((bf16[8,8,3072]{2,1,0:T(8,128)(2,1)}), bf16[8,8,3072]{2,1,0:T(8,128)(2,1)S(1)}, u32[]{:S(2)}, u32[]{:S(2)}) %all-to-all-start) | async-done | bytes 393248 | tf_op jit(solution)/shard_map/all_to_all | solution.py:35
  61.7 3.9 %all-to-all-start.2 = ((bf16[8,64,192]{2,1,0:T(8,128)(2,1)}), bf16[8,64,192]{2,1,0:T(8,128)(2,1)S(1)}, u32[]{:S(2)}, u32[]{:S(2)}) async-start(bf16[8,64,192]{2,1,0:T(8,128)(2,1)} %bitcast.9), calls=%async_computation.2 | async-start | bytes 524288 | tf_op jit(solution)/shard_map/all_to_all | solution.py:35
  67.4 4.0 %collective-permute-done.8.refs_6_ = bf16[48,384]{1,0:T(8,128)(2,1)S(1)} collective-permute-done((bf16[48,384]{1,0:T(8,128)(2,1)S(1)}, bf16[48,384]{1,0:T(8,128)(2,1)S(1)}, u32[]{:S(2)}, u32[]{:S(2)}) %collective-permute-start.8) | collective-permute-done | bytes 36896 | tf_op jit(solution)/shard_map/ppermute | solution.py:438
  73.7 3.9 %all-to-all-start.3 = ((bf16[8,64,384]{2,1,0:T(8,128)(2,1)}), bf16[8,64,384]{2,1,0:T(8,128)(2,1)S(1)}, u32[]{:S(2)}, u32[]{:S(2)}) async-start(bf16[8,64,384]{2,1,0:T(8,128)(2,1)} %bitcast.14), calls=%async_computation.3 | async-start | bytes 786432 | tf_op jit(solution)/shard_map/all_to_all | solution.py:35
  77.6 2.0 %collective-permute-start.11 = (bf16[96,384]{1,0:T(8,128)(2,1)S(1)}, bf16[96,384]{1,0:T(8,128)(2,1)S(1)}, u32[]{:S(2)}, u32[]{:S(2)}) collective-permute-start(bf16[96,384]{1,0:T(8,128)(2,1)S(1)} %get-tuple-element.29.refs_3_), channel_id=1, source_target_pairs={{0,16},{16,32},{32,48},{48,64},{64,80},{80,96},{96,112},{112,0},{1... | collective-permute-start | bytes 221192 | tf_op jit(solution)/shard_map/ppermute | solution.py:465
  79.6 2.4 %collective-permute-start.12 = (bf16[96,384]{1,0:T(8,128)(2,1)S(1)}, bf16[96,384]{1,0:T(8,128)(2,1)S(1)}, u32[]{:S(2)}, u32[]{:S(2)}) collective-permute-start(bf16[96,384]{1,0:T(8,128)(2,1)S(1)} %get-tuple-element.29.refs_3_), channel_id=1, source_target_pairs={{0,32},{16,48},{32,64},{48,80},{64,96},{80,112},{96,0},{112,16},{1... | collective-permute-start | bytes 221192 | tf_op jit(solution)/shard_map/ppermute | solution.py:465
  82.0 2.7 %collective-permute-start.13 = (bf16[96,384]{1,0:T(8,128)(2,1)S(1)}, bf16[96,384]{1,0:T(8,128)(2,1)S(1)}, u32[]{:S(2)}, u32[]{:S(2)}) collective-permute-start(bf16[96,384]{1,0:T(8,128)(2,1)S(1)} %get-tuple-element.29.refs_3_), channel_id=1, source_target_pairs={{0,48},{16,64},{32,80},{48,96},{64,112},{80,0},{96,16},{112,32},{1... | collective-permute-start | bytes 221192 | tf_op jit(solution)/shard_map/ppermute | solution.py:465
  84.7 2.4 %collective-permute-start.14 = (bf16[96,384]{1,0:T(8,128)(2,1)S(1)}, bf16[96,384]{1,0:T(8,128)(2,1)S(1)}, u32[]{:S(2)}, u32[]{:S(2)}) collective-permute-start(bf16[96,384]{1,0:T(8,128)(2,1)S(1)} %get-tuple-element.29.refs_3_), channel_id=1, source_target_pairs={{0,64},{16,80},{32,96},{48,112},{64,0},{80,16},{96,32},{112,48},{1... | collective-permute-start | bytes 221192 | tf_op jit(solution)/shard_map/ppermute | solution.py:465
  87.0 2.1 %collective-permute-start.9 = (bf16[64,192]{1,0:T(8,128)(2,1)S(1)}, bf16[64,192]{1,0:T(8,128)(2,1)S(1)}, u32[]{:S(2)}, u32[]{:S(2)}) collective-permute-start(bf16[64,192]{1,0:T(8,128)(2,1)S(1)} %get-tuple-element.25.refs_0_), channel_id=1, source_target_pairs={{0,128},{128,0},{1,129},{129,1},{2,130},{130,2},{3,131},{131,3},{4... | collective-permute-start | bytes 73736 | tf_op jit(solution)/shard_map/ppermute | solution.py:468
  89.2 3.5 %all-to-all-done.3 = bf16[8,64,384]{2,1,0:T(8,128)(2,1)S(1)} async-done(((bf16[8,64,384]{2,1,0:T(8,128)(2,1)}), bf16[8,64,384]{2,1,0:T(8,128)(2,1)S(1)}, u32[]{:S(2)}, u32[]{:S(2)}) %all-to-all-start.3) | async-done | bytes 393248 | tf_op jit(solution)/shard_map/all_to_all | solution.py:35
  92.7 2.4 %all_gather.3.refs_2_ = bf16[1024,384]{1,0:T(8,128)(2,1)S(1)} all-gather(bf16[512,384]{1,0:T(8,128)(2,1)S(1)} %bitcast.31), channel_id=1, replica_groups=mesh['yh'=2,'z'=8,'k'=2,'x'=4,'yl'=2] {'k'}, dimensions={0}, use_global_device_ids=true | all-gather | bytes 1179648 | tf_op jit(solution)/shard_map/all_gather | solution.py:470
  95.3 3.4 %collective-permute-start.16 = (bf16[96,384]{1,0:T(8,128)(2,1)S(1)}, bf16[96,384]{1,0:T(8,128)(2,1)S(1)}, u32[]{:S(2)}, u32[]{:S(2)}) collective-permute-start(bf16[96,384]{1,0:T(8,128)(2,1)S(1)} %get-tuple-element.29.refs_3_), channel_id=1, source_target_pairs={{0,96},{16,112},{32,0},{48,16},{64,32},{80,48},{96,64},{112,80},{1... | collective-permute-start | bytes 221192 | tf_op jit(solution)/shard_map/ppermute | solution.py:465
  101.4 2.2 %collective-permute-start.10 = (f32[64,256]{1,0:T(8,128)S(1)}, f32[64,256]{1,0:T(8,128)S(1)}, u32[]{:S(2)}, u32[]{:S(2)}) collective-permute-start(f32[64,256]{1,0:T(8,128)S(1)} %get-tuple-element.28), channel_id=1, source_target_pairs={{0,128},{128,0},{1,129},{129,1},{2,130},{130,2},{3,131},{131,3},{4... | collective-permute-start | bytes 196616 | tf_op jit(solution)/shard_map/ppermute | solution.py:478
  104.2 2.0 %collective-permute-done.17.refs_10_ = bf16[96,384]{1,0:T(8,128)(2,1)S(1)} collective-permute-done((bf16[96,384]{1,0:T(8,128)(2,1)S(1)}, bf16[96,384]{1,0:T(8,128)(2,1)S(1)}, u32[]{:S(2)}, u32[]{:S(2)}) %collective-permute-start.17) | collective-permute-done | bytes 73760 | tf_op jit(solution)/shard_map/ppermute | solution.py:465
  108.0 12.0 %all_to_all.61 = bf16[8,64,192]{2,1,0:T(8,128)(2,1)S(1)} all-to-all(bf16[8,64,192]{2,1,0:T(8,128)(2,1)S(1)} %bitcast.26), channel_id=1, replica_groups=mesh['yh'=2,'z'=8,'k'=2,'x'=4,'yl'=2] {'x','yl'}, dimensions={0} | all-to-all | bytes 393216 | tf_op jit(solution)/shard_map/all_to_all | solution.py:35
  121.1 10.8 %all_to_all.62 = bf16[8,8,3072]{2,1,0:T(8,128)(2,1)S(1)} all-to-all(bf16[8,8,3072]{2,1,0:T(8,128)(2,1)S(1)} %bitcast.23), channel_id=1, replica_groups=mesh['yh'=2,'z'=8,'k'=2,'x'=4,'yl'=2] {'x','yl'}, dimensions={0} | all-to-all | bytes 786432 | tf_op jit(solution)/shard_map/all_to_all | solution.py:35
  (82 shorter events, 23.7 us)
Async XLA Ops:
  0.9 21.1 %collective-permute-start = (bf16[8,8,384]{2,1,0:T(8,128)(2,1)S(1)}, bf16[8,8,384]{2,1,0:T(8,128)(2,1)S(1)}, u32[]{:S(2)}, u32[]{:S(2)}) collective-permute-start(bf16[8,8,384]{2,1,0:T(8,128)(2,1)S(1)} %get-tuple-element.36), channel_id=1, source_target_pairs={{0,1},{1,2},{2,3},{3,4},{4,5},{5,6},{6,7},{8,9},{9,10},{10,11},{11... | collective-permute-start | bytes 147464 | tf_op jit(solution)/shard_map/ppermute | solution.py:360
  4.3 17.7 %collective-permute-start.1 = (bf16[8,8,384]{2,1,0:T(8,128)(2,1)S(1)}, bf16[8,8,384]{2,1,0:T(8,128)(2,1)S(1)}, u32[]{:S(2)}, u32[]{:S(2)}) collective-permute-start(bf16[8,8,384]{2,1,0:T(8,128)(2,1)S(1)} %get-tuple-element.35), channel_id=1, source_target_pairs={{1,0},{2,1},{3,2},{4,3},{5,4},{6,5},{7,6},{9,8},{10,9},{11,10},{12... | collective-permute-start | bytes 147464 | tf_op jit(solution)/shard_map/ppermute | solution.py:361
  6.9 28.8 %collective-permute-start.4 = (bf16[48,384]{1,0:T(8,128)(2,1)}, bf16[48,384]{1,0:T(8,128)(2,1)S(1)}, u32[]{:S(2)}, u32[]{:S(2)}) collective-permute-start(bf16[48,384]{1,0:T(8,128)(2,1)} %param.30), channel_id=1, source_target_pairs={{0,0},{1,16},{2,32},{3,48},{4,64},{5,80},{6,96},{7,112},{8,8},{9,2... | collective-permute-start | bytes 110600 | tf_op jit(solution)/shard_map/ppermute | solution.py:394
  11.2 21.8 %all-to-all-start.1 = ((bf16[8,48,384]{2,1,0:T(8,128)(2,1)}), bf16[8,48,384]{2,1,0:T(8,128)(2,1)S(1)}, u32[]{:S(2)}, u32[]{:S(2)}) async-start(bf16[8,48,384]{2,1,0:T(8,128)(2,1)} %copies.1), calls=%async_computation.1 | async-start | bytes 589824 | tf_op jit(solution)/shard_map/all_to_all | solution.py:35
  22.1 13.7 %collective-permute-start.2 = (bf16[3,32,384]{2,1,0:T(8,128)(2,1)S(1)}, bf16[3,32,384]{2,1,0:T(8,128)(2,1)S(1)}, u32[]{:S(2)}, u32[]{:S(2)}) collective-permute-start(bf16[3,32,384]{2,1,0:T(8,128)(2,1)S(1)} %get-tuple-element.20), channel_id=1, source_target_pairs={{0,8},{8,16},{16,24},{24,32},{32,40},{40,48},{48,56},{56,64},{64,7... | collective-permute-start | bytes 221192 | tf_op jit(solution)/shard_map/ppermute | solution.py:365
  23.4 12.4 %collective-permute-start.3 = (bf16[3,32,384]{2,1,0:T(8,128)(2,1)S(1)}, bf16[3,32,384]{2,1,0:T(8,128)(2,1)S(1)}, u32[]{:S(2)}, u32[]{:S(2)}) collective-permute-start(bf16[3,32,384]{2,1,0:T(8,128)(2,1)S(1)} %get-tuple-element.21), channel_id=1, source_target_pairs={{8,0},{16,8},{24,16},{32,24},{40,32},{48,40},{56,48},{64,56},{72,6... | collective-permute-start | bytes 221192 | tf_op jit(solution)/shard_map/ppermute | solution.py:366
  25.9 33.0 %copy-start.2 = (s32[7]{0:T(128)S(1)}, s32[7]{0:T(128)}, u32[]{:S(2)}) copy-start(s32[7]{0:T(128)} %stack.23.refs_0_) | copy-start | bytes 88
  33.0 18.4 %collective-permute-start.6 = (bf16[8,48,384]{2,1,0:T(8,128)(2,1)S(1)}, bf16[8,48,384]{2,1,0:T(8,128)(2,1)S(1)}, u32[]{:S(2)}, u32[]{:S(2)}) collective-permute-start(bf16[8,48,384]{2,1,0:T(8,128)(2,1)S(1)} %all-to-all-done.1.refs_2_), channel_id=1, source_target_pairs={{0,128},{128,0},{1,129},{129,1},{2,130},{130,2},{3,131},{131,3},{4... | collective-permute-start | bytes 884744 | tf_op jit(solution)/shard_map/ppermute | solution.py:398
  45.0 13.2 %all-to-all-start = ((bf16[8,8,3072]{2,1,0:T(8,128)(2,1)}), bf16[8,8,3072]{2,1,0:T(8,128)(2,1)S(1)}, u32[]{:S(2)}, u32[]{:S(2)}) async-start(bf16[8,8,3072]{2,1,0:T(8,128)(2,1)} %bitcast.32), calls=%async_computation | async-start | bytes 786432 | tf_op jit(solution)/shard_map/all_to_all | solution.py:35
  51.4 6.8 %collective-permute-start.5 = (bf16[8,48,384]{2,1,0:T(8,128)(2,1)S(1)}, bf16[8,48,384]{2,1,0:T(8,128)(2,1)S(1)}, u32[]{:S(2)}, u32[]{:S(2)}) collective-permute-start(bf16[8,48,384]{2,1,0:T(8,128)(2,1)S(1)} %all-to-all-done.1.refs_2_), channel_id=1, source_target_pairs={{0,8},{8,0},{1,9},{9,1},{2,10},{10,2},{3,11},{11,3},{4,12},{12,4},... | collective-permute-start | bytes 884744 | tf_op jit(solution)/shard_map/ppermute | solution.py:439
  51.4 6.8 %collective-permute-start.7 = (bf16[8,48,384]{2,1,0:T(8,128)(2,1)S(1)}, bf16[8,48,384]{2,1,0:T(8,128)(2,1)S(1)}, u32[]{:S(2)}, u32[]{:S(2)}) collective-permute-start(bf16[8,48,384]{2,1,0:T(8,128)(2,1)S(1)} %collective-permute-done.6.refs_4_), channel_id=1, source_target_pairs={{0,8},{8,0},{1,9},{9,1},{2,10},{10,2},{3,11},{11,3},{4,12},{12,4},... | collective-permute-start | bytes 884744 | tf_op jit(solution)/shard_map/ppermute | solution.py:439
  61.7 10.1 %all-to-all-start.2 = ((bf16[8,64,192]{2,1,0:T(8,128)(2,1)}), bf16[8,64,192]{2,1,0:T(8,128)(2,1)S(1)}, u32[]{:S(2)}, u32[]{:S(2)}) async-start(bf16[8,64,192]{2,1,0:T(8,128)(2,1)} %bitcast.9), calls=%async_computation.2 | async-start | bytes 524288 | tf_op jit(solution)/shard_map/all_to_all | solution.py:35
  65.6 5.8 %collective-permute-start.8 = (bf16[48,384]{1,0:T(8,128)(2,1)S(1)}, bf16[48,384]{1,0:T(8,128)(2,1)S(1)}, u32[]{:S(2)}, u32[]{:S(2)}) collective-permute-start(bf16[48,384]{1,0:T(8,128)(2,1)S(1)} %copy-done.13), channel_id=1, source_target_pairs={{0,128},{128,0},{1,129},{129,1},{2,130},{130,2},{3,131},{131,3},{4... | collective-permute-start | bytes 110600 | tf_op jit(solution)/shard_map/ppermute | solution.py:438
  73.7 19.0 %all-to-all-start.3 = ((bf16[8,64,384]{2,1,0:T(8,128)(2,1)}), bf16[8,64,384]{2,1,0:T(8,128)(2,1)S(1)}, u32[]{:S(2)}, u32[]{:S(2)}) async-start(bf16[8,64,384]{2,1,0:T(8,128)(2,1)} %bitcast.14), calls=%async_computation.3 | async-start | bytes 786432 | tf_op jit(solution)/shard_map/all_to_all | solution.py:35
  77.6 17.7 %collective-permute-start.11 = (bf16[96,384]{1,0:T(8,128)(2,1)S(1)}, bf16[96,384]{1,0:T(8,128)(2,1)S(1)}, u32[]{:S(2)}, u32[]{:S(2)}) collective-permute-start(bf16[96,384]{1,0:T(8,128)(2,1)S(1)} %get-tuple-element.29.refs_3_), channel_id=1, source_target_pairs={{0,16},{16,32},{32,48},{48,64},{64,80},{80,96},{96,112},{112,0},{1... | collective-permute-start | bytes 221192 | tf_op jit(solution)/shard_map/ppermute | solution.py:465
  79.6 19.1 %collective-permute-start.12 = (bf16[96,384]{1,0:T(8,128)(2,1)S(1)}, bf16[96,384]{1,0:T(8,128)(2,1)S(1)}, u32[]{:S(2)}, u32[]{:S(2)}) collective-permute-start(bf16[96,384]{1,0:T(8,128)(2,1)S(1)} %get-tuple-element.29.refs_3_), channel_id=1, source_target_pairs={{0,32},{16,48},{32,64},{48,80},{64,96},{80,112},{96,0},{112,16},{1... | collective-permute-start | bytes 221192 | tf_op jit(solution)/shard_map/ppermute | solution.py:465
  82.0 19.4 %collective-permute-start.13 = (bf16[96,384]{1,0:T(8,128)(2,1)S(1)}, bf16[96,384]{1,0:T(8,128)(2,1)S(1)}, u32[]{:S(2)}, u32[]{:S(2)}) collective-permute-start(bf16[96,384]{1,0:T(8,128)(2,1)S(1)} %get-tuple-element.29.refs_3_), channel_id=1, source_target_pairs={{0,48},{16,64},{32,80},{48,96},{64,112},{80,0},{96,16},{112,32},{1... | collective-permute-start | bytes 221192 | tf_op jit(solution)/shard_map/ppermute | solution.py:465
  84.7 19.0 %collective-permute-start.14 = (bf16[96,384]{1,0:T(8,128)(2,1)S(1)}, bf16[96,384]{1,0:T(8,128)(2,1)S(1)}, u32[]{:S(2)}, u32[]{:S(2)}) collective-permute-start(bf16[96,384]{1,0:T(8,128)(2,1)S(1)} %get-tuple-element.29.refs_3_), channel_id=1, source_target_pairs={{0,64},{16,80},{32,96},{48,112},{64,0},{80,16},{96,32},{112,48},{1... | collective-permute-start | bytes 221192 | tf_op jit(solution)/shard_map/ppermute | solution.py:465
  87.0 8.0 %collective-permute-start.9 = (bf16[64,192]{1,0:T(8,128)(2,1)S(1)}, bf16[64,192]{1,0:T(8,128)(2,1)S(1)}, u32[]{:S(2)}, u32[]{:S(2)}) collective-permute-start(bf16[64,192]{1,0:T(8,128)(2,1)S(1)} %get-tuple-element.25.refs_0_), channel_id=1, source_target_pairs={{0,128},{128,0},{1,129},{129,1},{2,130},{130,2},{3,131},{131,3},{4... | collective-permute-start | bytes 73736 | tf_op jit(solution)/shard_map/ppermute | solution.py:468
  95.1 8.6 %collective-permute-start.15 = (bf16[96,384]{1,0:T(8,128)(2,1)S(1)}, bf16[96,384]{1,0:T(8,128)(2,1)S(1)}, u32[]{:S(2)}, u32[]{:S(2)}) collective-permute-start(bf16[96,384]{1,0:T(8,128)(2,1)S(1)} %get-tuple-element.29.refs_3_), channel_id=1, source_target_pairs={{0,80},{16,96},{32,112},{48,0},{64,16},{80,32},{96,48},{112,64},{1... | collective-permute-start | bytes 221192 | tf_op jit(solution)/shard_map/ppermute | solution.py:465
  95.3 8.9 %collective-permute-start.16 = (bf16[96,384]{1,0:T(8,128)(2,1)S(1)}, bf16[96,384]{1,0:T(8,128)(2,1)S(1)}, u32[]{:S(2)}, u32[]{:S(2)}) collective-permute-start(bf16[96,384]{1,0:T(8,128)(2,1)S(1)} %get-tuple-element.29.refs_3_), channel_id=1, source_target_pairs={{0,96},{16,112},{32,0},{48,16},{64,32},{80,48},{96,64},{112,80},{1... | collective-permute-start | bytes 221192 | tf_op jit(solution)/shard_map/ppermute | solution.py:465
  98.7 7.5 %collective-permute-start.17 = (bf16[96,384]{1,0:T(8,128)(2,1)S(1)}, bf16[96,384]{1,0:T(8,128)(2,1)S(1)}, u32[]{:S(2)}, u32[]{:S(2)}) collective-permute-start(bf16[96,384]{1,0:T(8,128)(2,1)S(1)} %get-tuple-element.29.refs_3_), channel_id=1, source_target_pairs={{0,112},{16,0},{32,16},{48,32},{64,48},{80,64},{96,80},{112,96},{1... | collective-permute-start | bytes 221192 | tf_op jit(solution)/shard_map/ppermute | solution.py:465
  101.4 5.9 %collective-permute-start.10 = (f32[64,256]{1,0:T(8,128)S(1)}, f32[64,256]{1,0:T(8,128)S(1)}, u32[]{:S(2)}, u32[]{:S(2)}) collective-permute-start(f32[64,256]{1,0:T(8,128)S(1)} %get-tuple-element.28), channel_id=1, source_target_pairs={{0,128},{128,0},{1,129},{129,1},{2,130},{130,2},{3,131},{131,3},{4... | collective-permute-start | bytes 196616 | tf_op jit(solution)/shard_map/ppermute | solution.py:478
  107.9 12.1 %collective-permute-start.18 = (bf16[8,96,384]{2,1,0:T(8,128)(2,1)S(1)}, bf16[8,96,384]{2,1,0:T(8,128)(2,1)S(1)}, u32[]{:S(2)}, u32[]{:S(2)}) collective-permute-start(bf16[8,96,384]{2,1,0:T(8,128)(2,1)S(1)} %get-tuple-element.32.refs_3_), channel_id=1, source_target_pairs={{0,8},{8,0},{1,9},{9,1},{2,10},{10,2},{3,11},{11,3},{4,12},{12,4},... | collective-permute-start | bytes 1769480 | tf_op jit(solution)/shard_map/ppermute | solution.py:486
  (19 other events, 171.5 us)
